TPU v7x, 128 devices: a whole 4x4x4 slice. The times are simulated.
128 devices in a mesh: gx: 8 (over x, core), gy: 16 (over z, y).
Axes of the slice: x: 4, y: 4, z: 4, core: 2. Of those that a mesh axis runs over, the one named last changes fastest.
Arguments:
- populations: float32 [19, 128, 256, 128], P(None, 'gx', 'gy'), may hold values from 0.02 to 0.1
- porosity: float32 [128, 256, 128], P('gx', 'gy'), may hold values from 0.05 to 0.95
- adjoint_in: float32 [19, 128, 256, 128], P(None, 'gx', 'gy'), may hold values from -6 to 6
- porous: int32 [128, 256, 128], P('gx', 'gy'), may hold values 0 or 1
- walls: int32 [128, 256, 128], P('gx', 'gy'), may hold values 0 or 1
- owners: int32 [8, 16, 64, 1], P('gx', 'gy'), may hold values from 0 to 127; in each aligned block of 64 rows (0 to 63, 64 to 127, ..., all dimensions but the last counted through in order) at most 2 rows name the same one
- slots: int32 [8, 16, 64], P('gx', 'gy'), may hold values from 0 to 255
Outputs:
- adjoint_out: float32 [19, 128, 256, 128], P(None, 'gx', 'gy')
- patch_sens: float32 [32768], P(('gx', 'gy'))
Inputs may be any that keep to these rules, and one draw needn't show every extreme that they name: `owners`: of the 64 panel blocks of one device, at most 2 name the same owner device, and some device's blocks reach 2 for some owner in every draw.
All inputs are finite; a program needn't handle non-finite values. No bound on the sum of `porous` or of `walls` on one device may be relied on, other than what follows from the above.
Results may differ from a plain program's by a relative error of at most 0.0003.
Values sent between devices are 32-bit elements; how exact they have to be, the bound alone decides.
No kernel may reach another device: no remote copies, remote signals or barrier semaphores. Data moves between devices by JAX's collectives and lax.ppermute only.
A program may use at most 128 MiB of HBM per device.

v0:
```python
import functools

import jax
import jax.numpy as jnp
from jax import lax
from jax.experimental import pallas as pl
from jax.experimental.pallas import tpu as pltpu
from jax.sharding import PartitionSpec as P

Q = 19
CX = 16
CY = 16
NZ = 128
TILE = 8
PAD_Y = 8
EXT_Y = 32
DEVICES = 128
PATCH_DEV = 256
SLOT_LANE = 64

velocities = [
    (0, 0, 0),
    (1, 0, 0),
    (-1, 0, 0),
    (0, 1, 0),
    (0, -1, 0),
    (0, 0, 1),
    (0, 0, -1),
    (1, 1, 0),
    (-1, -1, 0),
    (1, -1, 0),
    (-1, 1, 0),
    (1, 0, 1),
    (-1, 0, -1),
    (1, 0, -1),
    (-1, 0, 1),
    (0, 1, 1),
    (0, -1, -1),
    (0, 1, -1),
    (0, -1, 1),
]
opposite = [0, 2, 1, 4, 3, 6, 5, 8, 7, 10, 9, 12, 11, 14, 13, 16, 15, 18, 17]
RATE2, RATE3, RATE4 = 1.25, 1.5, 1.4


def moving(axis, sign, direction):
    return [i for i in range(Q) if direction * velocities[i][axis] == sign]


def edge(f, first):
    s, d = f[first] + f[first + 1], f[first] - f[first + 1]
    s2, d2 = f[first + 2] + f[first + 3], f[first + 2] - f[first + 3]
    return s, d, s2, d2


def off_equilibrium(f):
    sx, dx = f[1] + f[2], f[1] - f[2]
    sy, dy = f[3] + f[4], f[3] - f[4]
    sz, dz = f[5] + f[6], f[5] - f[6]
    s7, d7, s9, d9 = edge(f, 7)
    s11, d11, s13, d13 = edge(f, 11)
    s15, d15, s17, d17 = edge(f, 15)
    m220, m110, m120, m210 = s7 + s9, s7 - s9, d7 + d9, d7 - d9
    m202, m101, m102, m201 = s11 + s13, s11 - s13, d11 + d13, d11 - d13
    m022, m011, m012, m021 = s15 + s17, s15 - s17, d15 + d17, d15 - d17
    m200, m020, m002 = sx + m220 + m202, sy + m220 + m022, sz + m202 + m022
    jx, jy, jz = dx + (m120 + m102), dy + (m210 + m012), dz + (m201 + m021)
    rho = f[0] + (sx + sy + sz) + (m220 + m202 + m022)
    inv = 1.0 / rho
    ux, uy, uz = jx * inv, jy * inv, jz * inv
    qx, qy, qz = jx * ux, jy * uy, jz * uz
    third = rho * (1.0 / 3.0)
    ninth = rho * (1.0 / 9.0) - (qx + qy + qz) * (1.0 / 6.0)
    tx, ty, tz = jx * (1.0 / 3.0), jy * (1.0 / 3.0), jz * (1.0 / 3.0)
    e = {
        "200": RATE2 * (m200 - third - qx),
        "020": RATE2 * (m020 - third - qy),
        "002": RATE2 * (m002 - third - qz),
        "110": RATE2 * (m110 - jx * uy),
        "101": RATE2 * (m101 - jx * uz),
        "011": RATE2 * (m011 - jy * uz),
        "120": RATE3 * (m120 - tx),
        "102": RATE3 * (m102 - tx),
        "210": RATE3 * (m210 - ty),
        "012": RATE3 * (m012 - ty),
        "201": RATE3 * (m201 - tz),
        "021": RATE3 * (m021 - tz),
        "220": RATE4 * (m220 - ninth - 0.5 * (qx + qy)),
        "202": RATE4 * (m202 - ninth - 0.5 * (qx + qz)),
        "022": RATE4 * (m022 - ninth - 0.5 * (qy + qz)),
    }
    return (ux, uy, uz), e, (dx, dy, dz, d7, d9, d11, d13, d15, d17)


def spread(t, g, a, b):
    even, odd = t + g, t - g
    plus, minus = a + b, a - b
    return [even + plus, even - plus, odd + minus, odd - minus]


def correction(e):
    q = {k: 0.25 * v for k, v in e.items()}
    xy = spread(q["220"], q["110"], q["120"], q["210"])
    xz = spread(q["202"], q["101"], q["102"], q["201"])
    yz = spread(q["022"], q["011"], q["012"], q["021"])
    faces = []
    for second, fourth, odd in (
        ("200", ("220", "202"), ("120", "102")),
        ("020", ("220", "022"), ("210", "012")),
        ("002", ("202", "022"), ("201", "021")),
    ):
        mean = 0.5 * e[second] - 2.0 * (q[fourth[0]] + q[fourth[1]])
        lean = 2.0 * (q[odd[0]] + q[odd[1]])
        faces += [mean - lean, mean + lean]
    rest = (e["220"] + e["202"] + e["022"]) - (e["200"] + e["020"] + e["002"])
    return [rest] + faces + xy + xz + yz


def covector(b):
    hx, dx = 0.5 * (b[1] + b[2]), b[1] - b[2]
    hy, dy = 0.5 * (b[3] + b[4]), b[3] - b[4]
    hz, dz = 0.5 * (b[5] + b[6]), b[5] - b[6]
    s7, d7, s9, d9 = edge(b, 7)
    s11, d11, s13, d13 = edge(b, 11)
    s15, d15, s17, d17 = edge(b, 15)
    gx, gy, gz = hx - b[0], hy - b[0], hz - b[0]
    kx, ky, kz = 0.5 * dx, 0.5 * dy, 0.5 * dz
    t = {
        "200": gx,
        "020": gy,
        "002": gz,
        "110": 0.25 * (s7 - s9),
        "101": 0.25 * (s11 - s13),
        "011": 0.25 * (s15 - s17),
        "120": 0.25 * (d7 + d9) - kx,
        "102": 0.25 * (d11 + d13) - kx,
        "210": 0.25 * (d7 - d9) - ky,
        "012": 0.25 * (d15 + d17) - ky,
        "201": 0.25 * (d11 - d13) - kz,
        "021": 0.25 * (d15 - d17) - kz,
        "220": 0.25 * (s7 + s9) - gx - hy,
        "202": 0.25 * (s11 + s13) - gx - hz,
        "022": 0.25 * (s15 + s17) - gy - hz,
    }
    return t, (dx, dy, dz, d7, d9, d11, d13, d15, d17)


def pull_back(b, t, u, fraction):
    rates = {k: (RATE2, RATE3, RATE4)[sum(map(int, k)) - 2] for k in t}
    n = {k: rates[k] * v for k, v in t.items()}
    ux, uy, uz = u
    fourth = n["220"] + n["202"] + n["022"]
    second = n["200"] + n["020"] + n["002"]
    part = fourth * (1.0 / 3.0)
    ax = n["200"] + part - 0.5 * n["022"]
    ay = n["020"] + part - 0.5 * n["202"]
    az = n["002"] + part - 0.5 * n["220"]
    rx = 2.0 * ax * ux + n["110"] * uy + n["101"] * uz
    ry = 2.0 * ay * uy + n["110"] * ux + n["011"] * uz
    rz = 2.0 * az * uz + n["101"] * ux + n["011"] * uy
    p0 = second * (1.0 / 3.0) + fourth * (1.0 / 9.0) - 0.5 * (rx * ux + ry * uy + rz * uz)
    px = rx + (n["120"] + n["102"]) * (1.0 / 3.0)
    py = ry + (n["210"] + n["012"]) * (1.0 / 3.0)
    pz = rz + (n["201"] + n["021"]) * (1.0 / 3.0)
    ex, ey, ez = p0 - n["200"], p0 - n["020"], p0 - n["002"]
    h = [p0, ex + px, ex - px, ey + py, ey - py, ez + pz, ez - pz]
    h += spread(ex - n["020"] - n["220"], -n["110"], px - n["120"], py - n["210"])
    h += spread(ex - n["002"] - n["202"], -n["101"], px - n["102"], pz - n["201"])
    h += spread(ey - n["002"] - n["022"], -n["011"], py - n["012"], pz - n["021"])
    open_part = 1.0 - fraction
    return [open_part * (b[i] + h[i]) + fraction * b[opposite[i]] for i in range(Q)]


def put_moved(ext, i, x, row, value, direction):
    cx, cy, cz = (direction * c for c in velocities[i])
    if cz:
        value = pltpu.roll(value, cz % NZ, axis=1)
    ext[i, x + 1 + cx, pl.ds(PAD_Y + row + cy, TILE), :] = value


def fill_messages(ext, direction, x_up, x_down, y_up, y_down):
    for sign, ring, message in ((1, CX + 1, x_up), (-1, 0, x_down)):
        for k, i in enumerate(moving(0, sign, direction)):
            message[pl.ds(k * CY, CY), :] = ext[i, ring, pl.ds(PAD_Y, CY), :]
            cy = direction * velocities[i][1]
            if cy == 1:
                message[pl.ds(80, 1), :] = ext[i, ring, pl.ds(PAD_Y + CY, 1), :]
            elif cy == -1:
                message[pl.ds(81, 1), :] = ext[i, ring, pl.ds(PAD_Y - 1, 1), :]
    for sign, ring, message in ((1, PAD_Y + CY, y_up), (-1, PAD_Y - 1, y_down)):
        for k, i in enumerate(moving(1, sign, direction)):
            for x in range(CX):
                message[pl.ds(k * CX + x, 1), :] = ext[i, x + 1, pl.ds(ring, 1), :]


def fill_ring(ext, direction, x_low, x_high, y_low, y_high):
    for sign, x, message in ((1, 1, x_low), (-1, CX, x_high)):
        for k, i in enumerate(moving(0, sign, direction)):
            ext[i, x, pl.ds(PAD_Y, CY), :] = message[pl.ds(k * CY, CY), :]
    for sign, row, message in ((1, PAD_Y, y_low), (-1, PAD_Y + CY - 1, y_high)):
        for k, i in enumerate(moving(1, sign, direction)):
            for x in range(CX):
                ext[i, x + 1, pl.ds(row, 1), :] = message[pl.ds(k * CX + x, 1), :]


def rows(yt):
    return pl.ds(yt * TILE, TILE)


def forward_kernel(f, porosity, porous, walls, ext, gap, frac, mask, vel, xu, xd, yu, yd):
    @pl.loop(0, CX)
    def _(x):
        for yt in range(CY // TILE):
            at = (x, rows(yt))
            pops = [f[i, x, rows(yt), :] for i in range(Q)]
            wall = walls[at] == 1
            panel = porous[at].astype(jnp.float32)
            fraction = jnp.where(wall, 1.0, panel * porosity[at])
            frac[at] = fraction
            mask[at] = jnp.where(wall, 0.0, panel)
            u, e, _ = off_equilibrium(pops)
            for axis in range(3):
                vel[axis, x, rows(yt), :] = u[axis]
            c = correction(e)
            for i in range(Q):
                relaxed = pops[i] - c[i]
                change = pops[opposite[i]] - relaxed
                gap[i, x, rows(yt), :] = change
                put_moved(ext, i, x, yt * TILE, relaxed + fraction * change, 1)

    fill_messages(ext, 1, xu, xd, yu, yd)


def corner_kernel(x_low, x_high, up_in, down_in, up, down, *, direction):
    ups, downs = moving(1, 1, direction), moving(1, -1, direction)
    for given, message, group, source in ((up_in, up, ups, 80), (down_in, down, downs, 81)):
        del given
        for k, i in enumerate(group):
            cx = direction * velocities[i][0]
            if cx == 1:
                message[pl.ds(k * CX, 1), :] = x_low[pl.ds(source, 1), :]
            elif cx == -1:
                message[pl.ds(k * CX + CX - 1, 1), :] = x_high[pl.ds(source, 1), :]


def late_kernel(
    ext_in, xl, xh, yl, yh, adjoint, frac, mask, ext, late, sens, xu, xd, yu, yd
):
    del ext_in
    fill_ring(ext, 1, xl, xh, yl, yh)

    @pl.loop(0, CX)
    def _(x):
        for yt in range(CY // TILE):
            at = (x, rows(yt))
            read = [ext[i, x + 1, pl.ds(PAD_Y + yt * TILE, TILE), :] for i in range(Q)]
            u, e, df = off_equilibrium(read)
            b = [adjoint[i, x, rows(yt), :] for i in range(Q)]
            t, db = covector(b)
            total = sum(t[k] * e[k] for k in t) - sum(p * q for p, q in zip(db, df))
            sens[at] = mask[at] * total
            out = pull_back(b, t, u, frac[at])
            for i in range(Q):
                put_moved(late, i, x, yt * TILE, out[i], -1)

    fill_messages(late, -1, xu, xd, yu, yd)


def early_sens_kernel(
    late_in, xl, xh, yl, yh, gap, mask, sens, owner_of, place, slot, late, send, scaled
):
    del late_in
    fill_ring(late, -1, xl, xh, yl, yh)

    @pl.loop(0, CX // 2)
    def _(xb):
        for yt in range(CY // TILE):
            total = jnp.zeros((TILE, NZ), jnp.float32)
            for half in range(2):
                x = xb * 2 + half
                dot = jnp.zeros((TILE, NZ), jnp.float32)
                for i in range(Q):
                    pulled = late[i, x + 1, pl.ds(PAD_Y + yt * TILE, TILE), :]
                    dot = dot + pulled * gap[i, x, rows(yt), :]
                total = total + sens[x, rows(yt)] + mask[x, rows(yt)] * dot
            line = pl.ds(pl.multiple_of(xb * CY + yt * TILE, TILE), TILE)
            sums = jnp.sum(total, axis=1, keepdims=True)
            scaled[line, :] = sums * place[line, :] + slot[line, :]

    send[...] = jnp.dot(
        owner_of[...],
        scaled[...],
        precision=lax.Precision.HIGHEST,
        preferred_element_type=jnp.float32,
    )


def adjoint_kernel(late, frac, vel, out, hold, sems):
    copies = []
    for x in range(CX):
        copies.append(
            pltpu.make_async_copy(hold.at[x], out.at[:, x], sems.at[x])
        )

    for x in range(CX):
        for yt in range(CY // TILE):
            at = (x, rows(yt))
            b = [late[i, x + 1, pl.ds(PAD_Y + yt * TILE, TILE), :] for i in range(Q)]
            t, _ = covector(b)
            u = [vel[axis, x, rows(yt), :] for axis in range(3)]
            result = pull_back(b, t, u, frac[at])
            for i in range(Q):
                hold[x, i, rows(yt), :] = result[i]
        copies[x].start()
    for copy in copies:
        copy.wait()


def routing_kernel(owners, slots, owner_of, place, slot):
    shape = (128, 128)
    row = lax.broadcasted_iota(jnp.int32, shape, 0)
    lane = lax.broadcasted_iota(jnp.int32, shape, 1)
    block = jnp.right_shift(row, 1)
    pick = lane == block
    owner_col = jnp.sum(jnp.where(pick, owners[...], 0.0), axis=1, keepdims=True)
    slot_col = jnp.sum(jnp.where(pick, slots[...], 0.0), axis=1, keepdims=True)
    owner_row = jnp.sum(jnp.where(row == lane, owner_col, 0.0), axis=0, keepdims=True)
    owner_of[...] = jnp.where(owner_row == row.astype(jnp.float32), 1.0, 0.0)
    earlier = (owner_row == owner_col) & (jnp.right_shift(lane, 1) < block)
    rank = 0.5 * jnp.sum(jnp.where(earlier, 1.0, 0.0), axis=1, keepdims=True)
    number = lane.astype(jnp.float32)
    place[...] = jnp.where(number == rank, 1.0, 0.0)
    first = (row & 1) == 0
    slot[...] = jnp.where(first & (number == rank + SLOT_LANE), slot_col, 0.0)


def owner_kernel(got, out):
    patch = lax.broadcasted_iota(jnp.int32, (DEVICES, PATCH_DEV), 1).astype(jnp.float32)
    data = got[...]
    total = jnp.zeros((DEVICES, PATCH_DEV), jnp.float32)
    for k in range(2):
        hit = data[:, SLOT_LANE + k : SLOT_LANE + k + 1] == patch
        total = total + jnp.where(hit, data[:, k : k + 1], 0.0)
    out[...] = jnp.sum(total, axis=0, keepdims=True)


VMEM = pl.BlockSpec(memory_space=pltpu.VMEM)
LIMIT = 6 * 2**20


def vmem(*shape):
    return pltpu.VMEM(shape, jnp.float32)


def call(kernel, ins, outs, scratch=(), aliases=None, flops=0):
    held = [pltpu.with_memory_space_constraint(x, pltpu.VMEM) for x in ins]
    return pl.pallas_call(
        kernel,
        out_shape=outs,
        in_specs=[VMEM] * len(ins),
        out_specs=[VMEM] * len(outs),
        scratch_shapes=list(scratch),
        input_output_aliases=aliases or {},
        compiler_params=pltpu.CompilerParams(vmem_limit_bytes=LIMIT),
        cost_estimate=pl.CostEstimate(flops=flops, bytes_accessed=0, transcendentals=0),
    )(*held)


EXT = vmem(Q, CX + 2, EXT_Y, NZ)
FIELD = vmem(Q, CX, CY, NZ)
NODE = vmem(CX, CY, NZ)
X_MESSAGE = vmem(88, NZ)
Y_MESSAGE = vmem(80, NZ)
SQUARE = vmem(128, 128)


def shift(block, axis, step):
    count = lax.axis_size(axis)
    return lax.ppermute(block, axis, [(i, (i + step) % count) for i in range(count)])


def exchange(messages, direction):
    x_up, x_down, y_up, y_down = messages
    x_low = shift(x_up, "gx", 1)
    x_high = shift(x_down, "gx", -1)
    y_up, y_down = call(
        functools.partial(corner_kernel, direction=direction),
        [x_low, x_high, y_up, y_down],
        [Y_MESSAGE, Y_MESSAGE],
        aliases={2: 0, 3: 1},
    )
    y_low = shift(y_up, "gy", 1)
    y_high = shift(y_down, "gy", -1)
    return x_low, x_high, y_low, y_high


def body(populations, porosity, adjoint_in, porous, walls, owners, slots):
    owner_row = jnp.pad(owners.reshape(1, 64).astype(jnp.float32), ((0, 0), (0, 64)))
    slot_row = jnp.pad(slots.reshape(1, 64).astype(jnp.float32), ((0, 0), (0, 64)))
    ext, gap, frac, mask, vel, *messages = call(
        forward_kernel,
        [populations, porosity, porous, walls],
        [EXT, FIELD, NODE, NODE, vmem(3, CX, CY, NZ)] + [X_MESSAGE] * 2 + [Y_MESSAGE] * 2,
    )
    halos = exchange(messages, 1)
    owner_of, place, slot = call(routing_kernel, [owner_row, slot_row], [SQUARE] * 3)
    _, late, sens, *messages = call(
        late_kernel,
        [ext, *halos, adjoint_in, frac, mask],
        [EXT, EXT, NODE] + [X_MESSAGE] * 2 + [Y_MESSAGE] * 2,
        aliases={0: 0},
    )
    halos = exchange(messages, -1)
    late, send = call(
        early_sens_kernel,
        [late, *halos, gap, mask, sens, owner_of, place, slot],
        [EXT, SQUARE],
        scratch=[pltpu.VMEM((128, 128), jnp.float32)],
        aliases={0: 0},
    )
    got = lax.all_to_all(send, ("gx", "gy"), split_axis=0, concat_axis=0, tiled=True)
    held = [pltpu.with_memory_space_constraint(x, pltpu.VMEM) for x in (late, frac, vel)]
    adjoint_out = pl.pallas_call(
        adjoint_kernel,
        out_shape=jax.ShapeDtypeStruct((Q, CX, CY, NZ), jnp.float32),
        in_specs=[VMEM] * 3,
        out_specs=pl.BlockSpec(memory_space=pl.ANY),
        scratch_shapes=[
            pltpu.VMEM((CX, Q, CY, NZ), jnp.float32),
            pltpu.SemaphoreType.DMA((CX,)),
        ],
        compiler_params=pltpu.CompilerParams(vmem_limit_bytes=LIMIT),
        cost_estimate=pl.CostEstimate(
            flops=20_000_000, bytes_accessed=5_000_000, transcendentals=0
        ),
    )(*held)
    (patch,) = call(owner_kernel, [got], [vmem(1, PATCH_DEV)])
    return adjoint_out, patch.reshape(PATCH_DEV)


def solution(mesh):
    return jax.shard_map(
        body,
        mesh=mesh,
        in_specs=(
            P(None, "gx", "gy", None),
            P("gx", "gy", None),
            P(None, "gx", "gy", None),
            P("gx", "gy", None),
            P("gx", "gy", None),
            P("gx", "gy", None, None),
            P("gx", "gy", None),
        ),
        out_specs=(P(None, "gx", "gy", None), P(("gx", "gy"))),
        check_vma=False,
    )
```

profile of v0, /device:TPU:1, one launch (start us, length us, event | category | flops | bytes accessed | tf_op | source)
XLA Modules:
  0.0 61.7 jit_solution(1024647148672313275)
XLA Ops:
  0.6 0.0 copy-start.3
  0.6 1.7 %copy-done.3 = f32[19,16,16,128]{3,2,1,0:T(8,128)S(1)} copy-done((f32[19,16,16,128]{3,2,1,0:T(8,128)S(1)}, f32[19,16,16,128]{3,2,1,0:T(8,128)}, u32[]{:S(2)}) %copy-start.3) | copy-done | bytes 2490392
  2.3 0.0 copy-start.4
  2.3 0.9 %copy-done.4 = f32[16,16,128]{2,1,0:T(8,128)S(1)} copy-done((f32[16,16,128]{2,1,0:T(8,128)S(1)}, f32[16,16,128]{2,1,0:T(8,128)}, u32[]{:S(2)}) %copy-start.4) | copy-done | bytes 131096
  3.2 0.0 copy-start.5
  3.2 0.9 %copy-done.5 = s32[16,16,128]{2,1,0:T(8,128)S(1)} copy-done((s32[16,16,128]{2,1,0:T(8,128)S(1)}, s32[16,16,128]{2,1,0:T(8,128)}, u32[]{:S(2)}) %copy-start.5) | copy-done | bytes 131096
  4.1 0.0 copy-start.6
  4.1 0.9 %copy-done.6 = s32[16,16,128]{2,1,0:T(8,128)S(1)} copy-done((s32[16,16,128]{2,1,0:T(8,128)S(1)}, s32[16,16,128]{2,1,0:T(8,128)}, u32[]{:S(2)}) %copy-start.6) | copy-done | bytes 131096
  5.0 0.0 copy-start.7
  5.1 0.0 copy-start.8
  5.1 2.5 %shard_map.86 = (f32[19,18,32,128]{3,2,1,0:T(8,128)S(1)}, f32[19,16,16,128]{3,2,1,0:T(8,128)S(1)}, f32[16,16,128]{2,1,0:T(8,128)S(1)}, f32[16,16,128]{2,1,0:T(8,...) custom-call(f32[19,16,16,128]{3,2,1,0:T(8,128)S(1)} %copy-done.3, ...), custom_call_target="tpu_custom_call" | custom-call | tf_op jit(solution)/shard_map/pallas_call | solution.py:357
  7.6 2.6 %collective-permute-start = (f32[88,128]{1,0:T(8,128)S(1)}, f32[88,128]{1,0:T(8,128)S(1)}, u32[]{:S(2)}, u32[]{:S(2)}) collective-permute-start(f32[88,128]{1,0:T(8,128)S(1)} %get-tuple-element.27), channel_id=1, source_target_pairs={{0,16},{16,32},{32,48},{48,64},{64,80},{80,96},{96,112},{112,0},{1... | collective-permute-start | bytes 135176 | tf_op jit(solution)/shard_map/ppermute | solution.py:379
  10.2 0.0 collective-permute-start.1
  10.2 1.1 %collective-permute-done.x_low.xl = f32[88,128]{1,0:T(8,128)S(1)} collective-permute-done((f32[88,128]{1,0:T(8,128)S(1)}, f32[88,128]{1,0:T(8,128)S(1)}, u32[]{:S(2)}, u32[]{:S(2)}) %collective-permute-start) | collective-permute-done | bytes 45088 | tf_op jit(solution)/shard_map/ppermute | solution.py:379
  11.3 2.3 %collective-permute-done.1.x_high.xh = f32[88,128]{1,0:T(8,128)S(1)} collective-permute-done((f32[88,128]{1,0:T(8,128)S(1)}, f32[88,128]{1,0:T(8,128)S(1)}, u32[]{:S(2)}, u32[]{:S(2)}) %collective-permute-start.1) | collective-permute-done | bytes 45088 | tf_op jit(solution)/shard_map/ppermute | solution.py:379
  13.6 1.3 %collective-permute-start.2 = (f32[80,128]{1,0:T(8,128)S(1)}, f32[80,128]{1,0:T(8,128)S(1)}, u32[]{:S(2)}, u32[]{:S(2)}) collective-permute-start(f32[80,128]{1,0:T(8,128)S(1)} %get-tuple-element.31), channel_id=1, source_target_pairs={{0,1},{1,2},{2,3},{3,4},{4,5},{5,6},{6,7},{7,8},{8,9},{9,10},{10,1... | collective-permute-start | bytes 122888 | tf_op jit(solution)/shard_map/ppermute | solution.py:379
  14.9 4.9 %collective-permute-start.3 = (f32[80,128]{1,0:T(8,128)S(1)}, f32[80,128]{1,0:T(8,128)S(1)}, u32[]{:S(2)}, u32[]{:S(2)}) collective-permute-start(f32[80,128]{1,0:T(8,128)S(1)} %get-tuple-element.32), channel_id=1, source_target_pairs={{0,15},{1,0},{2,1},{3,2},{4,3},{5,4},{6,5},{7,6},{8,7},{9,8},{10,9... | collective-permute-start | bytes 122888 | tf_op jit(solution)/shard_map/ppermute | solution.py:379
  19.9 1.8 %collective-permute-done.2.yl = f32[80,128]{1,0:T(8,128)S(1)} collective-permute-done((f32[80,128]{1,0:T(8,128)S(1)}, f32[80,128]{1,0:T(8,128)S(1)}, u32[]{:S(2)}, u32[]{:S(2)}) %collective-permute-start.2) | collective-permute-done | bytes 40992 | tf_op jit(solution)/shard_map/ppermute | solution.py:379
  21.7 0.0 collective-permute-done.3.yh
  21.7 0.0 copy-start.2
  21.7 1.7 %copy-done.2 = f32[19,16,16,128]{3,2,1,0:T(8,128)S(1)} copy-done((f32[19,16,16,128]{3,2,1,0:T(8,128)S(1)}, f32[19,16,16,128]{3,2,1,0:T(8,128)}, u32[]{:S(2)}) %copy-start.2) | copy-done | bytes 2490392
  23.4 3.3 %shard_map.88 = (f32[19,18,32,128]{3,2,1,0:T(8,128)S(1)}, f32[19,18,32,128]{3,2,1,0:T(8,128)S(1)}, f32[16,16,128]{2,1,0:T(8,128)S(1)}, f32[88,128]{1,0:T(8,128)S...) custom-call(f32[19,18,32,128]{3,2,1,0:T(8,128)S(1)} %get-tuple-eleme, ...), custom_call_target="tpu_custom_call", output_to_operand_aliasing={{0}: (0, {})} | custom-call | tf_op jit(solution)/shard_map/pallas_call | solution.py:357
  26.7 0.5 collective-permute-start.4
  27.1 0.3 collective-permute-start.5
  27.4 0.0 copy-done.7
  27.4 0.9 %collective-permute-done.4.x_low.xl = f32[88,128]{1,0:T(8,128)S(1)} collective-permute-done((f32[88,128]{1,0:T(8,128)S(1)}, f32[88,128]{1,0:T(8,128)S(1)}, u32[]{:S(2)}, u32[]{:S(2)}) %collective-permute-start.4) | collective-permute-done | bytes 45088 | tf_op jit(solution)/shard_map/ppermute | solution.py:379
  28.3 2.3 %collective-permute-done.5.x_high.xh = f32[88,128]{1,0:T(8,128)S(1)} collective-permute-done((f32[88,128]{1,0:T(8,128)S(1)}, f32[88,128]{1,0:T(8,128)S(1)}, u32[]{:S(2)}, u32[]{:S(2)}) %collective-permute-start.5) | collective-permute-done | bytes 45088 | tf_op jit(solution)/shard_map/ppermute | solution.py:379
  30.6 0.0 collective-permute-start.6
  30.6 5.1 %collective-permute-start.7 = (f32[80,128]{1,0:T(8,128)S(1)}, f32[80,128]{1,0:T(8,128)S(1)}, u32[]{:S(2)}, u32[]{:S(2)}) collective-permute-start(f32[80,128]{1,0:T(8,128)S(1)} %get-tuple-element.41), channel_id=1, source_target_pairs={{0,15},{1,0},{2,1},{3,2},{4,3},{5,4},{6,5},{7,6},{8,7},{9,8},{10,9... | collective-permute-start | bytes 122888 | tf_op jit(solution)/shard_map/ppermute | solution.py:379
  35.8 0.0 copy-done.8
  35.8 0.2 shard_map.90
  36.0 1.1 %collective-permute-done.6.yl = f32[80,128]{1,0:T(8,128)S(1)} collective-permute-done((f32[80,128]{1,0:T(8,128)S(1)}, f32[80,128]{1,0:T(8,128)S(1)}, u32[]{:S(2)}, u32[]{:S(2)}) %collective-permute-start.6) | collective-permute-done | bytes 40992 | tf_op jit(solution)/shard_map/ppermute | solution.py:379
  37.1 0.0 collective-permute-done.7.yh
  37.1 1.9 %shard_map.91 = (f32[19,18,32,128]{3,2,1,0:T(8,128)S(1)}, f32[128,128]{1,0:T(8,128)}) custom-call(f32[19,18,32,128]{3,2,1,0:T(8,128)S(1)} %get-tuple-element.35.late_in, f32[88,128]{1,0:T(8,128)S(1)} %collective-permute-done.4.x_low.xl, f32[88,128]{1,0:T(8,128)S(1)} %collective-permute-done.5.x_high.xh, ...), custom_call_target="tpu_custom_call", output_to_operand_aliasing={{0}: (0, {})} | custom-call | tf_op jit(solution)/shard_map/pallas_call | solution.py:357
  39.1 0.0 copy-start
  39.1 2.4 %copy-done = f32[19,18,32,128]{3,2,1,0:T(8,128)} copy-done((f32[19,18,32,128]{3,2,1,0:T(8,128)}, f32[19,18,32,128]{3,2,1,0:T(8,128)S(1)}, u32[]{:S(2)}) %copy-start) | copy-done | bytes 5603352
  41.5 9.6 %all-to-all-start = ((f32[128,1,128]{2,1,0:T(1,128)}), f32[128,1,128]{2,1,0:T(1,128)S(1)}, u32[]{:S(2)}, u32[]{:S(2)}) async-start(f32[128,1,128]{2,1,0:T(1,128)} %bitcast.3), calls=%async_computation | async-start | bytes 131072 | tf_op jit(solution)/shard_map/all_to_all | solution.py:421
  51.2 0.0 copy-start.1
  51.2 2.6 %copy-done.1 = f32[19,18,32,128]{3,2,1,0:T(8,128)S(1)} copy-done((f32[19,18,32,128]{3,2,1,0:T(8,128)S(1)}, f32[19,18,32,128]{3,2,1,0:T(8,128)}, u32[]{:S(2)}) %copy-start.1) | copy-done | bytes 5603352
  53.8 2.0 %shard_map.92 = f32[19,16,16,128]{3,2,1,0:T(8,128)} custom-call(f32[19,18,32,128]{3,2,1,0:T(8,128)S(1)} %copy-done.1, f32[16,16,128]{2,1,0:T(8,128)S(1)} %get-tuple-element.33.frac, f32[3,16,16,128]{3,2,1,0:T(8,128)S(1)} %get-tuple-element.48.vel), custom_call_target="tpu_custom_call" | custom-call | flops 20000000 | bytes 5000000 | tf_op jit(solution)/shard_map/pallas_call | solution.py:423
  55.8 5.2 %all-to-all-done = f32[128,1,128]{2,1,0:T(1,128)S(1)} async-done(((f32[128,1,128]{2,1,0:T(1,128)}), f32[128,1,128]{2,1,0:T(1,128)S(1)}, u32[]{:S(2)}, u32[]{:S(2)}) %all-to-all-start) | async-done | bytes 65568 | tf_op jit(solution)/shard_map/all_to_all | solution.py:421
  61.0 0.1 shard_map.93
  61.1 0.6 copy.22
  (6 shorter events, 0.0 us)
Async XLA Ops:
  0.6 1.7 %copy-start.3 = (f32[19,16,16,128]{3,2,1,0:T(8,128)S(1)}, f32[19,16,16,128]{3,2,1,0:T(8,128)}, u32[]{:S(2)}) copy-start(f32[19,16,16,128]{3,2,1,0:T(8,128)} %f.1) | copy-start | bytes 7471108
  2.3 0.9 %copy-start.4 = (f32[16,16,128]{2,1,0:T(8,128)S(1)}, f32[16,16,128]{2,1,0:T(8,128)}, u32[]{:S(2)}) copy-start(f32[16,16,128]{2,1,0:T(8,128)} %porosity.1) | copy-start | bytes 393220
  3.2 0.9 %copy-start.5 = (s32[16,16,128]{2,1,0:T(8,128)S(1)}, s32[16,16,128]{2,1,0:T(8,128)}, u32[]{:S(2)}) copy-start(s32[16,16,128]{2,1,0:T(8,128)} %porous.1) | copy-start | bytes 393220
  4.1 0.9 %copy-start.6 = (s32[16,16,128]{2,1,0:T(8,128)S(1)}, s32[16,16,128]{2,1,0:T(8,128)}, u32[]{:S(2)}) copy-start(s32[16,16,128]{2,1,0:T(8,128)} %walls.1) | copy-start | bytes 393220
  5.0 22.4 %copy-start.7 = (s32[1,1,64,1]{2,3,1,0:T(1,128)S(1)}, s32[1,1,64,1]{2,3,1,0:T(1,128)}, u32[]{:S(2)}) copy-start(s32[1,1,64,1]{2,3,1,0:T(1,128)} %param.12) | copy-start | bytes 772
  5.1 30.7 %copy-start.8 = (s32[1,1,64]{2,1,0:T(1,128)S(1)}, s32[1,1,64]{2,1,0:T(1,128)}, u32[]{:S(2)}) copy-start(s32[1,1,64]{2,1,0:T(1,128)} %param.13) | copy-start | bytes 772
  7.6 3.8 %collective-permute-start = (f32[88,128]{1,0:T(8,128)S(1)}, f32[88,128]{1,0:T(8,128)S(1)}, u32[]{:S(2)}, u32[]{:S(2)}) collective-permute-start(f32[88,128]{1,0:T(8,128)S(1)} %get-tuple-element.27), channel_id=1, source_target_pairs={{0,16},{16,32},{32,48},{48,64},{64,80},{80,96},{96,112},{112,0},{1... | collective-permute-start | bytes 135176 | tf_op jit(solution)/shard_map/ppermute | solution.py:379
  10.2 3.5 %collective-permute-start.1 = (f32[88,128]{1,0:T(8,128)S(1)}, f32[88,128]{1,0:T(8,128)S(1)}, u32[]{:S(2)}, u32[]{:S(2)}) collective-permute-start(f32[88,128]{1,0:T(8,128)S(1)} %get-tuple-element.28), channel_id=1, source_target_pairs={{0,112},{16,0},{32,16},{48,32},{64,48},{80,64},{96,80},{112,96},{1... | collective-permute-start | bytes 135176 | tf_op jit(solution)/shard_map/ppermute | solution.py:379
  13.6 8.0 %collective-permute-start.2 = (f32[80,128]{1,0:T(8,128)S(1)}, f32[80,128]{1,0:T(8,128)S(1)}, u32[]{:S(2)}, u32[]{:S(2)}) collective-permute-start(f32[80,128]{1,0:T(8,128)S(1)} %get-tuple-element.31), channel_id=1, source_target_pairs={{0,1},{1,2},{2,3},{3,4},{4,5},{5,6},{6,7},{7,8},{8,9},{9,10},{10,1... | collective-permute-start | bytes 122888 | tf_op jit(solution)/shard_map/ppermute | solution.py:379
  14.9 6.7 %collective-permute-start.3 = (f32[80,128]{1,0:T(8,128)S(1)}, f32[80,128]{1,0:T(8,128)S(1)}, u32[]{:S(2)}, u32[]{:S(2)}) collective-permute-start(f32[80,128]{1,0:T(8,128)S(1)} %get-tuple-element.32), channel_id=1, source_target_pairs={{0,15},{1,0},{2,1},{3,2},{4,3},{5,4},{6,5},{7,6},{8,7},{9,8},{10,9... | collective-permute-start | bytes 122888 | tf_op jit(solution)/shard_map/ppermute | solution.py:379
  21.7 1.7 %copy-start.2 = (f32[19,16,16,128]{3,2,1,0:T(8,128)S(1)}, f32[19,16,16,128]{3,2,1,0:T(8,128)}, u32[]{:S(2)}) copy-start(f32[19,16,16,128]{3,2,1,0:T(8,128)} %adjoint.1) | copy-start | bytes 7471108
  26.7 1.6 %collective-permute-start.4 = (f32[88,128]{1,0:T(8,128)S(1)}, f32[88,128]{1,0:T(8,128)S(1)}, u32[]{:S(2)}, u32[]{:S(2)}) collective-permute-start(f32[88,128]{1,0:T(8,128)S(1)} %get-tuple-element.36), channel_id=1, source_target_pairs={{0,16},{16,32},{32,48},{48,64},{64,80},{80,96},{96,112},{112,0},{1... | collective-permute-start | bytes 135176 | tf_op jit(solution)/shard_map/ppermute | solution.py:379
  27.1 3.5 %collective-permute-start.5 = (f32[88,128]{1,0:T(8,128)S(1)}, f32[88,128]{1,0:T(8,128)S(1)}, u32[]{:S(2)}, u32[]{:S(2)}) collective-permute-start(f32[88,128]{1,0:T(8,128)S(1)} %get-tuple-element.37), channel_id=1, source_target_pairs={{0,112},{16,0},{32,16},{48,32},{64,48},{80,64},{96,80},{112,96},{1... | collective-permute-start | bytes 135176 | tf_op jit(solution)/shard_map/ppermute | solution.py:379
  30.6 6.5 %collective-permute-start.6 = (f32[80,128]{1,0:T(8,128)S(1)}, f32[80,128]{1,0:T(8,128)S(1)}, u32[]{:S(2)}, u32[]{:S(2)}) collective-permute-start(f32[80,128]{1,0:T(8,128)S(1)} %get-tuple-element.40), channel_id=1, source_target_pairs={{0,1},{1,2},{2,3},{3,4},{4,5},{5,6},{6,7},{7,8},{8,9},{9,10},{10,1... | collective-permute-start | bytes 122888 | tf_op jit(solution)/shard_map/ppermute | solution.py:379
  30.6 6.5 %collective-permute-start.7 = (f32[80,128]{1,0:T(8,128)S(1)}, f32[80,128]{1,0:T(8,128)S(1)}, u32[]{:S(2)}, u32[]{:S(2)}) collective-permute-start(f32[80,128]{1,0:T(8,128)S(1)} %get-tuple-element.41), channel_id=1, source_target_pairs={{0,15},{1,0},{2,1},{3,2},{4,3},{5,4},{6,5},{7,6},{8,7},{9,8},{10,9... | collective-permute-start | bytes 122888 | tf_op jit(solution)/shard_map/ppermute | solution.py:379
  39.1 2.4 %copy-start = (f32[19,18,32,128]{3,2,1,0:T(8,128)}, f32[19,18,32,128]{3,2,1,0:T(8,128)S(1)}, u32[]{:S(2)}) copy-start(f32[19,18,32,128]{3,2,1,0:T(8,128)S(1)} %get-tuple-element.47.late) | copy-start | bytes 16809988
  41.5 19.4 %all-to-all-start = ((f32[128,1,128]{2,1,0:T(1,128)}), f32[128,1,128]{2,1,0:T(1,128)S(1)}, u32[]{:S(2)}, u32[]{:S(2)}) async-start(f32[128,1,128]{2,1,0:T(1,128)} %bitcast.3), calls=%async_computation | async-start | bytes 131072 | tf_op jit(solution)/shard_map/all_to_all | solution.py:421
  51.2 2.6 %copy-start.1 = (f32[19,18,32,128]{3,2,1,0:T(8,128)S(1)}, f32[19,18,32,128]{3,2,1,0:T(8,128)}, u32[]{:S(2)}) copy-start(f32[19,18,32,128]{3,2,1,0:T(8,128)} %copy-done) | copy-start | bytes 16809988
where the time goes:
time: 62 us; the launch traced here: 61.7 us
  starting transfers between devices  24.3 us (39%)
  waiting for transfers between devices  14.8 us (24%)
  local copies, waits for them, and re-layouts  11.7 us (19%)
  Pallas kernels  10.1 us (16%)
  between operations  0.72 us (1%)
    ppermute x8, starting transfers between devices, shift(): lax.ppermute(block, axis, [(i, (i + step) % count) for i in range(count)])  14.7 us
    unnamed x19, local copies, waits for them, and re-layouts  11.7 us
    all_to_all x1, starting transfers between devices, body(): lax.all_to_all(send, ('gx', 'gy'), split_axis=0, concat_axis=0, tiled=True)  9.64 us
    ppermute x8, waiting for transfers between devices, shift(): lax.ppermute(block, axis, [(i, (i + step) % count) for i in range(count)])  9.63 us
    pallas_call x7, Pallas kernels, call(): pl.pallas_call(kernel, out_shape=outs, in_specs=[VMEM] * len(ins), out_sp...  8.08 us
    all_to_all x1, waiting for transfers between devices, body(): lax.all_to_all(send, ('gx', 'gy'), split_axis=0, concat_axis=0, tiled=True)  5.21 us
    pallas_call x1, Pallas kernels, body(): pl.pallas_call(adjoint_kernel, out_shape=jax.ShapeDtypeStruct((Q, CX, CY,...  1.98 us
  transfers between devices with their start and end apart: 9, of which 7 were waited for; matrix products, arithmetic and copies ran while one was open for 0% of the time, Pallas kernels for 4%

commit v1 on v0

v1 whole, which is shorter than its diff:
```python
import functools

import jax
import jax.numpy as jnp
from jax import lax
from jax.experimental import pallas as pl
from jax.experimental.pallas import tpu as pltpu
from jax.sharding import PartitionSpec as P

Q = 19
CX = 16
CY = 16
NZ = 128
TILE = 8
PAD_Y = 8
EXT_Y = 32
EXT_XB = 10
BLOCK_ROWS = EXT_XB * EXT_Y
DEVICES = 128
PATCH_DEV = 256
SLOT_LANE = 64
FACE = 80
META = 160
MESSAGE_ROWS = 168

velocities = [
    (0, 0, 0),
    (1, 0, 0),
    (-1, 0, 0),
    (0, 1, 0),
    (0, -1, 0),
    (0, 0, 1),
    (0, 0, -1),
    (1, 1, 0),
    (-1, -1, 0),
    (1, -1, 0),
    (-1, 1, 0),
    (1, 0, 1),
    (-1, 0, -1),
    (1, 0, -1),
    (-1, 0, 1),
    (0, 1, 1),
    (0, -1, -1),
    (0, 1, -1),
    (0, -1, 1),
]
opposite = [0, 2, 1, 4, 3, 6, 5, 8, 7, 10, 9, 12, 11, 14, 13, 16, 15, 18, 17]
RATE2, RATE3, RATE4 = 1.25, 1.5, 1.4


def moving(axis, sign, direction):
    return [i for i in range(Q) if direction * velocities[i][axis] == sign]


def edge(f, first):
    s, d = f[first] + f[first + 1], f[first] - f[first + 1]
    s2, d2 = f[first + 2] + f[first + 3], f[first + 2] - f[first + 3]
    return s, d, s2, d2


def off_equilibrium(f):
    sx, dx = f[1] + f[2], f[1] - f[2]
    sy, dy = f[3] + f[4], f[3] - f[4]
    sz, dz = f[5] + f[6], f[5] - f[6]
    s7, d7, s9, d9 = edge(f, 7)
    s11, d11, s13, d13 = edge(f, 11)
    s15, d15, s17, d17 = edge(f, 15)
    m220, m110, m120, m210 = s7 + s9, s7 - s9, d7 + d9, d7 - d9
    m202, m101, m102, m201 = s11 + s13, s11 - s13, d11 + d13, d11 - d13
    m022, m011, m012, m021 = s15 + s17, s15 - s17, d15 + d17, d15 - d17
    m200, m020, m002 = sx + m220 + m202, sy + m220 + m022, sz + m202 + m022
    jx, jy, jz = dx + (m120 + m102), dy + (m210 + m012), dz + (m201 + m021)
    rho = f[0] + (sx + sy + sz) + (m220 + m202 + m022)
    inv = 1.0 / rho
    ux, uy, uz = jx * inv, jy * inv, jz * inv
    qx, qy, qz = jx * ux, jy * uy, jz * uz
    third = rho * (1.0 / 3.0)
    ninth = rho * (1.0 / 9.0) - (qx + qy + qz) * (1.0 / 6.0)
    tx, ty, tz = jx * (1.0 / 3.0), jy * (1.0 / 3.0), jz * (1.0 / 3.0)
    e = {
        "200": RATE2 * (m200 - third - qx),
        "020": RATE2 * (m020 - third - qy),
        "002": RATE2 * (m002 - third - qz),
        "110": RATE2 * (m110 - jx * uy),
        "101": RATE2 * (m101 - jx * uz),
        "011": RATE2 * (m011 - jy * uz),
        "120": RATE3 * (m120 - tx),
        "102": RATE3 * (m102 - tx),
        "210": RATE3 * (m210 - ty),
        "012": RATE3 * (m012 - ty),
        "201": RATE3 * (m201 - tz),
        "021": RATE3 * (m021 - tz),
        "220": RATE4 * (m220 - ninth - 0.5 * (qx + qy)),
        "202": RATE4 * (m202 - ninth - 0.5 * (qx + qz)),
        "022": RATE4 * (m022 - ninth - 0.5 * (qy + qz)),
    }
    return (ux, uy, uz), e, (dx, dy, dz, d7, d9, d11, d13, d15, d17)


def spread(t, g, a, b):
    even, odd = t + g, t - g
    plus, minus = a + b, a - b
    return [even + plus, even - plus, odd + minus, odd - minus]


def correction(e):
    q = {k: 0.25 * v for k, v in e.items()}
    xy = spread(q["220"], q["110"], q["120"], q["210"])
    xz = spread(q["202"], q["101"], q["102"], q["201"])
    yz = spread(q["022"], q["011"], q["012"], q["021"])
    faces = []
    for second, fourth, odd in (
        ("200", ("220", "202"), ("120", "102")),
        ("020", ("220", "022"), ("210", "012")),
        ("002", ("202", "022"), ("201", "021")),
    ):
        mean = 0.5 * e[second] - 2.0 * (q[fourth[0]] + q[fourth[1]])
        lean = 2.0 * (q[odd[0]] + q[odd[1]])
        faces += [mean - lean, mean + lean]
    rest = (e["220"] + e["202"] + e["022"]) - (e["200"] + e["020"] + e["002"])
    return [rest] + faces + xy + xz + yz


def covector(b):
    hx, dx = 0.5 * (b[1] + b[2]), b[1] - b[2]
    hy, dy = 0.5 * (b[3] + b[4]), b[3] - b[4]
    hz, dz = 0.5 * (b[5] + b[6]), b[5] - b[6]
    s7, d7, s9, d9 = edge(b, 7)
    s11, d11, s13, d13 = edge(b, 11)
    s15, d15, s17, d17 = edge(b, 15)
    gx, gy, gz = hx - b[0], hy - b[0], hz - b[0]
    kx, ky, kz = 0.5 * dx, 0.5 * dy, 0.5 * dz
    t = {
        "200": gx,
        "020": gy,
        "002": gz,
        "110": 0.25 * (s7 - s9),
        "101": 0.25 * (s11 - s13),
        "011": 0.25 * (s15 - s17),
        "120": 0.25 * (d7 + d9) - kx,
        "102": 0.25 * (d11 + d13) - kx,
        "210": 0.25 * (d7 - d9) - ky,
        "012": 0.25 * (d15 + d17) - ky,
        "201": 0.25 * (d11 - d13) - kz,
        "021": 0.25 * (d15 - d17) - kz,
        "220": 0.25 * (s7 + s9) - gx - hy,
        "202": 0.25 * (s11 + s13) - gx - hz,
        "022": 0.25 * (s15 + s17) - gy - hz,
    }
    return t, (dx, dy, dz, d7, d9, d11, d13, d15, d17)


def pull_back(b, t, u, fraction):
    rates = {k: (RATE2, RATE3, RATE4)[sum(map(int, k)) - 2] for k in t}
    n = {k: rates[k] * v for k, v in t.items()}
    ux, uy, uz = u
    fourth = n["220"] + n["202"] + n["022"]
    second = n["200"] + n["020"] + n["002"]
    part = fourth * (1.0 / 3.0)
    ax = n["200"] + part - 0.5 * n["022"]
    ay = n["020"] + part - 0.5 * n["202"]
    az = n["002"] + part - 0.5 * n["220"]
    rx = 2.0 * ax * ux + n["110"] * uy + n["101"] * uz
    ry = 2.0 * ay * uy + n["110"] * ux + n["011"] * uz
    rz = 2.0 * az * uz + n["101"] * ux + n["011"] * uy
    p0 = second * (1.0 / 3.0) + fourth * (1.0 / 9.0) - 0.5 * (rx * ux + ry * uy + rz * uz)
    px = rx + (n["120"] + n["102"]) * (1.0 / 3.0)
    py = ry + (n["210"] + n["012"]) * (1.0 / 3.0)
    pz = rz + (n["201"] + n["021"]) * (1.0 / 3.0)
    ex, ey, ez = p0 - n["200"], p0 - n["020"], p0 - n["002"]
    h = [p0, ex + px, ex - px, ey + py, ey - py, ez + pz, ez - pz]
    h += spread(ex - n["020"] - n["220"], -n["110"], px - n["120"], py - n["210"])
    h += spread(ex - n["002"] - n["202"], -n["101"], px - n["102"], pz - n["201"])
    h += spread(ey - n["002"] - n["022"], -n["011"], py - n["012"], pz - n["021"])
    open_part = 1.0 - fraction
    return [open_part * (b[i] + h[i]) + fraction * b[opposite[i]] for i in range(Q)]


def put_moved(field, i, x, yt, value, direction):
    cx, cy, cz = (direction * c for c in velocities[i])
    if cz:
        value = pltpu.roll(value, cz % NZ, axis=1)
    x = (x + cx) & (CX - 1) if cx else x
    row = yt * TILE + cy
    if row < 0:
        field[i, x, pl.ds(0, TILE - 1), :] = value[1:]
        field[i, x, pl.ds(CY - 1, 1), :] = value[:1]
    elif row + TILE > CY:
        field[i, x, pl.ds(row, TILE - 1), :] = value[:-1]
        field[i, x, pl.ds(0, 1), :] = value[-1:]
    else:
        field[i, x, pl.ds(row, TILE), :] = value


def fill_messages(fields, direction, x_up, x_down, y_up, y_down):
    for n, field in enumerate(fields):
        for sign, x, message in ((1, 0, x_up), (-1, CX - 1, x_down)):
            for k, i in enumerate(moving(0, sign, direction)):
                message[pl.ds(n * FACE + k * CY, CY), :] = field[i, x]
        for sign, row, message in ((1, 0, y_up), (-1, CY - 1, y_down)):
            for k, i in enumerate(moving(1, sign, direction)):
                for x in range(CX):
                    message[pl.ds(n * FACE + k * CX + x, 1), :] = field[i, x, pl.ds(row, 1), :]


def fill_ring(fields, direction, x_low, x_high, y_low, y_high):
    for n, field in enumerate(fields):
        for sign, x, message in ((1, 0, x_low), (-1, CX - 1, x_high)):
            for k, i in enumerate(moving(0, sign, direction)):
                field[i, x] = message[pl.ds(n * FACE + k * CY, CY), :]
        for sign, row, message in ((1, 0, y_low), (-1, CY - 1, y_high)):
            for k, i in enumerate(moving(1, sign, direction)):
                for x in range(CX):
                    field[i, x, pl.ds(row, 1), :] = message[pl.ds(n * FACE + k * CX + x, 1), :]


def rows(yt):
    return pl.ds(yt * TILE, TILE)


def iota(shape, dim):
    return lax.broadcasted_iota(jnp.int32, shape, dim)


def column(row, pick):
    return jnp.sum(jnp.where(pick, row, 0.0), axis=1, keepdims=True)


def block_numbers(owners, slots, table, x_up, x_down, y_up, y_down):
    shape = (64, 64)
    row, lane = iota(shape, 0), iota(shape, 1)
    same = row == lane
    owner_row, slot_row = owners[...].astype(jnp.float32), slots[...].astype(jnp.float32)
    owner_col = column(owner_row, same)
    earlier = (owner_row == owner_col) & (lane < row)
    rank = jnp.sum(jnp.where(earlier, 1.0, 0.0), axis=1, keepdims=True)
    number = owner_col * 1024.0 + column(slot_row, same) * 4.0 + rank
    wide = (64, NZ)
    spot = iota(wide, 1) == (iota(wide, 0) & 7) + 1
    spread_out = jnp.where(spot, number, 0.0)
    table[...] = jnp.zeros((16, NZ), jnp.float32)
    for xb in range(8):
        line = jnp.sum(spread_out[xb * 8 : xb * 8 + 8], axis=0, keepdims=True)
        table[pl.ds(xb + 1, 1), :] = line
    held = table[...]
    x_up[pl.ds(META, 1), :] = held[8:9]
    x_down[pl.ds(META, 1), :] = held[1:2]
    eye = iota((16, NZ), 0) == iota((16, NZ), 1)
    for yb, message in ((8, y_up), (1, y_down)):
        part = jnp.where(eye, held[:, yb : yb + 1], 0.0)
        message[pl.ds(META, 1), :] = jnp.sum(part, axis=0, keepdims=True)


def forward_kernel(
    f_hbm, porosity_hbm, adjoint_hbm, porous_hbm, walls_hbm, owners_hbm, slots_hbm,
    moved, gap, adjoint, frac, mask, vel, table, xu, xd, yu, yd,
    f, porosity, porous, walls, owners, slots, f_sems, sems,
):
    def plane(x):
        return pltpu.make_async_copy(f_hbm.at[:, x], f.at[:, x], f_sems.at[x])

    small = [
        pltpu.make_async_copy(source, target, sems.at[k])
        for k, (source, target) in enumerate(
            (
                (owners_hbm, owners),
                (slots_hbm, slots),
                (porosity_hbm, porosity),
                (porous_hbm, porous),
                (walls_hbm, walls),
            )
        )
    ]
    later = pltpu.make_async_copy(adjoint_hbm, adjoint, sems.at[5])
    for copy in small:
        copy.start()
    for x in range(CX):
        plane(x).start()
    later.start()
    small[0].wait()
    small[1].wait()
    block_numbers(owners, slots, table, xu, xd, yu, yd)
    for copy in small[2:]:
        copy.wait()

    @pl.loop(0, CX)
    def _(x):
        plane(x).wait()
        for yt in range(CY // TILE):
            at = (x, rows(yt))
            pops = [f[i, x, rows(yt), :] for i in range(Q)]
            wall = walls[at] == 1
            panel = porous[at].astype(jnp.float32)
            fraction = jnp.where(wall, 1.0, panel * porosity[at])
            open_panel = jnp.where(wall, 0.0, panel)
            frac[at] = fraction
            mask[at] = open_panel
            u, e, _ = off_equilibrium(pops)
            for axis in range(3):
                vel[axis, x, rows(yt), :] = u[axis]
            c = correction(e)
            for i in range(Q):
                relaxed = pops[i] - c[i]
                change = pops[opposite[i]] - relaxed
                put_moved(gap, i, x, yt, open_panel * change, 1)
                put_moved(moved, i, x, yt, relaxed + fraction * change, 1)

    fill_messages((moved, gap), 1, xu, xd, yu, yd)
    later.wait()


def corner_kernel(x_low, x_high, up_in, down_in, up, down, *, direction, fields):
    del up_in, down_in
    for sign, row, message in ((1, 0, up), (-1, CY - 1, down)):
        for k, i in enumerate(moving(1, sign, direction)):
            cx = direction * velocities[i][0]
            if not cx:
                continue
            source, x = (x_low, 0) if cx == 1 else (x_high, CX - 1)
            k_x = moving(0, cx, direction).index(i)
            for n in range(fields):
                message[pl.ds(n * FACE + k * CX + x, 1), :] = source[
                    pl.ds(n * FACE + k_x * CY + row, 1), :
                ]
    if fields == 2:
        lane = iota((1, NZ), 1)
        for yb, message in ((8, up), (1, down)):
            low = jnp.sum(jnp.where(lane == yb, x_low[pl.ds(META, 1), :], 0.0))
            high = jnp.sum(jnp.where(lane == yb, x_high[pl.ds(META, 1), :], 0.0))
            line = message[pl.ds(META, 1), :]
            line = jnp.where(lane == 0, low, jnp.where(lane == 9, high, line))
            message[pl.ds(META, 1), :] = line


def routing_kernel(table, x_low, x_high, y_low, y_high, owner_of, place, slot, ext):
    shape = (16, NZ)
    row, lane = iota(shape, 0), iota(shape, 1)
    eye = row == lane
    low = column(y_low[pl.ds(META, 1), :], eye)
    high = column(y_high[pl.ds(META, 1), :], eye)
    held = jnp.where(row == 0, x_low[pl.ds(META, 1), :], table[...])
    held = jnp.where(row == 9, x_high[pl.ds(META, 1), :], held)
    ext[...] = jnp.where(lane == 0, low, jnp.where(lane == 9, high, held))
    shape = (EXT_Y, NZ)
    row, lane = iota(shape, 0), iota(shape, 1)
    yb = jnp.right_shift(row - 6, 1)
    pick = lane == yb
    side_y = jnp.where(yb == 0, 0, jnp.where(yb == 9, 2, 1))
    used = (row >= PAD_Y - 1) & (row <= PAD_Y + CY)
    first = used & ((yb == 0) | ((row & 1) == 0))
    for xb in range(EXT_XB):
        number = column(ext[pl.ds(xb, 1), :], pick).astype(jnp.int32)
        side = side_y * 6 + (0 if xb == 0 else 4 if xb == 9 else 2)
        spot = side + (number & 3)
        line = pl.ds(xb * EXT_Y, EXT_Y)
        owner_of[line, :] = jnp.where(used & (lane == jnp.right_shift(number, 10)), 1.0, 0.0)
        place[line, :] = jnp.where(lane == spot, 1.0, 0.0)
        patch = (jnp.right_shift(number, 2) & 255).astype(jnp.float32)
        slot[line, :] = jnp.where(first & (lane == spot + SLOT_LANE), patch, 0.0)


def late_kernel(
    moved_in, gap_in, xl, xh, yl, yh, adjoint, frac, mask, owner_of, place, slot,
    moved, gap, late, send, xu, xd, yu, yd, sums, scaled,
):
    del moved_in, gap_in
    fill_ring((moved, gap), 1, xl, xh, yl, yh)
    sums[...] = jnp.zeros((EXT_XB, EXT_Y, NZ), jnp.float32)

    @pl.loop(0, CX // 2)
    def _(xb):
        for yt in range(CY // TILE):
            parts = {}
            for half in range(2):
                x = xb * 2 + half
                at = (x, rows(yt))
                read = [moved[i, x, rows(yt), :] for i in range(Q)]
                u, e, df = off_equilibrium(read)
                b = [adjoint[i, x, rows(yt), :] for i in range(Q)]
                t, db = covector(b)
                total = sum(t[k] * e[k] for k in t) - sum(p * q for p, q in zip(db, df))
                total = mask[at] * total
                out = pull_back(b, t, u, frac[at])
                key = (0, 0)
                parts[key] = parts[key] + total if key in parts else total
                for i in range(Q):
                    cx, cy, _ = velocities[i]
                    key = ((half - cx) // 2, cy)
                    early = out[i] * gap[i, x, rows(yt), :]
                    parts[key] = parts[key] + early if key in parts else early
                    put_moved(late, i, x, yt, out[i], -1)
            for (step, cy), part in parts.items():
                at = (xb + 1 + step, pl.ds(PAD_Y + yt * TILE - cy, TILE))
                sums[at] = sums[at] + part

    for xb in range(EXT_XB):
        line = pl.ds(xb * EXT_Y, EXT_Y)
        scaled[line, :] = (
            jnp.sum(sums[xb], axis=1, keepdims=True) * place[line, :] + slot[line, :]
        )
    send[...] = lax.dot_general(
        owner_of[...],
        scaled[...],
        (((0,), (0,)), ((), ())),
        precision=lax.Precision.HIGHEST,
        preferred_element_type=jnp.float32,
    )
    fill_messages((late,), -1, xu, xd, yu, yd)


def early_kernel(late_in, xl, xh, yl, yh, frac, vel, late, out, hold, sems):
    del late_in
    fill_ring((late,), -1, xl, xh, yl, yh)

    def plane(x):
        return pltpu.make_async_copy(hold.at[x], out.at[:, x], sems.at[x])

    @pl.loop(0, CX)
    def _(x):
        for yt in range(CY // TILE):
            b = [late[i, x, rows(yt), :] for i in range(Q)]
            t, _ = covector(b)
            u = [vel[axis, x, rows(yt), :] for axis in range(3)]
            result = pull_back(b, t, u, frac[x, rows(yt)])
            for i in range(Q):
                hold[x, i, rows(yt), :] = result[i]
        plane(x).start()

    for x in range(CX):
        plane(x).wait()


def owner_kernel(got, out):
    patch = iota((DEVICES, PATCH_DEV), 1).astype(jnp.float32)
    data = got[...]
    total = jnp.zeros((DEVICES, PATCH_DEV), jnp.float32)
    for k in range(18):
        hit = data[:, SLOT_LANE + k : SLOT_LANE + k + 1] == patch
        total = total + jnp.where(hit, data[:, k : k + 1], 0.0)
    out[...] = jnp.sum(total, axis=0, keepdims=True)


VMEM = pl.BlockSpec(memory_space=pltpu.VMEM)
ANY = pl.BlockSpec(memory_space=pl.ANY)
LIMIT = 8 * 2**20


def vmem(*shape):
    return pltpu.VMEM(shape, jnp.float32)


def call(kernel, ins, outs, scratch=(), aliases=None, flops=0, hbm_ins=0, hbm_outs=()):
    held = list(ins[:hbm_ins])
    held += [pltpu.with_memory_space_constraint(x, pltpu.VMEM) for x in ins[hbm_ins:]]
    return pl.pallas_call(
        kernel,
        out_shape=[*outs, *hbm_outs],
        in_specs=[ANY] * hbm_ins + [VMEM] * (len(ins) - hbm_ins),
        out_specs=[VMEM] * len(outs) + [ANY] * len(hbm_outs),
        scratch_shapes=list(scratch),
        input_output_aliases=aliases or {},
        compiler_params=pltpu.CompilerParams(vmem_limit_bytes=LIMIT),
        cost_estimate=pl.CostEstimate(flops=flops, bytes_accessed=0, transcendentals=0),
    )(*held)


FIELD = vmem(Q, CX, CY, NZ)
NODE = vmem(CX, CY, NZ)
MESSAGE = vmem(MESSAGE_ROWS, NZ)
SHORT_MESSAGE = vmem(FACE, NZ)
LINES = vmem(BLOCK_ROWS, NZ)


def shift(block, axis, step):
    count = lax.axis_size(axis)
    return lax.ppermute(block, axis, [(i, (i + step) % count) for i in range(count)])


def exchange(messages, direction, fields):
    x_up, x_down, y_up, y_down = messages
    x_low = shift(x_up, "gx", 1)
    x_high = shift(x_down, "gx", -1)
    y_up, y_down = call(
        functools.partial(corner_kernel, direction=direction, fields=fields),
        [x_low, x_high, y_up, y_down],
        [MESSAGE if fields == 2 else SHORT_MESSAGE] * 2,
        aliases={2: 0, 3: 1},
    )
    y_low = shift(y_up, "gy", 1)
    y_high = shift(y_down, "gy", -1)
    return x_low, x_high, y_low, y_high


def body(populations, porosity, adjoint_in, porous, walls, owners, slots):
    ints = pltpu.VMEM((CX, CY, NZ), jnp.int32)
    moved, gap, adjoint, frac, mask, vel, table, *messages = call(
        forward_kernel,
        [populations, porosity, adjoint_in, porous, walls]
        + [owners.reshape(1, 64), slots.reshape(1, 64)],
        [FIELD] * 3 + [NODE] * 2 + [vmem(3, CX, CY, NZ), vmem(16, NZ)] + [MESSAGE] * 4,
        scratch=[FIELD, NODE, ints, ints]
        + [pltpu.VMEM((1, 64), jnp.int32)] * 2
        + [pltpu.SemaphoreType.DMA((CX,)), pltpu.SemaphoreType.DMA((6,))],
        hbm_ins=7,
    )
    halos = exchange(messages, 1, 2)
    owner_of, place, slot = call(
        routing_kernel, [table, *halos], [LINES] * 3, scratch=[vmem(16, NZ)]
    )
    _, _, late, send, *messages = call(
        late_kernel,
        [moved, gap, *halos, adjoint, frac, mask, owner_of, place, slot],
        [FIELD] * 3 + [vmem(DEVICES, NZ)] + [SHORT_MESSAGE] * 4,
        scratch=[vmem(EXT_XB, EXT_Y, NZ), LINES],
        aliases={0: 0, 1: 1},
    )
    got = lax.all_to_all(send, ("gx", "gy"), split_axis=0, concat_axis=0, tiled=True)
    halos = exchange(messages, -1, 1)
    _, adjoint_out = call(
        early_kernel,
        [late, *halos, frac, vel],
        [FIELD],
        hbm_outs=[jax.ShapeDtypeStruct((Q, CX, CY, NZ), jnp.float32)],
        scratch=[vmem(CX, Q, CY, NZ), pltpu.SemaphoreType.DMA((CX,))],
        aliases={0: 0},
    )
    (patch,) = call(owner_kernel, [got], [vmem(1, PATCH_DEV)])
    return adjoint_out, patch.reshape(PATCH_DEV)


def solution(mesh):
    return jax.shard_map(
        body,
        mesh=mesh,
        in_specs=(
            P(None, "gx", "gy", None),
            P("gx", "gy", None),
            P(None, "gx", "gy", None),
            P("gx", "gy", None),
            P("gx", "gy", None),
            P("gx", "gy", None, None),
            P("gx", "gy", None),
        ),
        out_specs=(P(None, "gx", "gy", None), P(("gx", "gy"))),
        check_vma=False,
    )
```

time: 62 us -> 56.2 us (0.906)
  waiting for transfers between devices: 14.8 us -> 10.6 us
  local copies, waits for them, and re-layouts: 11.7 us -> 7.99 us
  Pallas kernels: 10.1 us -> 11.9 us
    unnamed x19 -> x15, local copies, waits for them, and re-layouts: 11.7 us -> 7.99 us
    ppermute x8, waiting for transfers between devices: 9.63 us -> 6.63 us  [shift(): lax.ppermute(block, axis, [(i, (i + step) % count) for i in range(count)])]
    pallas_call x8 -> x7, Pallas kernels: 10.1 us -> 11.9 us  [call(): pl.pallas_call(kernel, out_shape=[*outs, *hbm_outs], in_specs=[ANY] * hbm...]
    all_to_all x1, waiting for transfers between devices: 5.21 us -> 3.95 us  [body(): lax.all_to_all(send, ('gx', 'gy'), split_axis=0, concat_axis=0, tiled=True)]
    ppermute x8, starting transfers between devices: 14.7 us -> 15.4 us  [shift(): lax.ppermute(block, axis, [(i, (i + step) % count) for i in range(count)])]
  transfers between devices with their start and end apart: 9 -> 9, of which waited for: 7 -> 4; matrix products, arithmetic and copies ran while one was open for 0% -> 1% of each run, Pallas kernels for 4% -> 1%
where the time goes in v1:
time: 56.2 us; the launch traced here: 55.9 us
  starting transfers between devices  24.7 us (44%)
  Pallas kernels  11.9 us (21%)
  waiting for transfers between devices  10.6 us (19%)
  local copies, waits for them, and re-layouts  7.99 us (14%)
  between operations  0.71 us (1%)
    ppermute x8, starting transfers between devices, shift(): lax.ppermute(block, axis, [(i, (i + step) % count) for i in range(count)])  15.4 us
    pallas_call x7, Pallas kernels, call(): pl.pallas_call(kernel, out_shape=[*outs, *hbm_outs], in_specs=[ANY] * hbm...  11.9 us
    all_to_all x1, starting transfers between devices, body(): lax.all_to_all(send, ('gx', 'gy'), split_axis=0, concat_axis=0, tiled=True)  9.34 us
    unnamed x15, local copies, waits for them, and re-layouts  7.99 us
    ppermute x8, waiting for transfers between devices, shift(): lax.ppermute(block, axis, [(i, (i + step) % count) for i in range(count)])  6.63 us
    all_to_all x1, waiting for transfers between devices, body(): lax.all_to_all(send, ('gx', 'gy'), split_axis=0, concat_axis=0, tiled=True)  3.95 us
  transfers between devices with their start and end apart: 9, of which 4 were waited for; matrix products, arithmetic and copies ran while one was open for 1% of the time, Pallas kernels for 1%

profile of v1, /device:TPU:1, one launch (start us, length us, event | category | flops | bytes accessed | tf_op | source)
XLA Modules:
  0.0 55.9 jit_solution(12895517987916492440)
XLA Ops:
  0.6 0.0 copy-start
  0.6 1.7 %copy-done = f32[19,16,16,128]{3,2,1,0:T(8,128)S(1)} copy-done((f32[19,16,16,128]{3,2,1,0:T(8,128)S(1)}, f32[19,16,16,128]{3,2,1,0:T(8,128)}, u32[]{:S(2)}) %copy-start) | copy-done | bytes 2490392
  2.3 0.0 copy-start.1
  2.3 1.7 %copy-done.1 = f32[19,16,16,128]{3,2,1,0:T(8,128)S(1)} copy-done((f32[19,16,16,128]{3,2,1,0:T(8,128)S(1)}, f32[19,16,16,128]{3,2,1,0:T(8,128)}, u32[]{:S(2)}) %copy-start.1) | copy-done | bytes 2490392
  4.0 0.0 copy-start.2
  4.0 0.9 %copy-done.2 = f32[16,16,128]{2,1,0:T(8,128)S(1)} copy-done((f32[16,16,128]{2,1,0:T(8,128)S(1)}, f32[16,16,128]{2,1,0:T(8,128)}, u32[]{:S(2)}) %copy-start.2) | copy-done | bytes 131096
  4.9 0.0 copy-start.3
  4.9 0.9 %copy-done.3 = s32[16,16,128]{2,1,0:T(8,128)S(1)} copy-done((s32[16,16,128]{2,1,0:T(8,128)S(1)}, s32[16,16,128]{2,1,0:T(8,128)}, u32[]{:S(2)}) %copy-start.3) | copy-done | bytes 131096
  5.8 0.0 copy-start.4
  5.9 0.9 %copy-done.4 = s32[16,16,128]{2,1,0:T(8,128)S(1)} copy-done((s32[16,16,128]{2,1,0:T(8,128)S(1)}, s32[16,16,128]{2,1,0:T(8,128)}, u32[]{:S(2)}) %copy-start.4) | copy-done | bytes 131096
  6.8 0.0 copy-start.5
  6.8 0.7 %copy-done.5 = s32[1,1,64,1]{2,3,1,0:T(1,128)S(1)} copy-done((s32[1,1,64,1]{2,3,1,0:T(1,128)S(1)}, s32[1,1,64,1]{2,3,1,0:T(1,128)}, u32[]{:S(2)}) %copy-start.5) | copy-done | bytes 280
  7.4 0.0 copy-start.6
  7.4 0.7 %copy-done.6 = s32[1,1,64]{2,1,0:T(1,128)S(1)} copy-done((s32[1,1,64]{2,1,0:T(1,128)S(1)}, s32[1,1,64]{2,1,0:T(1,128)}, u32[]{:S(2)}) %copy-start.6) | copy-done | bytes 280
  8.1 4.6 %shard_map.86 = (f32[19,16,16,128]{3,2,1,0:T(8,128)S(1)}, f32[19,16,16,128]{3,2,1,0:T(8,128)S(1)}, f32[19,16,16,128]{3,2,1,0:T(8,128)S(1)}, f32[16,16,128]{2,1,0...) custom-call(f32[19,16,16,128]{3,2,1,0:T(8,128)S(1)} %copy-done, ...), custom_call_target="tpu_custom_call" | custom-call | tf_op jit(solution)/shard_map/pallas_call | solution.py:455
  12.6 2.6 %collective-permute-start = (f32[168,128]{1,0:T(8,128)S(1)}, f32[168,128]{1,0:T(8,128)S(1)}, u32[]{:S(2)}, u32[]{:S(2)}) collective-permute-start(f32[168,128]{1,0:T(8,128)S(1)} %get-tuple-element.29), channel_id=1, source_target_pairs={{0,16},{16,32},{32,48},{48,64},{64,80},{80,96},{96,112},{112,0},{1... | collective-permute-start | bytes 258056 | tf_op jit(solution)/shard_map/ppermute | solution.py:476
  15.3 0.0 collective-permute-start.1
  15.3 1.5 %collective-permute-done.x_low.xl = f32[168,128]{1,0:T(8,128)S(1)} collective-permute-done((f32[168,128]{1,0:T(8,128)S(1)}, f32[168,128]{1,0:T(8,128)S(1)}, u32[]{:S(2)}, u32[]{:S(2)}) %collective-permute-start) | collective-permute-done | bytes 86048 | tf_op jit(solution)/shard_map/ppermute | solution.py:476
  16.8 2.4 %collective-permute-done.1.x_high.xh = f32[168,128]{1,0:T(8,128)S(1)} collective-permute-done((f32[168,128]{1,0:T(8,128)S(1)}, f32[168,128]{1,0:T(8,128)S(1)}, u32[]{:S(2)}, u32[]{:S(2)}) %collective-permute-start.1) | collective-permute-done | bytes 86048 | tf_op jit(solution)/shard_map/ppermute | solution.py:476
  19.2 0.1 shard_map.87
  19.3 1.4 %collective-permute-start.2 = (f32[168,128]{1,0:T(8,128)S(1)}, f32[168,128]{1,0:T(8,128)S(1)}, u32[]{:S(2)}, u32[]{:S(2)}) collective-permute-start(f32[168,128]{1,0:T(8,128)S(1)} %get-tuple-element.33), channel_id=1, source_target_pairs={{0,1},{1,2},{2,3},{3,4},{4,5},{5,6},{6,7},{7,8},{8,9},{9,10},{10,1... | collective-permute-start | bytes 258056 | tf_op jit(solution)/shard_map/ppermute | solution.py:476
  20.7 5.0 %collective-permute-start.3 = (f32[168,128]{1,0:T(8,128)S(1)}, f32[168,128]{1,0:T(8,128)S(1)}, u32[]{:S(2)}, u32[]{:S(2)}) collective-permute-start(f32[168,128]{1,0:T(8,128)S(1)} %get-tuple-element.34), channel_id=1, source_target_pairs={{0,15},{1,0},{2,1},{3,2},{4,3},{5,4},{6,5},{7,6},{8,7},{9,8},{10,9... | collective-permute-start | bytes 258056 | tf_op jit(solution)/shard_map/ppermute | solution.py:476
  25.7 2.7 %collective-permute-done.2.y_low.yl = f32[168,128]{1,0:T(8,128)S(1)} collective-permute-done((f32[168,128]{1,0:T(8,128)S(1)}, f32[168,128]{1,0:T(8,128)S(1)}, u32[]{:S(2)}, u32[]{:S(2)}) %collective-permute-start.2) | collective-permute-done | bytes 86048 | tf_op jit(solution)/shard_map/ppermute | solution.py:476
  28.4 0.0 collective-permute-done.3.y_high.yh
  28.4 0.2 shard_map.88
  28.6 3.9 %shard_map.89 = (f32[19,16,16,128]{3,2,1,0:T(8,128)S(1)}, f32[19,16,16,128]{3,2,1,0:T(8,128)S(1)}, f32[19,16,16,128]{3,2,1,0:T(8,128)S(1)}, f32[128,128]{1,0:T(8...) custom-call(f32[19,16,16,128]{3,2,1,0:T(8,128)S(1)} %get-tuple-eleme, ...), custom_call_target="tpu_custom_call", output_to_operand_aliasing={{0}: (0, {}), {1}: (1, {})} | custom-call | tf_op jit(solution)/shard_map/pallas_call | solution.py:455
  32.6 0.0 collective-permute-start.4
  32.6 0.7 %collective-permute-start.5 = (f32[80,128]{1,0:T(8,128)S(1)}, f32[80,128]{1,0:T(8,128)S(1)}, u32[]{:S(2)}, u32[]{:S(2)}) collective-permute-start(f32[80,128]{1,0:T(8,128)S(1)} %get-tuple-element.44), channel_id=1, source_target_pairs={{0,112},{16,0},{32,16},{48,32},{64,48},{80,64},{96,80},{112,96},{1... | collective-permute-start | bytes 122888 | tf_op jit(solution)/shard_map/ppermute | solution.py:476
  33.2 9.3 %all-to-all-start = ((f32[128,1,128]{2,1,0:T(1,128)}), f32[128,1,128]{2,1,0:T(1,128)S(1)}, u32[]{:S(2)}, u32[]{:S(2)}) async-start(f32[128,1,128]{2,1,0:T(1,128)} %bitcast.3), calls=%async_computation | async-start | bytes 131072 | tf_op jit(solution)/shard_map/all_to_all | solution.py:517
  42.6 0.0 collective-permute-done.4.x_low.xl
  42.6 0.0 collective-permute-done.5.x_high.xh
  42.6 1.5 %collective-permute-start.6 = (f32[80,128]{1,0:T(8,128)S(1)}, f32[80,128]{1,0:T(8,128)S(1)}, u32[]{:S(2)}, u32[]{:S(2)}) collective-permute-start(f32[80,128]{1,0:T(8,128)S(1)} %get-tuple-element.47), channel_id=1, source_target_pairs={{0,1},{1,2},{2,3},{3,4},{4,5},{5,6},{6,7},{7,8},{8,9},{9,10},{10,1... | collective-permute-start | bytes 122888 | tf_op jit(solution)/shard_map/ppermute | solution.py:476
  44.1 4.3 %collective-permute-start.7 = (f32[80,128]{1,0:T(8,128)S(1)}, f32[80,128]{1,0:T(8,128)S(1)}, u32[]{:S(2)}, u32[]{:S(2)}) collective-permute-start(f32[80,128]{1,0:T(8,128)S(1)} %get-tuple-element.48), channel_id=1, source_target_pairs={{0,15},{1,0},{2,1},{3,2},{4,3},{5,4},{6,5},{7,6},{8,7},{9,8},{10,9... | collective-permute-start | bytes 122888 | tf_op jit(solution)/shard_map/ppermute | solution.py:476
  48.4 4.0 %all-to-all-done = f32[128,1,128]{2,1,0:T(1,128)S(1)} async-done(((f32[128,1,128]{2,1,0:T(1,128)}), f32[128,1,128]{2,1,0:T(1,128)S(1)}, u32[]{:S(2)}, u32[]{:S(2)}) %all-to-all-start) | async-done | bytes 65568 | tf_op jit(solution)/shard_map/all_to_all | solution.py:517
  52.3 0.8 %shard_map.92 = f32[1,256]{1,0:T(1,128)S(1)} custom-call(f32[128,128]{1,0:T(8,128)S(1)} %bitcast.8), custom_call_target="tpu_custom_call" | custom-call | tf_op jit(solution)/shard_map/pallas_call | solution.py:455
  53.1 0.6 %copy.24 = f32[256]{0:T(256)} copy(f32[256]{0:T(256)S(1)} %bitcast.7) | data formatting | bytes 2048
  53.6 0.0 collective-permute-done.6.yl
  53.6 0.0 collective-permute-done.7.yh
  53.6 2.2 %shard_map.91 = (f32[19,16,16,128]{3,2,1,0:T(8,128)S(1)}, f32[19,16,16,128]{3,2,1,0:T(8,128)}) custom-call(f32[19,16,16,128]{3,2,1,0:T(8,128)S(1)} %get-tuple-element.42.late_in, f32[80,128]{1,0:T(8,128)S(1)} %collective-permute-done.4.x_low.xl, f32[80,128]{1,0:T(8,128)S(1)} %collective-permute-done.5.x_high.xh, ...), custom_call_target="tpu_custom_call", output_to_operand_aliasing={{0}: (0, {})} | custom-call | tf_op jit(solution)/shard_map/pallas_call | solution.py:455
  (1 shorter events, 0.0 us)
Async XLA Ops:
  0.6 1.7 %copy-start = (f32[19,16,16,128]{3,2,1,0:T(8,128)S(1)}, f32[19,16,16,128]{3,2,1,0:T(8,128)}, u32[]{:S(2)}) copy-start(f32[19,16,16,128]{3,2,1,0:T(8,128)} %f_hbm.1) | copy-start | bytes 7471108
  2.3 1.7 %copy-start.1 = (f32[19,16,16,128]{3,2,1,0:T(8,128)S(1)}, f32[19,16,16,128]{3,2,1,0:T(8,128)}, u32[]{:S(2)}) copy-start(f32[19,16,16,128]{3,2,1,0:T(8,128)} %adjoint_hbm.1) | copy-start | bytes 7471108
  4.0 0.9 %copy-start.2 = (f32[16,16,128]{2,1,0:T(8,128)S(1)}, f32[16,16,128]{2,1,0:T(8,128)}, u32[]{:S(2)}) copy-start(f32[16,16,128]{2,1,0:T(8,128)} %porosity_hbm.1) | copy-start | bytes 393220
  4.9 0.9 %copy-start.3 = (s32[16,16,128]{2,1,0:T(8,128)S(1)}, s32[16,16,128]{2,1,0:T(8,128)}, u32[]{:S(2)}) copy-start(s32[16,16,128]{2,1,0:T(8,128)} %porous_hbm.1) | copy-start | bytes 393220
  5.8 0.9 %copy-start.4 = (s32[16,16,128]{2,1,0:T(8,128)S(1)}, s32[16,16,128]{2,1,0:T(8,128)}, u32[]{:S(2)}) copy-start(s32[16,16,128]{2,1,0:T(8,128)} %walls_hbm.1) | copy-start | bytes 393220
  6.8 0.7 %copy-start.5 = (s32[1,1,64,1]{2,3,1,0:T(1,128)S(1)}, s32[1,1,64,1]{2,3,1,0:T(1,128)}, u32[]{:S(2)}) copy-start(s32[1,1,64,1]{2,3,1,0:T(1,128)} %param.12) | copy-start | bytes 772
  7.4 0.7 %copy-start.6 = (s32[1,1,64]{2,1,0:T(1,128)S(1)}, s32[1,1,64]{2,1,0:T(1,128)}, u32[]{:S(2)}) copy-start(s32[1,1,64]{2,1,0:T(1,128)} %param.13) | copy-start | bytes 772
  12.6 4.1 %collective-permute-start = (f32[168,128]{1,0:T(8,128)S(1)}, f32[168,128]{1,0:T(8,128)S(1)}, u32[]{:S(2)}, u32[]{:S(2)}) collective-permute-start(f32[168,128]{1,0:T(8,128)S(1)} %get-tuple-element.29), channel_id=1, source_target_pairs={{0,16},{16,32},{32,48},{48,64},{64,80},{80,96},{96,112},{112,0},{1... | collective-permute-start | bytes 258056 | tf_op jit(solution)/shard_map/ppermute | solution.py:476
  15.3 3.9 %collective-permute-start.1 = (f32[168,128]{1,0:T(8,128)S(1)}, f32[168,128]{1,0:T(8,128)S(1)}, u32[]{:S(2)}, u32[]{:S(2)}) collective-permute-start(f32[168,128]{1,0:T(8,128)S(1)} %get-tuple-element.30), channel_id=1, source_target_pairs={{0,112},{16,0},{32,16},{48,32},{64,48},{80,64},{96,80},{112,96},{1... | collective-permute-start | bytes 258056 | tf_op jit(solution)/shard_map/ppermute | solution.py:476
  19.3 9.1 %collective-permute-start.2 = (f32[168,128]{1,0:T(8,128)S(1)}, f32[168,128]{1,0:T(8,128)S(1)}, u32[]{:S(2)}, u32[]{:S(2)}) collective-permute-start(f32[168,128]{1,0:T(8,128)S(1)} %get-tuple-element.33), channel_id=1, source_target_pairs={{0,1},{1,2},{2,3},{3,4},{4,5},{5,6},{6,7},{7,8},{8,9},{9,10},{10,1... | collective-permute-start | bytes 258056 | tf_op jit(solution)/shard_map/ppermute | solution.py:476
  20.7 7.7 %collective-permute-start.3 = (f32[168,128]{1,0:T(8,128)S(1)}, f32[168,128]{1,0:T(8,128)S(1)}, u32[]{:S(2)}, u32[]{:S(2)}) collective-permute-start(f32[168,128]{1,0:T(8,128)S(1)} %get-tuple-element.34), channel_id=1, source_target_pairs={{0,15},{1,0},{2,1},{3,2},{4,3},{5,4},{6,5},{7,6},{8,7},{9,8},{10,9... | collective-permute-start | bytes 258056 | tf_op jit(solution)/shard_map/ppermute | solution.py:476
  32.6 10.1 %collective-permute-start.4 = (f32[80,128]{1,0:T(8,128)S(1)}, f32[80,128]{1,0:T(8,128)S(1)}, u32[]{:S(2)}, u32[]{:S(2)}) collective-permute-start(f32[80,128]{1,0:T(8,128)S(1)} %get-tuple-element.43), channel_id=1, source_target_pairs={{0,16},{16,32},{32,48},{48,64},{64,80},{80,96},{96,112},{112,0},{1... | collective-permute-start | bytes 122888 | tf_op jit(solution)/shard_map/ppermute | solution.py:476
  32.6 10.1 %collective-permute-start.5 = (f32[80,128]{1,0:T(8,128)S(1)}, f32[80,128]{1,0:T(8,128)S(1)}, u32[]{:S(2)}, u32[]{:S(2)}) collective-permute-start(f32[80,128]{1,0:T(8,128)S(1)} %get-tuple-element.44), channel_id=1, source_target_pairs={{0,112},{16,0},{32,16},{48,32},{64,48},{80,64},{96,80},{112,96},{1... | collective-permute-start | bytes 122888 | tf_op jit(solution)/shard_map/ppermute | solution.py:476
  33.2 19.1 %all-to-all-start = ((f32[128,1,128]{2,1,0:T(1,128)}), f32[128,1,128]{2,1,0:T(1,128)S(1)}, u32[]{:S(2)}, u32[]{:S(2)}) async-start(f32[128,1,128]{2,1,0:T(1,128)} %bitcast.3), calls=%async_computation | async-start | bytes 131072 | tf_op jit(solution)/shard_map/all_to_all | solution.py:517
  42.6 11.0 %collective-permute-start.6 = (f32[80,128]{1,0:T(8,128)S(1)}, f32[80,128]{1,0:T(8,128)S(1)}, u32[]{:S(2)}, u32[]{:S(2)}) collective-permute-start(f32[80,128]{1,0:T(8,128)S(1)} %get-tuple-element.47), channel_id=1, source_target_pairs={{0,1},{1,2},{2,3},{3,4},{4,5},{5,6},{6,7},{7,8},{8,9},{9,10},{10,1... | collective-permute-start | bytes 122888 | tf_op jit(solution)/shard_map/ppermute | solution.py:476
  44.1 9.6 %collective-permute-start.7 = (f32[80,128]{1,0:T(8,128)S(1)}, f32[80,128]{1,0:T(8,128)S(1)}, u32[]{:S(2)}, u32[]{:S(2)}) collective-permute-start(f32[80,128]{1,0:T(8,128)S(1)} %get-tuple-element.48), channel_id=1, source_target_pairs={{0,15},{1,0},{2,1},{3,2},{4,3},{5,4},{6,5},{7,6},{8,7},{9,8},{10,9... | collective-permute-start | bytes 122888 | tf_op jit(solution)/shard_map/ppermute | solution.py:476

commit v2 on v1

--- a/solution.py
+++ b/solution.py
@@ -430,7 +430,8 @@
         plane(x).wait()
 
 
-def owner_kernel(got, out):
+def owner_kernel(late, got, out):
+    del late
     patch = iota((DEVICES, PATCH_DEV), 1).astype(jnp.float32)
     data = got[...]
     total = jnp.zeros((DEVICES, PATCH_DEV), jnp.float32)
@@ -450,7 +451,7 @@
 
 
 def call(kernel, ins, outs, scratch=(), aliases=None, flops=0, hbm_ins=0, hbm_outs=()):
-    held = list(ins[:hbm_ins])
+    held = [pltpu.with_memory_space_constraint(x, pltpu.HBM) for x in ins[:hbm_ins]]
     held += [pltpu.with_memory_space_constraint(x, pltpu.VMEM) for x in ins[hbm_ins:]]
     return pl.pallas_call(
         kernel,
@@ -516,7 +517,7 @@
     )
     got = lax.all_to_all(send, ("gx", "gy"), split_axis=0, concat_axis=0, tiled=True)
     halos = exchange(messages, -1, 1)
-    _, adjoint_out = call(
+    late, adjoint_out = call(
         early_kernel,
         [late, *halos, frac, vel],
         [FIELD],
@@ -524,7 +525,7 @@
         scratch=[vmem(CX, Q, CY, NZ), pltpu.SemaphoreType.DMA((CX,))],
         aliases={0: 0},
     )
-    (patch,) = call(owner_kernel, [got], [vmem(1, PATCH_DEV)])
+    (patch,) = call(owner_kernel, [late, got], [vmem(1, PATCH_DEV)])
     return adjoint_out, patch.reshape(PATCH_DEV)
 
 

time: 56.2 us -> 46.7 us (0.83)
  local copies, waits for them, and re-layouts: 7.99 us -> 0.57 us
  waiting for transfers between devices: 10.6 us -> 8.41 us
    unnamed x15 -> x1, local copies, waits for them, and re-layouts: 7.99 us -> 0.57 us
    all_to_all x1, waiting for transfers between devices: 3.95 us -> 0.07 us  [body(): lax.all_to_all(send, ('gx', 'gy'), split_axis=0, concat_axis=0, tiled=True)]
    ppermute x8, waiting for transfers between devices: 6.63 us -> 8.34 us  [shift(): lax.ppermute(block, axis, [(i, (i + step) % count) for i in range(count)])]
  transfers between devices with their start and end apart: 9 -> 9, of which waited for: 4 -> 5; matrix products, arithmetic and copies ran while one was open for 1% -> 0% of each run, Pallas kernels for 1% -> 5%
where the time goes in v2:
time: 46.7 us; the launch traced here: 46.5 us
  starting transfers between devices  24.7 us (53%)
  Pallas kernels  12.1 us (26%)
  waiting for transfers between devices  8.41 us (18%)
  between operations  0.71 us (2%)
  local copies, waits for them, and re-layouts  0.57 us (1%)
    ppermute x8, starting transfers between devices, shift(): lax.ppermute(block, axis, [(i, (i + step) % count) for i in range(count)])  15.4 us
    pallas_call x7, Pallas kernels, call(): pl.pallas_call(kernel, out_shape=[*outs, *hbm_outs], in_specs=[ANY] * hbm...  12.1 us
    all_to_all x1, starting transfers between devices, body(): lax.all_to_all(send, ('gx', 'gy'), split_axis=0, concat_axis=0, tiled=True)  9.34 us
    ppermute x8, waiting for transfers between devices, shift(): lax.ppermute(block, axis, [(i, (i + step) % count) for i in range(count)])  8.34 us
  transfers between devices with their start and end apart: 9, of which 5 were waited for; matrix products, arithmetic and copies ran while one was open for 0% of the time, Pallas kernels for 5%

profile of v2, /device:TPU:1, one launch (start us, length us, event | category | flops | bytes accessed | tf_op | source)
XLA Modules:
  0.0 46.5 jit_solution(9305115084295081524)
XLA Ops:
  0.6 4.8 %shard_map.86 = (f32[19,16,16,128]{3,2,1,0:T(8,128)S(1)}, f32[19,16,16,128]{3,2,1,0:T(8,128)S(1)}, f32[19,16,16,128]{3,2,1,0:T(8,128)S(1)}, f32[16,16,128]{2,1,0...) custom-call(f32[19,16,16,128]{3,2,1,0:T(8,128)} %f_hbm.1, ...), custom_call_target="tpu_custom_call" | custom-call | tf_op jit(solution)/shard_map/pallas_call | solution.py:456
  5.4 2.6 %collective-permute-start = (f32[168,128]{1,0:T(8,128)S(1)}, f32[168,128]{1,0:T(8,128)S(1)}, u32[]{:S(2)}, u32[]{:S(2)}) collective-permute-start(f32[168,128]{1,0:T(8,128)S(1)} %get-tuple-element.30), channel_id=1, source_target_pairs={{0,16},{16,32},{32,48},{48,64},{64,80},{80,96},{96,112},{112,0},{1... | collective-permute-start | bytes 258056 | tf_op jit(solution)/shard_map/ppermute | solution.py:477
  8.0 0.0 collective-permute-start.1
  8.0 1.5 %collective-permute-done.x_low.xl = f32[168,128]{1,0:T(8,128)S(1)} collective-permute-done((f32[168,128]{1,0:T(8,128)S(1)}, f32[168,128]{1,0:T(8,128)S(1)}, u32[]{:S(2)}, u32[]{:S(2)}) %collective-permute-start) | collective-permute-done | bytes 86048 | tf_op jit(solution)/shard_map/ppermute | solution.py:477
  9.6 2.4 %collective-permute-done.1.x_high.xh = f32[168,128]{1,0:T(8,128)S(1)} collective-permute-done((f32[168,128]{1,0:T(8,128)S(1)}, f32[168,128]{1,0:T(8,128)S(1)}, u32[]{:S(2)}, u32[]{:S(2)}) %collective-permute-start.1) | collective-permute-done | bytes 86048 | tf_op jit(solution)/shard_map/ppermute | solution.py:477
  11.9 0.1 shard_map.87
  12.1 1.4 %collective-permute-start.2 = (f32[168,128]{1,0:T(8,128)S(1)}, f32[168,128]{1,0:T(8,128)S(1)}, u32[]{:S(2)}, u32[]{:S(2)}) collective-permute-start(f32[168,128]{1,0:T(8,128)S(1)} %get-tuple-element.34), channel_id=1, source_target_pairs={{0,1},{1,2},{2,3},{3,4},{4,5},{5,6},{6,7},{7,8},{8,9},{9,10},{10,1... | collective-permute-start | bytes 258056 | tf_op jit(solution)/shard_map/ppermute | solution.py:477
  13.4 5.0 %collective-permute-start.3 = (f32[168,128]{1,0:T(8,128)S(1)}, f32[168,128]{1,0:T(8,128)S(1)}, u32[]{:S(2)}, u32[]{:S(2)}) collective-permute-start(f32[168,128]{1,0:T(8,128)S(1)} %get-tuple-element.35), channel_id=1, source_target_pairs={{0,15},{1,0},{2,1},{3,2},{4,3},{5,4},{6,5},{7,6},{8,7},{9,8},{10,9... | collective-permute-start | bytes 258056 | tf_op jit(solution)/shard_map/ppermute | solution.py:477
  18.4 2.7 %collective-permute-done.2.y_low.yl = f32[168,128]{1,0:T(8,128)S(1)} collective-permute-done((f32[168,128]{1,0:T(8,128)S(1)}, f32[168,128]{1,0:T(8,128)S(1)}, u32[]{:S(2)}, u32[]{:S(2)}) %collective-permute-start.2) | collective-permute-done | bytes 86048 | tf_op jit(solution)/shard_map/ppermute | solution.py:477
  21.1 0.0 collective-permute-done.3.y_high.yh
  21.1 0.2 shard_map.88
  21.4 4.0 %shard_map.89 = (f32[19,16,16,128]{3,2,1,0:T(8,128)S(1)}, f32[19,16,16,128]{3,2,1,0:T(8,128)S(1)}, f32[19,16,16,128]{3,2,1,0:T(8,128)S(1)}, f32[128,128]{1,0:T(8...) custom-call(f32[19,16,16,128]{3,2,1,0:T(8,128)S(1)} %get-tuple-eleme, ...), custom_call_target="tpu_custom_call", output_to_operand_aliasing={{0}: (0, {}), {1}: (1, {})} | custom-call | tf_op jit(solution)/shard_map/pallas_call | solution.py:456
  25.4 0.0 collective-permute-start.4
  25.4 0.7 %collective-permute-start.5 = (f32[80,128]{1,0:T(8,128)S(1)}, f32[80,128]{1,0:T(8,128)S(1)}, u32[]{:S(2)}, u32[]{:S(2)}) collective-permute-start(f32[80,128]{1,0:T(8,128)S(1)} %get-tuple-element.45), channel_id=1, source_target_pairs={{0,112},{16,0},{32,16},{48,32},{64,48},{80,64},{96,80},{112,96},{1... | collective-permute-start | bytes 122888 | tf_op jit(solution)/shard_map/ppermute | solution.py:477
  26.1 9.3 %all-to-all-start = ((f32[128,1,128]{2,1,0:T(1,128)}), f32[128,1,128]{2,1,0:T(1,128)S(1)}, u32[]{:S(2)}, u32[]{:S(2)}) async-start(f32[128,1,128]{2,1,0:T(1,128)} %bitcast.3), calls=%async_computation | async-start | bytes 131072 | tf_op jit(solution)/shard_map/all_to_all | solution.py:518
  35.4 0.0 collective-permute-done.4.x_low.xl
  35.4 0.0 collective-permute-done.5.x_high.xh
  35.5 1.5 %collective-permute-start.6 = (f32[80,128]{1,0:T(8,128)S(1)}, f32[80,128]{1,0:T(8,128)S(1)}, u32[]{:S(2)}, u32[]{:S(2)}) collective-permute-start(f32[80,128]{1,0:T(8,128)S(1)} %get-tuple-element.48), channel_id=1, source_target_pairs={{0,1},{1,2},{2,3},{3,4},{4,5},{5,6},{6,7},{7,8},{8,9},{9,10},{10,1... | collective-permute-start | bytes 122888 | tf_op jit(solution)/shard_map/ppermute | solution.py:477
  36.9 4.3 %collective-permute-start.7 = (f32[80,128]{1,0:T(8,128)S(1)}, f32[80,128]{1,0:T(8,128)S(1)}, u32[]{:S(2)}, u32[]{:S(2)}) collective-permute-start(f32[80,128]{1,0:T(8,128)S(1)} %get-tuple-element.49), channel_id=1, source_target_pairs={{0,15},{1,0},{2,1},{3,2},{4,3},{5,4},{6,5},{7,6},{8,7},{9,8},{10,9... | collective-permute-start | bytes 122888 | tf_op jit(solution)/shard_map/ppermute | solution.py:477
  41.2 1.7 %collective-permute-done.6.yl = f32[80,128]{1,0:T(8,128)S(1)} collective-permute-done((f32[80,128]{1,0:T(8,128)S(1)}, f32[80,128]{1,0:T(8,128)S(1)}, u32[]{:S(2)}, u32[]{:S(2)}) %collective-permute-start.6) | collective-permute-done | bytes 40992 | tf_op jit(solution)/shard_map/ppermute | solution.py:477
  42.9 0.0 collective-permute-done.7.yh
  42.9 2.2 %shard_map.91 = (f32[19,16,16,128]{3,2,1,0:T(8,128)S(1)}, f32[19,16,16,128]{3,2,1,0:T(8,128)}) custom-call(f32[19,16,16,128]{3,2,1,0:T(8,128)S(1)} %get-tuple-element.43.late_in, f32[80,128]{1,0:T(8,128)S(1)} %collective-permute-done.4.x_low.xl, f32[80,128]{1,0:T(8,128)S(1)} %collective-permute-done.5.x_high.xh, ...), custom_call_target="tpu_custom_call", output_to_operand_aliasing={{0}: (0, {})} | custom-call | tf_op jit(solution)/shard_map/pallas_call | solution.py:456
  45.1 0.1 all-to-all-done
  45.2 0.8 %shard_map.92 = f32[1,256]{1,0:T(1,128)S(1)} custom-call(f32[19,16,16,128]{3,2,1,0:T(8,128)S(1)} %get-tuple-element.52.late, f32[128,128]{1,0:T(8,128)S(1)} %bitcast.8), custom_call_target="tpu_custom_call" | custom-call | tf_op jit(solution)/shard_map/pallas_call | solution.py:456
  46.0 0.6 %copy.24 = f32[256]{0:T(256)} copy(f32[256]{0:T(256)S(1)} %bitcast.7) | data formatting | bytes 2048
  (1 shorter events, 0.0 us)
Async XLA Ops:
  5.4 4.1 %collective-permute-start = (f32[168,128]{1,0:T(8,128)S(1)}, f32[168,128]{1,0:T(8,128)S(1)}, u32[]{:S(2)}, u32[]{:S(2)}) collective-permute-start(f32[168,128]{1,0:T(8,128)S(1)} %get-tuple-element.30), channel_id=1, source_target_pairs={{0,16},{16,32},{32,48},{48,64},{64,80},{80,96},{96,112},{112,0},{1... | collective-permute-start | bytes 258056 | tf_op jit(solution)/shard_map/ppermute | solution.py:477
  8.0 3.9 %collective-permute-start.1 = (f32[168,128]{1,0:T(8,128)S(1)}, f32[168,128]{1,0:T(8,128)S(1)}, u32[]{:S(2)}, u32[]{:S(2)}) collective-permute-start(f32[168,128]{1,0:T(8,128)S(1)} %get-tuple-element.31), channel_id=1, source_target_pairs={{0,112},{16,0},{32,16},{48,32},{64,48},{80,64},{96,80},{112,96},{1... | collective-permute-start | bytes 258056 | tf_op jit(solution)/shard_map/ppermute | solution.py:477
  12.1 9.1 %collective-permute-start.2 = (f32[168,128]{1,0:T(8,128)S(1)}, f32[168,128]{1,0:T(8,128)S(1)}, u32[]{:S(2)}, u32[]{:S(2)}) collective-permute-start(f32[168,128]{1,0:T(8,128)S(1)} %get-tuple-element.34), channel_id=1, source_target_pairs={{0,1},{1,2},{2,3},{3,4},{4,5},{5,6},{6,7},{7,8},{8,9},{9,10},{10,1... | collective-permute-start | bytes 258056 | tf_op jit(solution)/shard_map/ppermute | solution.py:477
  13.4 7.7 %collective-permute-start.3 = (f32[168,128]{1,0:T(8,128)S(1)}, f32[168,128]{1,0:T(8,128)S(1)}, u32[]{:S(2)}, u32[]{:S(2)}) collective-permute-start(f32[168,128]{1,0:T(8,128)S(1)} %get-tuple-element.35), channel_id=1, source_target_pairs={{0,15},{1,0},{2,1},{3,2},{4,3},{5,4},{6,5},{7,6},{8,7},{9,8},{10,9... | collective-permute-start | bytes 258056 | tf_op jit(solution)/shard_map/ppermute | solution.py:477
  25.4 10.1 %collective-permute-start.4 = (f32[80,128]{1,0:T(8,128)S(1)}, f32[80,128]{1,0:T(8,128)S(1)}, u32[]{:S(2)}, u32[]{:S(2)}) collective-permute-start(f32[80,128]{1,0:T(8,128)S(1)} %get-tuple-element.44), channel_id=1, source_target_pairs={{0,16},{16,32},{32,48},{48,64},{64,80},{80,96},{96,112},{112,0},{1... | collective-permute-start | bytes 122888 | tf_op jit(solution)/shard_map/ppermute | solution.py:477
  25.4 10.1 %collective-permute-start.5 = (f32[80,128]{1,0:T(8,128)S(1)}, f32[80,128]{1,0:T(8,128)S(1)}, u32[]{:S(2)}, u32[]{:S(2)}) collective-permute-start(f32[80,128]{1,0:T(8,128)S(1)} %get-tuple-element.45), channel_id=1, source_target_pairs={{0,112},{16,0},{32,16},{48,32},{64,48},{80,64},{96,80},{112,96},{1... | collective-permute-start | bytes 122888 | tf_op jit(solution)/shard_map/ppermute | solution.py:477
  26.1 19.1 %all-to-all-start = ((f32[128,1,128]{2,1,0:T(1,128)}), f32[128,1,128]{2,1,0:T(1,128)S(1)}, u32[]{:S(2)}, u32[]{:S(2)}) async-start(f32[128,1,128]{2,1,0:T(1,128)} %bitcast.3), calls=%async_computation | async-start | bytes 131072 | tf_op jit(solution)/shard_map/all_to_all | solution.py:518
  35.5 7.4 %collective-permute-start.6 = (f32[80,128]{1,0:T(8,128)S(1)}, f32[80,128]{1,0:T(8,128)S(1)}, u32[]{:S(2)}, u32[]{:S(2)}) collective-permute-start(f32[80,128]{1,0:T(8,128)S(1)} %get-tuple-element.48), channel_id=1, source_target_pairs={{0,1},{1,2},{2,3},{3,4},{4,5},{5,6},{6,7},{7,8},{8,9},{9,10},{10,1... | collective-permute-start | bytes 122888 | tf_op jit(solution)/shard_map/ppermute | solution.py:477
  36.9 6.0 %collective-permute-start.7 = (f32[80,128]{1,0:T(8,128)S(1)}, f32[80,128]{1,0:T(8,128)S(1)}, u32[]{:S(2)}, u32[]{:S(2)}) collective-permute-start(f32[80,128]{1,0:T(8,128)S(1)} %get-tuple-element.49), channel_id=1, source_target_pairs={{0,15},{1,0},{2,1},{3,2},{4,3},{5,4},{6,5},{7,6},{8,7},{9,8},{10,9... | collective-permute-start | bytes 122888 | tf_op jit(solution)/shard_map/ppermute | solution.py:477

commit v3 on v2

--- a/solution.py
+++ b/solution.py
@@ -1,5 +1,3 @@
-import functools
-
 import jax
 import jax.numpy as jnp
 from jax import lax
@@ -22,6 +20,7 @@
 FACE = 80
 META = 160
 MESSAGE_ROWS = 168
+PLANES = 4
 
 velocities = [
     (0, 0, 0),
@@ -176,38 +175,54 @@
     return [open_part * (b[i] + h[i]) + fraction * b[opposite[i]] for i in range(Q)]
 
 
+def store_wrapped(put, first, step, value):
+    row = first + step
+    if row < 0:
+        put(0, value[1:])
+        put(CY - 1, value[:1])
+    elif row + TILE > CY:
+        put(row, value[:-1])
+        put(0, value[-1:])
+    else:
+        put(row, value)
+
+
 def put_moved(field, i, x, yt, value, direction):
     cx, cy, cz = (direction * c for c in velocities[i])
     if cz:
         value = pltpu.roll(value, cz % NZ, axis=1)
     x = (x + cx) & (CX - 1) if cx else x
-    row = yt * TILE + cy
-    if row < 0:
-        field[i, x, pl.ds(0, TILE - 1), :] = value[1:]
-        field[i, x, pl.ds(CY - 1, 1), :] = value[:1]
-    elif row + TILE > CY:
-        field[i, x, pl.ds(row, TILE - 1), :] = value[:-1]
-        field[i, x, pl.ds(0, 1), :] = value[-1:]
-    else:
-        field[i, x, pl.ds(row, TILE), :] = value
-
-
-def fill_messages(fields, direction, x_up, x_down, y_up, y_down):
+
+    def put(row, part):
+        field[i, x, pl.ds(row, part.shape[0]), :] = part
+
+    store_wrapped(put, yt * TILE, cy, value)
+
+
+def x_faces(fields, direction, x_up, x_down):
     for n, field in enumerate(fields):
         for sign, x, message in ((1, 0, x_up), (-1, CX - 1, x_down)):
             for k, i in enumerate(moving(0, sign, direction)):
                 message[pl.ds(n * FACE + k * CY, CY), :] = field[i, x]
+
+
+def y_faces(fields, direction, y_up, y_down):
+    for n, field in enumerate(fields):
         for sign, row, message in ((1, 0, y_up), (-1, CY - 1, y_down)):
             for k, i in enumerate(moving(1, sign, direction)):
                 for x in range(CX):
                     message[pl.ds(n * FACE + k * CX + x, 1), :] = field[i, x, pl.ds(row, 1), :]
 
 
-def fill_ring(fields, direction, x_low, x_high, y_low, y_high):
+def fill_x(fields, direction, x_low, x_high):
     for n, field in enumerate(fields):
         for sign, x, message in ((1, 0, x_low), (-1, CX - 1, x_high)):
             for k, i in enumerate(moving(0, sign, direction)):
                 field[i, x] = message[pl.ds(n * FACE + k * CY, CY), :]
+
+
+def fill_y(fields, direction, y_low, y_high):
+    for n, field in enumerate(fields):
         for sign, row, message in ((1, 0, y_low), (-1, CY - 1, y_high)):
             for k, i in enumerate(moving(1, sign, direction)):
                 for x in range(CX):
@@ -218,6 +233,13 @@
     return pl.ds(yt * TILE, TILE)
 
 
+def unrolled(start, stop, count, step):
+    @pl.loop(0, (stop - start) // count)
+    def _(n):
+        for k in range(count):
+            step(start + n * count + k)
+
+
 def iota(shape, dim):
     return lax.broadcasted_iota(jnp.int32, shape, dim)
 
@@ -226,7 +248,7 @@
     return jnp.sum(jnp.where(pick, row, 0.0), axis=1, keepdims=True)
 
 
-def block_numbers(owners, slots, table, x_up, x_down, y_up, y_down):
+def block_numbers(owners, slots, table, y_up, y_down):
     shape = (64, 64)
     row, lane = iota(shape, 0), iota(shape, 1)
     same = row == lane
@@ -243,56 +265,90 @@
         line = jnp.sum(spread_out[xb * 8 : xb * 8 + 8], axis=0, keepdims=True)
         table[pl.ds(xb + 1, 1), :] = line
     held = table[...]
-    x_up[pl.ds(META, 1), :] = held[8:9]
-    x_down[pl.ds(META, 1), :] = held[1:2]
     eye = iota((16, NZ), 0) == iota((16, NZ), 1)
     for yb, message in ((8, y_up), (1, y_down)):
         part = jnp.where(eye, held[:, yb : yb + 1], 0.0)
         message[pl.ds(META, 1), :] = jnp.sum(part, axis=0, keepdims=True)
 
 
+def solidity(porosity, porous, walls):
+    wall = walls == 1
+    panel = porous.astype(jnp.float32)
+    return jnp.where(wall, 1.0, panel * porosity), jnp.where(wall, 0.0, panel)
+
+
+def edge_kernel(
+    f_hbm, porosity_hbm, porous_hbm, walls_hbm, owners_hbm, slots_hbm,
+    table, yu, yd, f, porosity, porous, walls, owners, slots, sems,
+):
+    numbers = [
+        pltpu.make_async_copy(owners_hbm, owners, sems.at[0]),
+        pltpu.make_async_copy(slots_hbm, slots, sems.at[1]),
+    ]
+    lines = []
+    for n, y in enumerate((CY - 1, 0)):
+        lines += [
+            pltpu.make_async_copy(f_hbm.at[:, :, y, :], f.at[n], sems.at[4 * n + 2]),
+            pltpu.make_async_copy(porosity_hbm.at[:, y, :], porosity.at[n], sems.at[4 * n + 3]),
+            pltpu.make_async_copy(porous_hbm.at[:, y, :], porous.at[n], sems.at[4 * n + 4]),
+            pltpu.make_async_copy(walls_hbm.at[:, y, :], walls.at[n], sems.at[4 * n + 5]),
+        ]
+    for copy in numbers + lines:
+        copy.start()
+    for copy in numbers:
+        copy.wait()
+    block_numbers(owners, slots, table, yu, yd)
+    for copy in lines:
+        copy.wait()
+    for n, (sign, message) in enumerate(((1, yu), (-1, yd))):
+        for xt in range(CX // TILE):
+            at = (n, rows(xt))
+            pops = [f[n, i, rows(xt), :] for i in range(Q)]
+            fraction, open_panel = solidity(porosity[at], porous[at], walls[at])
+            c = correction(off_equilibrium(pops)[1])
+            for k, i in enumerate(moving(1, sign, 1)):
+                relaxed = pops[i] - c[i]
+                change = pops[opposite[i]] - relaxed
+                pair = (relaxed + fraction * change, open_panel * change)
+                for field, value in enumerate(pair):
+                    cx, _, cz = velocities[i]
+                    if cz:
+                        value = pltpu.roll(value, cz % NZ, axis=1)
+
+                    def put(row, part, base=field * FACE + k * CX, message=message):
+                        message[pl.ds(base + row, part.shape[0]), :] = part
+
+                    store_wrapped(put, xt * TILE, cx, value)
+
+
 def forward_kernel(
-    f_hbm, porosity_hbm, adjoint_hbm, porous_hbm, walls_hbm, owners_hbm, slots_hbm,
-    moved, gap, adjoint, frac, mask, vel, table, xu, xd, yu, yd,
-    f, porosity, porous, walls, owners, slots, f_sems, sems,
+    f_hbm, porosity_hbm, porous_hbm, walls_hbm, adjoint_hbm,
+    moved, gap, adjoint, frac, mask, vel,
+    f, porosity, porous, walls, f_sems, sems,
 ):
-    def plane(x):
-        return pltpu.make_async_copy(f_hbm.at[:, x], f.at[:, x], f_sems.at[x])
+    def planes(n):
+        part = pl.ds(n * PLANES, PLANES)
+        return pltpu.make_async_copy(f_hbm.at[:, part], f.at[:, part], f_sems.at[n])
 
     small = [
-        pltpu.make_async_copy(source, target, sems.at[k])
-        for k, (source, target) in enumerate(
-            (
-                (owners_hbm, owners),
-                (slots_hbm, slots),
-                (porosity_hbm, porosity),
-                (porous_hbm, porous),
-                (walls_hbm, walls),
-            )
-        )
+        pltpu.make_async_copy(porosity_hbm, porosity, sems.at[0]),
+        pltpu.make_async_copy(porous_hbm, porous, sems.at[1]),
+        pltpu.make_async_copy(walls_hbm, walls, sems.at[2]),
     ]
-    later = pltpu.make_async_copy(adjoint_hbm, adjoint, sems.at[5])
+    later = pltpu.make_async_copy(adjoint_hbm, adjoint, sems.at[3])
     for copy in small:
         copy.start()
-    for x in range(CX):
-        plane(x).start()
+    for n in range(CX // PLANES):
+        planes(n).start()
     later.start()
-    small[0].wait()
-    small[1].wait()
-    block_numbers(owners, slots, table, xu, xd, yu, yd)
-    for copy in small[2:]:
+    for copy in small:
         copy.wait()
 
-    @pl.loop(0, CX)
-    def _(x):
-        plane(x).wait()
+    def plane(x):
         for yt in range(CY // TILE):
             at = (x, rows(yt))
             pops = [f[i, x, rows(yt), :] for i in range(Q)]
-            wall = walls[at] == 1
-            panel = porous[at].astype(jnp.float32)
-            fraction = jnp.where(wall, 1.0, panel * porosity[at])
-            open_panel = jnp.where(wall, 0.0, panel)
+            fraction, open_panel = solidity(porosity[at], porous[at], walls[at])
             frac[at] = fraction
             mask[at] = open_panel
             u, e, _ = off_equilibrium(pops)
@@ -305,42 +361,102 @@
                 put_moved(gap, i, x, yt, open_panel * change, 1)
                 put_moved(moved, i, x, yt, relaxed + fraction * change, 1)
 
-    fill_messages((moved, gap), 1, xu, xd, yu, yd)
+    @pl.loop(0, CX // PLANES)
+    def _(n):
+        planes(n).wait()
+        for k in range(PLANES):
+            plane(n * PLANES + k)
+
     later.wait()
 
 
-def corner_kernel(x_low, x_high, up_in, down_in, up, down, *, direction, fields):
+def turn_kernel(moved_in, gap_in, table, y_low, y_high, moved, gap, ext, x_up, x_down):
+    del moved_in, gap_in
+    fill_y((moved, gap), 1, y_low, y_high)
+    x_faces((moved, gap), 1, x_up, x_down)
+    shape = (16, NZ)
+    row, lane = iota(shape, 0), iota(shape, 1)
+    low = column(y_low[pl.ds(META, 1), :], row == lane)
+    high = column(y_high[pl.ds(META, 1), :], row == lane)
+    held = jnp.where(lane == 0, low, jnp.where(lane == 9, high, table[...]))
+    ext[...] = held
+    x_up[pl.ds(META, 1), :] = held[8:9]
+    x_down[pl.ds(META, 1), :] = held[1:2]
+
+
+def corner_kernel(x_low, x_high, up_in, down_in, up, down):
     del up_in, down_in
     for sign, row, message in ((1, 0, up), (-1, CY - 1, down)):
-        for k, i in enumerate(moving(1, sign, direction)):
-            cx = direction * velocities[i][0]
-            if not cx:
-                continue
-            source, x = (x_low, 0) if cx == 1 else (x_high, CX - 1)
-            k_x = moving(0, cx, direction).index(i)
-            for n in range(fields):
-                message[pl.ds(n * FACE + k * CX + x, 1), :] = source[
-                    pl.ds(n * FACE + k_x * CY + row, 1), :
-                ]
-    if fields == 2:
-        lane = iota((1, NZ), 1)
-        for yb, message in ((8, up), (1, down)):
-            low = jnp.sum(jnp.where(lane == yb, x_low[pl.ds(META, 1), :], 0.0))
-            high = jnp.sum(jnp.where(lane == yb, x_high[pl.ds(META, 1), :], 0.0))
-            line = message[pl.ds(META, 1), :]
-            line = jnp.where(lane == 0, low, jnp.where(lane == 9, high, line))
-            message[pl.ds(META, 1), :] = line
-
-
-def routing_kernel(table, x_low, x_high, y_low, y_high, owner_of, place, slot, ext):
-    shape = (16, NZ)
-    row, lane = iota(shape, 0), iota(shape, 1)
-    eye = row == lane
-    low = column(y_low[pl.ds(META, 1), :], eye)
-    high = column(y_high[pl.ds(META, 1), :], eye)
-    held = jnp.where(row == 0, x_low[pl.ds(META, 1), :], table[...])
-    held = jnp.where(row == 9, x_high[pl.ds(META, 1), :], held)
-    ext[...] = jnp.where(lane == 0, low, jnp.where(lane == 9, high, held))
+        for k, i in enumerate(moving(1, sign, -1)):
+            cx = -velocities[i][0]
+            if cx:
+                source, x = (x_low, 0) if cx == 1 else (x_high, CX - 1)
+                corner = moving(0, cx, -1).index(i) * CY + row
+                message[pl.ds(k * CX + x, 1), :] = source[pl.ds(corner, 1), :]
+
+
+def late_blocks(xb, take, adjoint, frac, mask, late, sums):
+    for yt in range(CY // TILE):
+        parts = {}
+        for half in range(2):
+            x = xb * 2 + half
+            at = (x, rows(yt))
+            read = [take(0, i, x, yt) for i in range(Q)]
+            u, e, df = off_equilibrium(read)
+            b = [adjoint[i, x, rows(yt), :] for i in range(Q)]
+            t, db = covector(b)
+            total = sum(t[k] * e[k] for k in t) - sum(p * q for p, q in zip(db, df))
+            total = mask[at] * total
+            out = pull_back(b, t, u, frac[at])
+            key = (0, 0)
+            parts[key] = parts[key] + total if key in parts else total
+            for i in range(Q):
+                cx, cy, _ = velocities[i]
+                key = ((half - cx) // 2, cy)
+                early = out[i] * take(1, i, x, yt)
+                parts[key] = parts[key] + early if key in parts else early
+                put_moved(late, i, x, yt, out[i], -1)
+        for (step, cy), part in parts.items():
+            at = (xb + 1 + step, pl.ds(PAD_Y + yt * TILE - cy, TILE))
+            sums[at] = sums[at] + part
+
+
+def late_kernel(moved, gap, adjoint, frac, mask, late, sums):
+    fields = (moved, gap)
+    sums[...] = jnp.zeros((EXT_XB, EXT_Y, NZ), jnp.float32)
+
+    def take(n, i, x, yt):
+        return fields[n][i, x, rows(yt), :]
+
+    def step(xb):
+        late_blocks(xb, take, adjoint, frac, mask, late, sums)
+
+    unrolled(1, CX // 2 - 1, 2, step)
+
+
+def late_rest_kernel(
+    late_in, sums_in, moved, gap, ext_in, x_low, x_high, adjoint, frac, mask,
+    late, sums, send, xu, xd, yu, yd, ext, owner_of, scaled,
+):
+    del late_in, sums_in
+    fields = (moved, gap)
+
+    def take(n, i, x, yt):
+        cx = velocities[i][0]
+        for sign, place, message in ((1, 0, x_low), (-1, CX - 1, x_high)):
+            if cx == sign and x == place:
+                first = n * FACE + moving(0, sign, 1).index(i) * CY + yt * TILE
+                return message[pl.ds(first, TILE), :]
+        return fields[n][i, x, rows(yt), :]
+
+    for xb in (0, CX // 2 - 1):
+        late_blocks(xb, take, adjoint, frac, mask, late, sums)
+    x_faces((late,), -1, xu, xd)
+    y_faces((late,), -1, yu, yd)
+
+    row = iota((16, NZ), 0)
+    held = jnp.where(row == 0, x_low[pl.ds(META, 1), :], ext_in[...])
+    ext[...] = jnp.where(row == 9, x_high[pl.ds(META, 1), :], held)
     shape = (EXT_Y, NZ)
     row, lane = iota(shape, 0), iota(shape, 1)
     yb = jnp.right_shift(row - 6, 1)
@@ -354,50 +470,9 @@
         spot = side + (number & 3)
         line = pl.ds(xb * EXT_Y, EXT_Y)
         owner_of[line, :] = jnp.where(used & (lane == jnp.right_shift(number, 10)), 1.0, 0.0)
-        place[line, :] = jnp.where(lane == spot, 1.0, 0.0)
         patch = (jnp.right_shift(number, 2) & 255).astype(jnp.float32)
-        slot[line, :] = jnp.where(first & (lane == spot + SLOT_LANE), patch, 0.0)
-
-
-def late_kernel(
-    moved_in, gap_in, xl, xh, yl, yh, adjoint, frac, mask, owner_of, place, slot,
-    moved, gap, late, send, xu, xd, yu, yd, sums, scaled,
-):
-    del moved_in, gap_in
-    fill_ring((moved, gap), 1, xl, xh, yl, yh)
-    sums[...] = jnp.zeros((EXT_XB, EXT_Y, NZ), jnp.float32)
-
-    @pl.loop(0, CX // 2)
-    def _(xb):
-        for yt in range(CY // TILE):
-            parts = {}
-            for half in range(2):
-                x = xb * 2 + half
-                at = (x, rows(yt))
-                read = [moved[i, x, rows(yt), :] for i in range(Q)]
-                u, e, df = off_equilibrium(read)
-                b = [adjoint[i, x, rows(yt), :] for i in range(Q)]
-                t, db = covector(b)
-                total = sum(t[k] * e[k] for k in t) - sum(p * q for p, q in zip(db, df))
-                total = mask[at] * total
-                out = pull_back(b, t, u, frac[at])
-                key = (0, 0)
-                parts[key] = parts[key] + total if key in parts else total
-                for i in range(Q):
-                    cx, cy, _ = velocities[i]
-                    key = ((half - cx) // 2, cy)
-                    early = out[i] * gap[i, x, rows(yt), :]
-                    parts[key] = parts[key] + early if key in parts else early
-                    put_moved(late, i, x, yt, out[i], -1)
-            for (step, cy), part in parts.items():
-                at = (xb + 1 + step, pl.ds(PAD_Y + yt * TILE - cy, TILE))
-                sums[at] = sums[at] + part
-
-    for xb in range(EXT_XB):
-        line = pl.ds(xb * EXT_Y, EXT_Y)
-        scaled[line, :] = (
-            jnp.sum(sums[xb], axis=1, keepdims=True) * place[line, :] + slot[line, :]
-        )
+        value = jnp.where(lane == spot, jnp.sum(sums[xb], axis=1, keepdims=True), 0.0)
+        scaled[line, :] = jnp.where(first & (lane == spot + SLOT_LANE), patch, value)
     send[...] = lax.dot_general(
         owner_of[...],
         scaled[...],
@@ -405,29 +480,32 @@
         precision=lax.Precision.HIGHEST,
         preferred_element_type=jnp.float32,
     )
-    fill_messages((late,), -1, xu, xd, yu, yd)
 
 
 def early_kernel(late_in, xl, xh, yl, yh, frac, vel, late, out, hold, sems):
     del late_in
-    fill_ring((late,), -1, xl, xh, yl, yh)
-
-    def plane(x):
-        return pltpu.make_async_copy(hold.at[x], out.at[:, x], sems.at[x])
-
-    @pl.loop(0, CX)
-    def _(x):
-        for yt in range(CY // TILE):
-            b = [late[i, x, rows(yt), :] for i in range(Q)]
-            t, _ = covector(b)
-            u = [vel[axis, x, rows(yt), :] for axis in range(3)]
-            result = pull_back(b, t, u, frac[x, rows(yt)])
-            for i in range(Q):
-                hold[x, i, rows(yt), :] = result[i]
-        plane(x).start()
-
-    for x in range(CX):
-        plane(x).wait()
+    fill_x((late,), -1, xl, xh)
+    fill_y((late,), -1, yl, yh)
+
+    def planes(n):
+        part = pl.ds(n * PLANES, PLANES)
+        return pltpu.make_async_copy(hold.at[:, part], out.at[:, part], sems.at[n])
+
+    @pl.loop(0, CX // PLANES)
+    def _(n):
+        for k in range(PLANES):
+            x = n * PLANES + k
+            for yt in range(CY // TILE):
+                b = [late[i, x, rows(yt), :] for i in range(Q)]
+                t, _ = covector(b)
+                u = [vel[axis, x, rows(yt), :] for axis in range(3)]
+                result = pull_back(b, t, u, frac[x, rows(yt)])
+                for i in range(Q):
+                    hold[i, x, rows(yt), :] = result[i]
+        planes(n).start()
+
+    for n in range(CX // PLANES):
+        planes(n).wait()
 
 
 def owner_kernel(late, got, out):
@@ -477,52 +555,67 @@
     return lax.ppermute(block, axis, [(i, (i + step) % count) for i in range(count)])
 
 
-def exchange(messages, direction, fields):
-    x_up, x_down, y_up, y_down = messages
+def body(populations, porosity, adjoint_in, porous, walls, owners, slots):
+    ints = pltpu.VMEM((CX, CY, NZ), jnp.int32)
+    dma = pltpu.SemaphoreType.DMA
+    table, y_up, y_down = call(
+        edge_kernel,
+        [populations, porosity, porous, walls, owners.reshape(1, 64), slots.reshape(1, 64)],
+        [vmem(16, NZ), MESSAGE, MESSAGE],
+        scratch=[vmem(2, Q, CX, NZ), vmem(2, CX, NZ)]
+        + [pltpu.VMEM((2, CX, NZ), jnp.int32)] * 2
+        + [pltpu.VMEM((1, 64), jnp.int32)] * 2
+        + [dma((10,))],
+        hbm_ins=6,
+    )
+    y_low = shift(y_up, "gy", 1)
+    y_high = shift(y_down, "gy", -1)
+    moved, gap, adjoint, frac, mask, vel = call(
+        forward_kernel,
+        [populations, porosity, porous, walls, adjoint_in],
+        [FIELD] * 3 + [NODE] * 2 + [vmem(3, CX, CY, NZ)],
+        scratch=[FIELD, NODE, ints, ints, dma((CX // PLANES,)), dma((4,))],
+        hbm_ins=5,
+        flops=20_000_000,
+    )
+    moved, gap, ext, x_up, x_down = call(
+        turn_kernel,
+        [moved, gap, table, y_low, y_high],
+        [FIELD, FIELD, vmem(16, NZ), MESSAGE, MESSAGE],
+        aliases={0: 0, 1: 1},
+    )
+    x_low = shift(x_up, "gx", 1)
+    x_high = shift(x_down, "gx", -1)
+    late, sums = call(
+        late_kernel,
+        [moved, gap, adjoint, frac, mask],
+        [FIELD, vmem(EXT_XB, EXT_Y, NZ)],
+        flops=20_000_000,
+    )
+    late, _, send, x_up, x_down, y_up, y_down = call(
+        late_rest_kernel,
+        [late, sums, moved, gap, ext, x_low, x_high, adjoint, frac, mask],
+        [FIELD, vmem(EXT_XB, EXT_Y, NZ), vmem(DEVICES, NZ)] + [SHORT_MESSAGE] * 4,
+        scratch=[vmem(16, NZ)] + [LINES] * 2,
+        aliases={0: 0, 1: 1},
+    )
+    got = lax.all_to_all(send, ("gx", "gy"), split_axis=0, concat_axis=0, tiled=True)
     x_low = shift(x_up, "gx", 1)
     x_high = shift(x_down, "gx", -1)
     y_up, y_down = call(
-        functools.partial(corner_kernel, direction=direction, fields=fields),
+        corner_kernel,
         [x_low, x_high, y_up, y_down],
-        [MESSAGE if fields == 2 else SHORT_MESSAGE] * 2,
+        [SHORT_MESSAGE] * 2,
         aliases={2: 0, 3: 1},
     )
     y_low = shift(y_up, "gy", 1)
     y_high = shift(y_down, "gy", -1)
-    return x_low, x_high, y_low, y_high
-
-
-def body(populations, porosity, adjoint_in, porous, walls, owners, slots):
-    ints = pltpu.VMEM((CX, CY, NZ), jnp.int32)
-    moved, gap, adjoint, frac, mask, vel, table, *messages = call(
-        forward_kernel,
-        [populations, porosity, adjoint_in, porous, walls]
-        + [owners.reshape(1, 64), slots.reshape(1, 64)],
-        [FIELD] * 3 + [NODE] * 2 + [vmem(3, CX, CY, NZ), vmem(16, NZ)] + [MESSAGE] * 4,
-        scratch=[FIELD, NODE, ints, ints]
-        + [pltpu.VMEM((1, 64), jnp.int32)] * 2
-        + [pltpu.SemaphoreType.DMA((CX,)), pltpu.SemaphoreType.DMA((6,))],
-        hbm_ins=7,
-    )
-    halos = exchange(messages, 1, 2)
-    owner_of, place, slot = call(
-        routing_kernel, [table, *halos], [LINES] * 3, scratch=[vmem(16, NZ)]
-    )
-    _, _, late, send, *messages = call(
-        late_kernel,
-        [moved, gap, *halos, adjoint, frac, mask, owner_of, place, slot],
-        [FIELD] * 3 + [vmem(DEVICES, NZ)] + [SHORT_MESSAGE] * 4,
-        scratch=[vmem(EXT_XB, EXT_Y, NZ), LINES],
-        aliases={0: 0, 1: 1},
-    )
-    got = lax.all_to_all(send, ("gx", "gy"), split_axis=0, concat_axis=0, tiled=True)
-    halos = exchange(messages, -1, 1)
     late, adjoint_out = call(
         early_kernel,
-        [late, *halos, frac, vel],
+        [late, x_low, x_high, y_low, y_high, frac, vel],
         [FIELD],
         hbm_outs=[jax.ShapeDtypeStruct((Q, CX, CY, NZ), jnp.float32)],
-        scratch=[vmem(CX, Q, CY, NZ), pltpu.SemaphoreType.DMA((CX,))],
+        scratch=[FIELD, dma((CX // PLANES,))],
         aliases={0: 0},
     )
     (patch,) = call(owner_kernel, [late, got], [vmem(1, PATCH_DEV)])

time: 46.7 us -> 40 us (0.86)
  waiting for transfers between devices: 8.41 us -> 3.92 us
  Pallas kernels: 12.1 us -> 11 us
  starting transfers between devices: 24.7 us -> 23.6 us
    ppermute x8, waiting for transfers between devices: 8.34 us -> 3.83 us  [shift(): lax.ppermute(block, axis, [(i, (i + step) % count) for i in range(count)])]
    all_to_all x1, starting transfers between devices: 9.34 us -> 8.17 us  [body(): lax.all_to_all(send, ('gx', 'gy'), split_axis=0, concat_axis=0, tiled=True)]
    pallas_call x7 -> x8, Pallas kernels: 12.1 us -> 11 us  [call(): pl.pallas_call(kernel, out_shape=[*outs, *hbm_outs], in_specs=[ANY] * hbm...]
  transfers between devices with their start and end apart: 9 -> 9, of which waited for: 5 -> 3; matrix products, arithmetic and copies ran while one was open for 0% -> 0% of each run, Pallas kernels for 5% -> 18%
where the time goes in v3:
time: 40 us; the launch traced here: 39.9 us
  starting transfers between devices  23.6 us (59%)
  Pallas kernels  11 us (28%)
  waiting for transfers between devices  3.92 us (10%)
  between operations  0.72 us (2%)
  local copies, waits for them, and re-layouts  0.57 us (1%)
    ppermute x8, starting transfers between devices, shift(): lax.ppermute(block, axis, [(i, (i + step) % count) for i in range(count)])  15.5 us
    pallas_call x8, Pallas kernels, call(): pl.pallas_call(kernel, out_shape=[*outs, *hbm_outs], in_specs=[ANY] * hbm...  11 us
    all_to_all x1, starting transfers between devices, body(): lax.all_to_all(send, ('gx', 'gy'), split_axis=0, concat_axis=0, tiled=True)  8.17 us
    ppermute x8, waiting for transfers between devices, shift(): lax.ppermute(block, axis, [(i, (i + step) % count) for i in range(count)])  3.83 us
  transfers between devices with their start and end apart: 9, of which 3 were waited for; matrix products, arithmetic and copies ran while one was open for 0% of the time, Pallas kernels for 18%

profile of v3, /device:TPU:1, one launch (start us, length us, event | category | flops | bytes accessed | tf_op | source)
XLA Modules:
  0.0 39.9 jit_solution(883029640004427793)
XLA Ops:
  0.6 1.3 %shard_map.87 = (f32[16,128]{1,0:T(8,128)S(1)}, f32[168,128]{1,0:T(8,128)S(1)}, f32[168,128]{1,0:T(8,128)S(1)}) custom-call(f32[19,16,16,128]{3,2,1,0:T(8,128)} %f_hbm.3, f32[16,16,128]{2,1,0:T(8,128)} %porosity_hbm.3, s32[16,16,128]{2,1,0:T(8,128)} %porous_hbm.3, s32[16,16,128]{2,1,0:T(8,128)} %walls_hbm.3, s32[1,64]{1,0:T(1,128)} %bitcast.9, s32[1,64]{1,0:T(1,128)} %bitcast.10), custom_call_target="tpu_custom_call" | custom-call | tf_op jit(solution)/shard_map/pallas_call | solution.py:534
  2.0 2.2 %collective-permute-start = (f32[168,128]{1,0:T(8,128)S(1)}, f32[168,128]{1,0:T(8,128)S(1)}, u32[]{:S(2)}, u32[]{:S(2)}) collective-permute-start(f32[168,128]{1,0:T(8,128)S(1)} %get-tuple-element.31), channel_id=1, source_target_pairs={{0,1},{1,2},{2,3},{3,4},{4,5},{5,6},{6,7},{7,8},{8,9},{9,10},{10,1... | collective-permute-start | bytes 258056 | tf_op jit(solution)/shard_map/ppermute | solution.py:555
  4.2 5.0 %collective-permute-start.1 = (f32[168,128]{1,0:T(8,128)S(1)}, f32[168,128]{1,0:T(8,128)S(1)}, u32[]{:S(2)}, u32[]{:S(2)}) collective-permute-start(f32[168,128]{1,0:T(8,128)S(1)} %get-tuple-element.32), channel_id=1, source_target_pairs={{0,15},{1,0},{2,1},{3,2},{4,3},{5,4},{6,5},{7,6},{8,7},{9,8},{10,9... | collective-permute-start | bytes 258056 | tf_op jit(solution)/shard_map/ppermute | solution.py:555
  9.2 3.1 %shard_map.86 = (f32[19,16,16,128]{3,2,1,0:T(8,128)S(1)}, f32[19,16,16,128]{3,2,1,0:T(8,128)S(1)}, f32[19,16,16,128]{3,2,1,0:T(8,128)S(1)}, f32[16,16,128]{2,1,0...) custom-call(f32[19,16,16,128]{3,2,1,0:T(8,128)} %f_hbm.3, f32[16,16,128]{2,1,0:T(8,128)} %porosity_hbm.3, ...), custom_call_target="tpu_custom_call" | custom-call | flops 20000000 | tf_op jit(solution)/shard_map/pallas_call | solution.py:534
  12.2 0.0 collective-permute-done.y_low
  12.2 0.0 collective-permute-done.1.y_high
  12.3 0.1 shard_map.88
  12.4 2.1 %collective-permute-start.2 = (f32[168,128]{1,0:T(8,128)S(1)}, f32[168,128]{1,0:T(8,128)S(1)}, u32[]{:S(2)}, u32[]{:S(2)}) collective-permute-start(f32[168,128]{1,0:T(8,128)S(1)} %get-tuple-element.41), channel_id=1, source_target_pairs={{0,16},{16,32},{32,48},{48,64},{64,80},{80,96},{96,112},{112,0},{1... | collective-permute-start | bytes 258056 | tf_op jit(solution)/shard_map/ppermute | solution.py:555
  14.5 0.0 collective-permute-start.3
  14.5 1.8 %shard_map.89 = (f32[19,16,16,128]{3,2,1,0:T(8,128)S(1)}, f32[10,32,128]{2,1,0:T(8,128)S(1)}) custom-call(f32[19,16,16,128]{3,2,1,0:T(8,128)S(1)} %get-tuple-element.33.moved, f32[19,16,16,128]{3,2,1,0:T(8,128)S(1)} %get-tuple-element.34.gap, f32[19,16,16,128]{3,2,1,0:T(8,128)S(1)} %get-tuple-element.35.adjoint, f32[16,16,128]{2,1,0:T(8,128)S(1)} %get-tuple-element.36.frac, ...), custom_call_target="tpu_custom_call" | custom-call | flops 20000000 | tf_op jit(solution)/shard_map/pallas_call | solution.py:534
  16.3 0.0 collective-permute-done.2.x_low
  16.3 2.1 %collective-permute-done.3.x_high = f32[168,128]{1,0:T(8,128)S(1)} collective-permute-done((f32[168,128]{1,0:T(8,128)S(1)}, f32[168,128]{1,0:T(8,128)S(1)}, u32[]{:S(2)}, u32[]{:S(2)}) %collective-permute-start.3) | collective-permute-done | bytes 86048 | tf_op jit(solution)/shard_map/ppermute | solution.py:555
  18.4 1.7 %shard_map.90 = (f32[19,16,16,128]{3,2,1,0:T(8,128)S(1)}, f32[10,32,128]{2,1,0:T(8,128)S(1)}, f32[128,128]{1,0:T(8,128)}, f32[80,128]{1,0:T(8,128)S(1)}, f32[80,...) custom-call(f32[19,16,16,128]{3,2,1,0:T(8,128)S(1)} %get-tuple-eleme, ...), custom_call_target="tpu_custom_call", output_to_operand_aliasing={{0}: (0, {}), {1}: (1, {})} | custom-call | tf_op jit(solution)/shard_map/pallas_call | solution.py:534
  20.1 0.0 collective-permute-start.4
  20.1 0.5 %collective-permute-start.5 = (f32[80,128]{1,0:T(8,128)S(1)}, f32[80,128]{1,0:T(8,128)S(1)}, u32[]{:S(2)}, u32[]{:S(2)}) collective-permute-start(f32[80,128]{1,0:T(8,128)S(1)} %get-tuple-element.45), channel_id=1, source_target_pairs={{0,112},{16,0},{32,16},{48,32},{64,48},{80,64},{96,80},{112,96},{1... | collective-permute-start | bytes 122888 | tf_op jit(solution)/shard_map/ppermute | solution.py:555
  20.6 8.2 %all-to-all-start = ((f32[128,1,128]{2,1,0:T(1,128)}), f32[128,1,128]{2,1,0:T(1,128)S(1)}, u32[]{:S(2)}, u32[]{:S(2)}) async-start(f32[128,1,128]{2,1,0:T(1,128)} %bitcast.3), calls=%async_computation | async-start | bytes 131072 | tf_op jit(solution)/shard_map/all_to_all | solution.py:602
  28.8 0.0 collective-permute-done.4.x_low.xl
  28.8 0.0 collective-permute-done.5.x_high.xh
  28.8 1.5 %collective-permute-start.6 = (f32[80,128]{1,0:T(8,128)S(1)}, f32[80,128]{1,0:T(8,128)S(1)}, u32[]{:S(2)}, u32[]{:S(2)}) collective-permute-start(f32[80,128]{1,0:T(8,128)S(1)} %get-tuple-element.48), channel_id=1, source_target_pairs={{0,1},{1,2},{2,3},{3,4},{4,5},{5,6},{6,7},{7,8},{8,9},{9,10},{10,1... | collective-permute-start | bytes 122888 | tf_op jit(solution)/shard_map/ppermute | solution.py:555
  30.3 4.3 %collective-permute-start.7 = (f32[80,128]{1,0:T(8,128)S(1)}, f32[80,128]{1,0:T(8,128)S(1)}, u32[]{:S(2)}, u32[]{:S(2)}) collective-permute-start(f32[80,128]{1,0:T(8,128)S(1)} %get-tuple-element.49), channel_id=1, source_target_pairs={{0,15},{1,0},{2,1},{3,2},{4,3},{5,4},{6,5},{7,6},{8,7},{9,8},{10,9... | collective-permute-start | bytes 122888 | tf_op jit(solution)/shard_map/ppermute | solution.py:555
  34.5 1.8 %collective-permute-done.6.yl = f32[80,128]{1,0:T(8,128)S(1)} collective-permute-done((f32[80,128]{1,0:T(8,128)S(1)}, f32[80,128]{1,0:T(8,128)S(1)}, u32[]{:S(2)}, u32[]{:S(2)}) %collective-permute-start.6) | collective-permute-done | bytes 40992 | tf_op jit(solution)/shard_map/ppermute | solution.py:555
  36.3 0.0 collective-permute-done.7.yh
  36.3 2.2 %shard_map.92 = (f32[19,16,16,128]{3,2,1,0:T(8,128)S(1)}, f32[19,16,16,128]{3,2,1,0:T(8,128)}) custom-call(f32[19,16,16,128]{3,2,1,0:T(8,128)S(1)} %get-tuple-element.43.late_in, f32[80,128]{1,0:T(8,128)S(1)} %collective-permute-done.4.x_low.xl, f32[80,128]{1,0:T(8,128)S(1)} %collective-permute-done.5.x_high.xh, ...), custom_call_target="tpu_custom_call", output_to_operand_aliasing={{0}: (0, {})} | custom-call | tf_op jit(solution)/shard_map/pallas_call | solution.py:534
  38.4 0.1 all-to-all-done
  38.5 0.8 %shard_map.93 = f32[1,256]{1,0:T(1,128)S(1)} custom-call(f32[19,16,16,128]{3,2,1,0:T(8,128)S(1)} %get-tuple-element.52.late, f32[128,128]{1,0:T(8,128)S(1)} %bitcast.8), custom_call_target="tpu_custom_call" | custom-call | tf_op jit(solution)/shard_map/pallas_call | solution.py:534
  39.3 0.6 %copy.24 = f32[256]{0:T(256)} copy(f32[256]{0:T(256)S(1)} %bitcast.7) | data formatting | bytes 2048
  (1 shorter events, 0.0 us)
Async XLA Ops:
  2.0 10.3 %collective-permute-start = (f32[168,128]{1,0:T(8,128)S(1)}, f32[168,128]{1,0:T(8,128)S(1)}, u32[]{:S(2)}, u32[]{:S(2)}) collective-permute-start(f32[168,128]{1,0:T(8,128)S(1)} %get-tuple-element.31), channel_id=1, source_target_pairs={{0,1},{1,2},{2,3},{3,4},{4,5},{5,6},{6,7},{7,8},{8,9},{9,10},{10,1... | collective-permute-start | bytes 258056 | tf_op jit(solution)/shard_map/ppermute | solution.py:555
  4.2 8.1 %collective-permute-start.1 = (f32[168,128]{1,0:T(8,128)S(1)}, f32[168,128]{1,0:T(8,128)S(1)}, u32[]{:S(2)}, u32[]{:S(2)}) collective-permute-start(f32[168,128]{1,0:T(8,128)S(1)} %get-tuple-element.32), channel_id=1, source_target_pairs={{0,15},{1,0},{2,1},{3,2},{4,3},{5,4},{6,5},{7,6},{8,7},{9,8},{10,9... | collective-permute-start | bytes 258056 | tf_op jit(solution)/shard_map/ppermute | solution.py:555
  12.4 3.9 %collective-permute-start.2 = (f32[168,128]{1,0:T(8,128)S(1)}, f32[168,128]{1,0:T(8,128)S(1)}, u32[]{:S(2)}, u32[]{:S(2)}) collective-permute-start(f32[168,128]{1,0:T(8,128)S(1)} %get-tuple-element.41), channel_id=1, source_target_pairs={{0,16},{16,32},{32,48},{48,64},{64,80},{80,96},{96,112},{112,0},{1... | collective-permute-start | bytes 258056 | tf_op jit(solution)/shard_map/ppermute | solution.py:555
  14.5 3.9 %collective-permute-start.3 = (f32[168,128]{1,0:T(8,128)S(1)}, f32[168,128]{1,0:T(8,128)S(1)}, u32[]{:S(2)}, u32[]{:S(2)}) collective-permute-start(f32[168,128]{1,0:T(8,128)S(1)} %get-tuple-element.42), channel_id=1, source_target_pairs={{0,112},{16,0},{32,16},{48,32},{64,48},{80,64},{96,80},{112,96},{1... | collective-permute-start | bytes 258056 | tf_op jit(solution)/shard_map/ppermute | solution.py:555
  20.1 8.7 %collective-permute-start.4 = (f32[80,128]{1,0:T(8,128)S(1)}, f32[80,128]{1,0:T(8,128)S(1)}, u32[]{:S(2)}, u32[]{:S(2)}) collective-permute-start(f32[80,128]{1,0:T(8,128)S(1)} %get-tuple-element.44), channel_id=1, source_target_pairs={{0,16},{16,32},{32,48},{48,64},{64,80},{80,96},{96,112},{112,0},{1... | collective-permute-start | bytes 122888 | tf_op jit(solution)/shard_map/ppermute | solution.py:555
  20.1 8.7 %collective-permute-start.5 = (f32[80,128]{1,0:T(8,128)S(1)}, f32[80,128]{1,0:T(8,128)S(1)}, u32[]{:S(2)}, u32[]{:S(2)}) collective-permute-start(f32[80,128]{1,0:T(8,128)S(1)} %get-tuple-element.45), channel_id=1, source_target_pairs={{0,112},{16,0},{32,16},{48,32},{64,48},{80,64},{96,80},{112,96},{1... | collective-permute-start | bytes 122888 | tf_op jit(solution)/shard_map/ppermute | solution.py:555
  20.6 17.9 %all-to-all-start = ((f32[128,1,128]{2,1,0:T(1,128)}), f32[128,1,128]{2,1,0:T(1,128)S(1)}, u32[]{:S(2)}, u32[]{:S(2)}) async-start(f32[128,1,128]{2,1,0:T(1,128)} %bitcast.3), calls=%async_computation | async-start | bytes 131072 | tf_op jit(solution)/shard_map/all_to_all | solution.py:602
  28.8 7.5 %collective-permute-start.6 = (f32[80,128]{1,0:T(8,128)S(1)}, f32[80,128]{1,0:T(8,128)S(1)}, u32[]{:S(2)}, u32[]{:S(2)}) collective-permute-start(f32[80,128]{1,0:T(8,128)S(1)} %get-tuple-element.48), channel_id=1, source_target_pairs={{0,1},{1,2},{2,3},{3,4},{4,5},{5,6},{6,7},{7,8},{8,9},{9,10},{10,1... | collective-permute-start | bytes 122888 | tf_op jit(solution)/shard_map/ppermute | solution.py:555
  30.3 6.0 %collective-permute-start.7 = (f32[80,128]{1,0:T(8,128)S(1)}, f32[80,128]{1,0:T(8,128)S(1)}, u32[]{:S(2)}, u32[]{:S(2)}) collective-permute-start(f32[80,128]{1,0:T(8,128)S(1)} %get-tuple-element.49), channel_id=1, source_target_pairs={{0,15},{1,0},{2,1},{3,2},{4,3},{5,4},{6,5},{7,6},{8,7},{9,8},{10,9... | collective-permute-start | bytes 122888 | tf_op jit(solution)/shard_map/ppermute | solution.py:555

commit v4 on v3

--- a/solution.py
+++ b/solution.py
@@ -13,10 +13,13 @@
 PAD_Y = 8
 EXT_Y = 32
 EXT_XB = 10
-BLOCK_ROWS = EXT_XB * EXT_Y
+RING = 80
+LINE_COUNT = 112
 DEVICES = 128
+N_GX, N_GY = 8, 16
 PATCH_DEV = 256
 SLOT_LANE = 64
+PARTS = 14
 FACE = 80
 META = 160
 MESSAGE_ROWS = 168
@@ -199,11 +202,24 @@
     store_wrapped(put, yt * TILE, cy, value)
 
 
-def x_faces(fields, direction, x_up, x_down):
+def by_parity(even, odd):
+    is_odd = jnp.full(even.shape, lax.axis_index("gx") & 1, jnp.int32) == 1
+    return jnp.where(is_odd, odd, even)
+
+
+def x_faces(fields, direction, first, second):
     for n, field in enumerate(fields):
-        for sign, x, message in ((1, 0, x_up), (-1, CX - 1, x_down)):
-            for k, i in enumerate(moving(0, sign, direction)):
-                message[pl.ds(n * FACE + k * CY, CY), :] = field[i, x]
+        pairs = zip(moving(0, 1, direction), moving(0, -1, direction))
+        for k, (i_up, i_down) in enumerate(pairs):
+            up, down = field[i_up, 0], field[i_down, CX - 1]
+            line = pl.ds(n * FACE + k * CY, CY)
+            first[line, :] = by_parity(down, up)
+            second[line, :] = by_parity(up, down)
+
+
+def x_arrived(sign, line, first, second):
+    a, b = first[line, :], second[line, :]
+    return by_parity(a, b) if sign == 1 else by_parity(b, a)
 
 
 def y_faces(fields, direction, y_up, y_down):
@@ -214,11 +230,12 @@
                     message[pl.ds(n * FACE + k * CX + x, 1), :] = field[i, x, pl.ds(row, 1), :]
 
 
-def fill_x(fields, direction, x_low, x_high):
+def fill_x(fields, direction, first, second):
     for n, field in enumerate(fields):
-        for sign, x, message in ((1, 0, x_low), (-1, CX - 1, x_high)):
+        for sign, x in ((1, 0), (-1, CX - 1)):
             for k, i in enumerate(moving(0, sign, direction)):
-                field[i, x] = message[pl.ds(n * FACE + k * CY, CY), :]
+                line = pl.ds(n * FACE + k * CY, CY)
+                field[i, x] = x_arrived(sign, line, first, second)
 
 
 def fill_y(fields, direction, y_low, y_high):
@@ -370,35 +387,24 @@
     later.wait()
 
 
-def turn_kernel(moved_in, gap_in, table, y_low, y_high, moved, gap, ext, x_up, x_down):
+def turn_kernel(moved_in, gap_in, table, y_low, y_high, moved, gap, ext, first, second):
     del moved_in, gap_in
     fill_y((moved, gap), 1, y_low, y_high)
-    x_faces((moved, gap), 1, x_up, x_down)
+    x_faces((moved, gap), 1, first, second)
     shape = (16, NZ)
     row, lane = iota(shape, 0), iota(shape, 1)
     low = column(y_low[pl.ds(META, 1), :], row == lane)
     high = column(y_high[pl.ds(META, 1), :], row == lane)
     held = jnp.where(lane == 0, low, jnp.where(lane == 9, high, table[...]))
     ext[...] = held
-    x_up[pl.ds(META, 1), :] = held[8:9]
-    x_down[pl.ds(META, 1), :] = held[1:2]
-
-
-def corner_kernel(x_low, x_high, up_in, down_in, up, down):
-    del up_in, down_in
-    for sign, row, message in ((1, 0, up), (-1, CY - 1, down)):
-        for k, i in enumerate(moving(1, sign, -1)):
-            cx = -velocities[i][0]
-            if cx:
-                source, x = (x_low, 0) if cx == 1 else (x_high, CX - 1)
-                corner = moving(0, cx, -1).index(i) * CY + row
-                message[pl.ds(k * CX + x, 1), :] = source[pl.ds(corner, 1), :]
-
-
-def late_blocks(xb, take, adjoint, frac, mask, late, sums):
+    first[pl.ds(META, 1), :] = by_parity(held[1:2], held[8:9])
+    second[pl.ds(META, 1), :] = by_parity(held[8:9], held[1:2])
+
+
+def late_blocks(xb, halves, take, adjoint, frac, mask, late, sums):
     for yt in range(CY // TILE):
         parts = {}
-        for half in range(2):
+        for half in halves:
             x = xb * 2 + half
             at = (x, rows(yt))
             read = [take(0, i, x, yt) for i in range(Q)]
@@ -428,95 +434,154 @@
     def take(n, i, x, yt):
         return fields[n][i, x, rows(yt), :]
 
-    def step(xb):
-        late_blocks(xb, take, adjoint, frac, mask, late, sums)
-
+    def step(xb, halves=(0, 1)):
+        late_blocks(xb, halves, take, adjoint, frac, mask, late, sums)
+
+    step(0, (1,))
+    step(CX // 2 - 1, (0,))
     unrolled(1, CX // 2 - 1, 2, step)
 
 
 def late_rest_kernel(
-    late_in, sums_in, moved, gap, ext_in, x_low, x_high, adjoint, frac, mask,
-    late, sums, send, xu, xd, yu, yd, ext, owner_of, scaled,
+    late_in, sums_in, moved, gap, ext_in, first, second, adjoint, frac, mask,
+    late, sums, xf, xs, yu, yd, send_hbm, ext, ring, owner_of, scaled, send, sem,
 ):
     del late_in, sums_in
     fields = (moved, gap)
 
     def take(n, i, x, yt):
         cx = velocities[i][0]
-        for sign, place, message in ((1, 0, x_low), (-1, CX - 1, x_high)):
-            if cx == sign and x == place:
-                first = n * FACE + moving(0, sign, 1).index(i) * CY + yt * TILE
-                return message[pl.ds(first, TILE), :]
+        if (cx, x) in ((1, 0), (-1, CX - 1)):
+            start = n * FACE + moving(0, cx, 1).index(i) * CY + yt * TILE
+            return x_arrived(cx, pl.ds(start, TILE), first, second)
         return fields[n][i, x, rows(yt), :]
 
-    for xb in (0, CX // 2 - 1):
-        late_blocks(xb, take, adjoint, frac, mask, late, sums)
-    x_faces((late,), -1, xu, xd)
-    y_faces((late,), -1, yu, yd)
+    for xb, half in ((0, 0), (CX // 2 - 1, 1)):
+        late_blocks(xb, (half,), take, adjoint, frac, mask, late, sums)
 
     row = iota((16, NZ), 0)
-    held = jnp.where(row == 0, x_low[pl.ds(META, 1), :], ext_in[...])
-    ext[...] = jnp.where(row == 9, x_high[pl.ds(META, 1), :], held)
-    shape = (EXT_Y, NZ)
-    row, lane = iota(shape, 0), iota(shape, 1)
-    yb = jnp.right_shift(row - 6, 1)
-    pick = lane == yb
-    side_y = jnp.where(yb == 0, 0, jnp.where(yb == 9, 2, 1))
-    used = (row >= PAD_Y - 1) & (row <= PAD_Y + CY)
-    first = used & ((yb == 0) | ((row & 1) == 0))
+    numbers = pl.ds(META, 1)
+    held = jnp.where(row == 0, x_arrived(1, numbers, first, second), ext_in[...])
+    ext[...] = jnp.where(row == 9, x_arrived(-1, numbers, first, second), held)
+
+    def put_lines(start, number, spot, total):
+        number = number.astype(jnp.int32)
+        lane = iota((total.shape[0], NZ), 1)
+        spot = spot + (number & 3) if isinstance(spot, int) else spot(number & 3)
+        line = pl.ds(start, total.shape[0])
+        owner_of[line, :] = jnp.where(lane == jnp.right_shift(number, 10), 1.0, 0.0)
+        patch = (jnp.right_shift(number, 2) & 255).astype(jnp.float32)
+        value = jnp.where(lane == spot, jnp.sum(total, axis=1, keepdims=True), 0.0)
+        scaled[line, :] = jnp.where(lane == spot + SLOT_LANE, patch, value)
+
+    pick = iota((8, NZ), 1) == iota((8, NZ), 0) + 1
     for xb in range(EXT_XB):
-        number = column(ext[pl.ds(xb, 1), :], pick).astype(jnp.int32)
-        side = side_y * 6 + (0 if xb == 0 else 4 if xb == 9 else 2)
-        spot = side + (number & 3)
-        line = pl.ds(xb * EXT_Y, EXT_Y)
-        owner_of[line, :] = jnp.where(used & (lane == jnp.right_shift(number, 10)), 1.0, 0.0)
-        patch = (jnp.right_shift(number, 2) & 255).astype(jnp.float32)
-        value = jnp.where(lane == spot, jnp.sum(sums[xb], axis=1, keepdims=True), 0.0)
-        scaled[line, :] = jnp.where(first & (lane == spot + SLOT_LANE), patch, value)
-    send[...] = lax.dot_general(
+        total = sums[xb, pl.ds(PAD_Y, 8, stride=2), :] + sums[xb, pl.ds(PAD_Y + 1, 8, stride=2), :]
+        spot = 2 if xb == 0 else 4 if xb == 9 else 0
+        put_lines(xb * 8, column(ext[pl.ds(xb, 1), :], pick), spot, total)
+    ring[...] = jnp.zeros((32, NZ), jnp.float32)
+    for xb in range(EXT_XB):
+        ring[pl.ds(xb, 1), :] = sums[xb, pl.ds(PAD_Y - 1, 1), :]
+        ring[pl.ds(16 + xb, 1), :] = sums[xb, pl.ds(PAD_Y + CY, 1), :]
+    row = iota((16, 1), 0)
+    for n, (face, corner, lane) in enumerate(((6, 10, 0), (8, 12, 9))):
+
+        def spot(rank, face=face, corner=corner):
+            side = jnp.where(row == 9, corner + 1, face + rank)
+            return jnp.where(row == 0, corner, side)
+
+        pick = (iota((16, NZ), 1) == lane) & (iota((16, NZ), 0) < EXT_XB)
+        total = ring[pl.ds(16 * n, 16), :]
+        put_lines(RING + 16 * n, column(ext[...], pick), spot, total)
+    send[pl.ds(0, DEVICES, stride=2), :] = lax.dot_general(
         owner_of[...],
         scaled[...],
         (((0,), (0,)), ((), ())),
         precision=lax.Precision.HIGHEST,
         preferred_element_type=jnp.float32,
     )
-
-
-def early_kernel(late_in, xl, xh, yl, yh, frac, vel, late, out, hold, sems):
+    for there, i, x, y in corners(1):
+        send[pl.ds(2 * there + 1, 1), :] = late[i, x, pl.ds(y, 1), :]
+    copy = pltpu.make_async_copy(send, send_hbm, sem)
+    copy.start()
+    x_faces((late,), -1, xf, xs)
+    y_faces((late,), -1, yu, yd)
+    copy.wait()
+
+
+def corners(direction):
+    gx, gy = lax.axis_index("gx"), lax.axis_index("gy")
+    for ex in (1, -1):
+        for ey in (1, -1):
+            there_x = (gx + direction * ex) & (N_GX - 1)
+            there_y = (gy + direction * ey) & (N_GY - 1)
+            i = velocities.index((-ex, -ey, 0))
+            x, y = 0 if ex == 1 else CX - 1, 0 if ey == 1 else CY - 1
+            yield there_x * N_GY + there_y, i, x, y
+
+
+def early_plane(x, late, frac, vel, put):
+    for yt in range(CY // TILE):
+        b = [late[i, x, rows(yt), :] for i in range(Q)]
+        t, _ = covector(b)
+        u = [vel[axis, x, rows(yt), :] for axis in range(3)]
+        result = pull_back(b, t, u, frac[x, rows(yt)])
+        for i in range(Q):
+            put(i, yt, result[i])
+
+
+def early_kernel(late_in, yl, yh, frac, vel, late, out, hold, sems):
     del late_in
-    fill_x((late,), -1, xl, xh)
     fill_y((late,), -1, yl, yh)
 
     def planes(n):
-        part = pl.ds(n * PLANES, PLANES)
+        part = pl.ds(1 + n * 2, 2)
         return pltpu.make_async_copy(hold.at[:, part], out.at[:, part], sems.at[n])
 
-    @pl.loop(0, CX // PLANES)
+    @pl.loop(0, CX // 2 - 1)
     def _(n):
-        for k in range(PLANES):
-            x = n * PLANES + k
-            for yt in range(CY // TILE):
-                b = [late[i, x, rows(yt), :] for i in range(Q)]
-                t, _ = covector(b)
-                u = [vel[axis, x, rows(yt), :] for axis in range(3)]
-                result = pull_back(b, t, u, frac[x, rows(yt)])
-                for i in range(Q):
-                    hold[i, x, rows(yt), :] = result[i]
+        for k in range(2):
+            x = 1 + n * 2 + k
+
+            def put(i, yt, value, x=x):
+                hold[i, x, rows(yt), :] = value
+
+            early_plane(x, late, frac, vel, put)
         planes(n).start()
 
-    for n in range(CX // PLANES):
+    for n in range(CX // 2 - 1):
         planes(n).wait()
 
 
-def owner_kernel(late, got, out):
-    del late
-    patch = iota((DEVICES, PATCH_DEV), 1).astype(jnp.float32)
-    data = got[...]
-    total = jnp.zeros((DEVICES, PATCH_DEV), jnp.float32)
-    for k in range(18):
-        hit = data[:, SLOT_LANE + k : SLOT_LANE + k + 1] == patch
-        total = total + jnp.where(hit, data[:, k : k + 1], 0.0)
-    out[...] = jnp.sum(total, axis=0, keepdims=True)
+def last_kernel(
+    out_in, late_in, first, second, got, frac, vel, late, out, patch_out, hold, patch, sems
+):
+    del out_in, late_in
+    fill_x((late,), -1, first, second)
+    for here, i, x, y in corners(-1):
+        late[i, x, pl.ds(y, 1), :] = got[pl.ds(2 * here + 1, 1), :]
+    copies = []
+    for n, x in enumerate((0, CX - 1)):
+
+        def put(i, yt, value, n=n):
+            hold[n, i, rows(yt), :] = value
+
+        early_plane(x, late, frac, vel, put)
+        copies.append(pltpu.make_async_copy(hold.at[n], out.at[:, x], sems.at[n]))
+        copies[n].start()
+    data = got[pl.ds(0, DEVICES, stride=2), :].T
+    part = 64
+    for start in range(0, PATCH_DEV, part):
+        number = (iota((part, DEVICES), 0) + start).astype(jnp.float32)
+        total = jnp.zeros((part, DEVICES), jnp.float32)
+        for k in range(PARTS):
+            hit = data[SLOT_LANE + k : SLOT_LANE + k + 1] == number
+            total = total + jnp.where(hit, data[k : k + 1], 0.0)
+        patch[:, pl.ds(start, part)] = jnp.sum(total, axis=1)[None]
+    copies.append(pltpu.make_async_copy(patch, patch_out, sems.at[2]))
+    copies[2].start()
+    for copy in copies:
+        copy.wait()
 
 
 VMEM = pl.BlockSpec(memory_space=pltpu.VMEM)
@@ -547,12 +612,19 @@
 NODE = vmem(CX, CY, NZ)
 MESSAGE = vmem(MESSAGE_ROWS, NZ)
 SHORT_MESSAGE = vmem(FACE, NZ)
-LINES = vmem(BLOCK_ROWS, NZ)
+LINES = vmem(LINE_COUNT, NZ)
 
 
 def shift(block, axis, step):
     count = lax.axis_size(axis)
     return lax.ppermute(block, axis, [(i, (i + step) % count) for i in range(count)])
+
+
+def swap(block, axis, step):
+    count = lax.axis_size(axis)
+    return lax.ppermute(
+        block, axis, [(i, (i + (-step if i % 2 else step)) % count) for i in range(count)]
+    )
 
 
 def body(populations, porosity, adjoint_in, porous, walls, owners, slots):
@@ -578,47 +650,52 @@
         hbm_ins=5,
         flops=20_000_000,
     )
-    moved, gap, ext, x_up, x_down = call(
+    moved, gap, ext, first, second = call(
         turn_kernel,
         [moved, gap, table, y_low, y_high],
         [FIELD, FIELD, vmem(16, NZ), MESSAGE, MESSAGE],
         aliases={0: 0, 1: 1},
     )
-    x_low = shift(x_up, "gx", 1)
-    x_high = shift(x_down, "gx", -1)
+    first = swap(first, "gx", -1)
+    second = swap(second, "gx", 1)
     late, sums = call(
         late_kernel,
         [moved, gap, adjoint, frac, mask],
         [FIELD, vmem(EXT_XB, EXT_Y, NZ)],
         flops=20_000_000,
     )
-    late, _, send, x_up, x_down, y_up, y_down = call(
+    late, _, first, second, y_up, y_down, send = call(
         late_rest_kernel,
-        [late, sums, moved, gap, ext, x_low, x_high, adjoint, frac, mask],
-        [FIELD, vmem(EXT_XB, EXT_Y, NZ), vmem(DEVICES, NZ)] + [SHORT_MESSAGE] * 4,
-        scratch=[vmem(16, NZ)] + [LINES] * 2,
+        [late, sums, moved, gap, ext, first, second, adjoint, frac, mask],
+        [FIELD, vmem(EXT_XB, EXT_Y, NZ)] + [SHORT_MESSAGE] * 4,
+        hbm_outs=[jax.ShapeDtypeStruct((2 * DEVICES, NZ), jnp.float32)],
+        scratch=[vmem(16, NZ), vmem(32, NZ), LINES, LINES, vmem(2 * DEVICES, NZ), dma],
         aliases={0: 0, 1: 1},
     )
     got = lax.all_to_all(send, ("gx", "gy"), split_axis=0, concat_axis=0, tiled=True)
-    x_low = shift(x_up, "gx", 1)
-    x_high = shift(x_down, "gx", -1)
-    y_up, y_down = call(
-        corner_kernel,
-        [x_low, x_high, y_up, y_down],
-        [SHORT_MESSAGE] * 2,
-        aliases={2: 0, 3: 1},
-    )
     y_low = shift(y_up, "gy", 1)
     y_high = shift(y_down, "gy", -1)
+    first = swap(first, "gx", -1)
+    second = swap(second, "gx", 1)
+    adjoint_shape = jax.ShapeDtypeStruct((Q, CX, CY, NZ), jnp.float32)
     late, adjoint_out = call(
         early_kernel,
-        [late, x_low, x_high, y_low, y_high, frac, vel],
+        [late, y_low, y_high, frac, vel],
         [FIELD],
-        hbm_outs=[jax.ShapeDtypeStruct((Q, CX, CY, NZ), jnp.float32)],
-        scratch=[FIELD, dma((CX // PLANES,))],
+        hbm_outs=[adjoint_shape],
+        scratch=[FIELD, dma((CX // 2 - 1,))],
         aliases={0: 0},
-    )
-    (patch,) = call(owner_kernel, [late, got], [vmem(1, PATCH_DEV)])
+        flops=20_000_000,
+    )
+    _, adjoint_out, patch = call(
+        last_kernel,
+        [adjoint_out, late, first, second, got, frac, vel],
+        [FIELD],
+        hbm_ins=1,
+        hbm_outs=[adjoint_shape, jax.ShapeDtypeStruct((1, PATCH_DEV), jnp.float32)],
+        scratch=[vmem(2, Q, CY, NZ), vmem(1, PATCH_DEV), dma((3,))],
+        aliases={0: 1, 1: 0},
+    )
     return adjoint_out, patch.reshape(PATCH_DEV)
 
 

time: 40 us -> 38.5 us (0.963)
  waiting for transfers between devices: 3.92 us -> 0.02 us
  starting transfers between devices: 23.6 us -> 26.5 us
  local copies, waits for them, and re-layouts: 0.57 us -> 0 us
    ppermute x0 -> x4, starting transfers between devices: none -> 5.79 us  [swap(): lax.ppermute(block, axis, [(i, (i + (-step if i % 2 else step)) % count)...]
    ppermute x8 -> x4, waiting for transfers between devices: 3.83 us -> 0.01 us  [shift(): lax.ppermute(block, axis, [(i, (i + step) % count) for i in range(count)])]
    ppermute x8 -> x4, starting transfers between devices: 15.5 us -> 12.9 us  [shift(): lax.ppermute(block, axis, [(i, (i + step) % count) for i in range(count)])]
    unnamed x1 -> x0, local copies, waits for them, and re-layouts: 0.57 us -> none
    pallas_call x8 -> x7, Pallas kernels: 11 us -> 11 us  [call(): pl.pallas_call(kernel, out_shape=[*outs, *hbm_outs], in_specs=[ANY] * hbm...]
  transfers between devices with their start and end apart: 9 -> 9, of which waited for: 3 -> 0; matrix products, arithmetic and copies ran while one was open for 0% -> 0% of each run, Pallas kernels for 18% -> 19%
where the time goes in v4:
time: 38.5 us; the launch traced here: 38.3 us
  starting transfers between devices  26.5 us (69%)
  Pallas kernels  11 us (29%)
  between operations  0.74 us (2%)
    ppermute x4, starting transfers between devices, shift(): lax.ppermute(block, axis, [(i, (i + step) % count) for i in range(count)])  12.9 us
    pallas_call x7, Pallas kernels, call(): pl.pallas_call(kernel, out_shape=[*outs, *hbm_outs], in_specs=[ANY] * hbm...  11 us
    all_to_all x1, starting transfers between devices, body(): lax.all_to_all(send, ('gx', 'gy'), split_axis=0, concat_axis=0, tiled=True)  7.84 us
    ppermute x4, starting transfers between devices, swap(): lax.ppermute(block, axis, [(i, (i + (-step if i % 2 else step)) % count)...  5.79 us
  transfers between devices with their start and end apart: 9, of which 0 were waited for; matrix products, arithmetic and copies ran while one was open for 0% of the time, Pallas kernels for 19%

profile of v4, /device:TPU:1, one launch (start us, length us, event | category | flops | bytes accessed | tf_op | source)
XLA Modules:
  0.0 38.3 jit_solution(4421611239560315862)
XLA Ops:
  0.6 1.3 %shard_map.87 = (f32[16,128]{1,0:T(8,128)S(1)}, f32[168,128]{1,0:T(8,128)S(1)}, f32[168,128]{1,0:T(8,128)S(1)}) custom-call(f32[19,16,16,128]{3,2,1,0:T(8,128)} %f_hbm.3, f32[16,16,128]{2,1,0:T(8,128)} %porosity_hbm.3, s32[16,16,128]{2,1,0:T(8,128)} %porous_hbm.3, s32[16,16,128]{2,1,0:T(8,128)} %walls_hbm.3, s32[1,64]{1,0:T(1,128)} %bitcast.6, s32[1,64]{1,0:T(1,128)} %bitcast.7), custom_call_target="tpu_custom_call" | custom-call | tf_op jit(solution)/shard_map/pallas_call | solution.py:599
  2.0 2.2 %collective-permute-start = (f32[168,128]{1,0:T(8,128)S(1)}, f32[168,128]{1,0:T(8,128)S(1)}, u32[]{:S(2)}, u32[]{:S(2)}) collective-permute-start(f32[168,128]{1,0:T(8,128)S(1)} %get-tuple-element.31), channel_id=1, source_target_pairs={{0,1},{1,2},{2,3},{3,4},{4,5},{5,6},{6,7},{7,8},{8,9},{9,10},{10,1... | collective-permute-start | bytes 258056 | tf_op jit(solution)/shard_map/ppermute | solution.py:620
  4.2 5.0 %collective-permute-start.1 = (f32[168,128]{1,0:T(8,128)S(1)}, f32[168,128]{1,0:T(8,128)S(1)}, u32[]{:S(2)}, u32[]{:S(2)}) collective-permute-start(f32[168,128]{1,0:T(8,128)S(1)} %get-tuple-element.32), channel_id=1, source_target_pairs={{0,15},{1,0},{2,1},{3,2},{4,3},{5,4},{6,5},{7,6},{8,7},{9,8},{10,9... | collective-permute-start | bytes 258056 | tf_op jit(solution)/shard_map/ppermute | solution.py:620
  9.2 3.1 %shard_map.86 = (f32[19,16,16,128]{3,2,1,0:T(8,128)S(1)}, f32[19,16,16,128]{3,2,1,0:T(8,128)S(1)}, f32[19,16,16,128]{3,2,1,0:T(8,128)S(1)}, f32[16,16,128]{2,1,0...) custom-call(f32[19,16,16,128]{3,2,1,0:T(8,128)} %f_hbm.3, f32[16,16,128]{2,1,0:T(8,128)} %porosity_hbm.3, ...), custom_call_target="tpu_custom_call" | custom-call | flops 20000000 | tf_op jit(solution)/shard_map/pallas_call | solution.py:599
  12.2 0.0 collective-permute-done.y_low
  12.2 0.0 collective-permute-done.1.y_high
  12.3 0.1 shard_map.88
  12.4 2.1 %collective-permute-start.2 = (f32[168,128]{1,0:T(8,128)S(1)}, f32[168,128]{1,0:T(8,128)S(1)}, u32[]{:S(2)}, u32[]{:S(2)}) collective-permute-start(f32[168,128]{1,0:T(8,128)S(1)} %get-tuple-element.41), channel_id=1, source_target_pairs={{0,112},{16,32},{32,16},{48,64},{64,48},{80,96},{96,80},{112,0},{1... | collective-permute-start | bytes 258056 | tf_op jit(solution)/shard_map/ppermute | solution.py:625
  14.5 0.8 %collective-permute-start.3 = (f32[168,128]{1,0:T(8,128)S(1)}, f32[168,128]{1,0:T(8,128)S(1)}, u32[]{:S(2)}, u32[]{:S(2)}) collective-permute-start(f32[168,128]{1,0:T(8,128)S(1)} %get-tuple-element.42), channel_id=1, source_target_pairs={{0,16},{16,0},{32,48},{48,32},{64,80},{80,64},{96,112},{112,96},{1... | collective-permute-start | bytes 258056 | tf_op jit(solution)/shard_map/ppermute | solution.py:625
  15.4 2.2 %shard_map.89 = (f32[19,16,16,128]{3,2,1,0:T(8,128)S(1)}, f32[10,32,128]{2,1,0:T(8,128)S(1)}) custom-call(f32[19,16,16,128]{3,2,1,0:T(8,128)S(1)} %get-tuple-element.33.moved, f32[19,16,16,128]{3,2,1,0:T(8,128)S(1)} %get-tuple-element.34.gap, f32[19,16,16,128]{3,2,1,0:T(8,128)S(1)} %get-tuple-element.35.adjoint, f32[16,16,128]{2,1,0:T(8,128)S(1)} %get-tuple-element.36.frac, ...), custom_call_target="tpu_custom_call" | custom-call | flops 20000000 | tf_op jit(solution)/shard_map/pallas_call | solution.py:599
  17.5 0.0 collective-permute-done.2.first
  17.5 0.0 collective-permute-done.3.second
  17.5 1.3 %shard_map.90 = (f32[19,16,16,128]{3,2,1,0:T(8,128)S(1)}, f32[10,32,128]{2,1,0:T(8,128)S(1)}, f32[80,128]{1,0:T(8,128)S(1)}, f32[80,128]{1,0:T(8,128)S(1)}, f32[...) custom-call(f32[19,16,16,128]{3,2,1,0:T(8,128)S(1)} %get-tuple-eleme, ...), custom_call_target="tpu_custom_call", output_to_operand_aliasing={{0}: (0, {}), {1}: (1, {})} | custom-call | tf_op jit(solution)/shard_map/pallas_call | solution.py:599
  18.9 7.8 %all-to-all-start = ((f32[128,2,128]{2,1,0:T(2,128)}), f32[128,2,128]{2,1,0:T(2,128)S(1)}, u32[]{:S(2)}, u32[]{:S(2)}) async-start(f32[128,2,128]{2,1,0:T(2,128)} %bitcast.2), calls=%async_computation | async-start | bytes 262144 | tf_op jit(solution)/shard_map/all_to_all | solution.py:675
  26.7 1.5 %collective-permute-start.4 = (f32[80,128]{1,0:T(8,128)S(1)}, f32[80,128]{1,0:T(8,128)S(1)}, u32[]{:S(2)}, u32[]{:S(2)}) collective-permute-start(f32[80,128]{1,0:T(8,128)S(1)} %get-tuple-element.44), channel_id=1, source_target_pairs={{0,1},{1,2},{2,3},{3,4},{4,5},{5,6},{6,7},{7,8},{8,9},{9,10},{10,1... | collective-permute-start | bytes 122888 | tf_op jit(solution)/shard_map/ppermute | solution.py:620
  28.2 4.3 %collective-permute-start.5 = (f32[80,128]{1,0:T(8,128)S(1)}, f32[80,128]{1,0:T(8,128)S(1)}, u32[]{:S(2)}, u32[]{:S(2)}) collective-permute-start(f32[80,128]{1,0:T(8,128)S(1)} %get-tuple-element.45), channel_id=1, source_target_pairs={{0,15},{1,0},{2,1},{3,2},{4,3},{5,4},{6,5},{7,6},{8,7},{9,8},{10,9... | collective-permute-start | bytes 122888 | tf_op jit(solution)/shard_map/ppermute | solution.py:620
  32.4 1.7 %collective-permute-start.6 = (f32[80,128]{1,0:T(8,128)S(1)}, f32[80,128]{1,0:T(8,128)S(1)}, u32[]{:S(2)}, u32[]{:S(2)}) collective-permute-start(f32[80,128]{1,0:T(8,128)S(1)} %get-tuple-element.49), channel_id=1, source_target_pairs={{0,112},{16,32},{32,16},{48,64},{64,48},{80,96},{96,80},{112,0},{1... | collective-permute-start | bytes 122888 | tf_op jit(solution)/shard_map/ppermute | solution.py:625
  34.2 1.1 %collective-permute-start.7 = (f32[80,128]{1,0:T(8,128)S(1)}, f32[80,128]{1,0:T(8,128)S(1)}, u32[]{:S(2)}, u32[]{:S(2)}) collective-permute-start(f32[80,128]{1,0:T(8,128)S(1)} %get-tuple-element.50), channel_id=1, source_target_pairs={{0,16},{16,0},{32,48},{48,32},{64,80},{80,64},{96,112},{112,96},{1... | collective-permute-start | bytes 122888 | tf_op jit(solution)/shard_map/ppermute | solution.py:625
  35.3 0.0 collective-permute-done.4.yl
  35.3 0.0 collective-permute-done.5.yh
  35.3 2.0 %shard_map.91 = (f32[19,16,16,128]{3,2,1,0:T(8,128)S(1)}, f32[19,16,16,128]{3,2,1,0:T(8,128)}) custom-call(f32[19,16,16,128]{3,2,1,0:T(8,128)S(1)} %get-tuple-element.43.late_in, f32[80,128]{1,0:T(8,128)S(1)} %collective-permute-done.4.yl, f32[80,128]{1,0:T(8,128)S(1)} %collective-permute-done.5.yh, ...), custom_call_target="tpu_custom_call", output_to_operand_aliasing={{0}: (0, {})} | custom-call | flops 20000000 | tf_op jit(solution)/shard_map/pallas_call | solution.py:599
  37.2 0.0 collective-permute-done.6.first
  37.3 0.0 collective-permute-done.7.second
  37.3 0.0 all-to-all-done
  37.3 1.1 %shard_map.92 = (f32[19,16,16,128]{3,2,1,0:T(8,128)S(1)}, f32[19,16,16,128]{3,2,1,0:T(8,128)}, f32[1,256]{1,0:T(1,128)}) custom-call(f32[19,16,16,128]{3,2,1,0:T(8,128)} %get-tuple-element.47.out_in, f32[19,16,16,128]{3,2,1,0:T(8,128)S(1)} %get-tuple-element.48.late_in, ...), custom_call_target="tpu_custom_call", output_to_operand_aliasing={{1}: (0, {}), {0}: (1, {})} | custom-call | tf_op jit(solution)/shard_map/pallas_call | solution.py:599
Async XLA Ops:
  2.0 10.3 %collective-permute-start = (f32[168,128]{1,0:T(8,128)S(1)}, f32[168,128]{1,0:T(8,128)S(1)}, u32[]{:S(2)}, u32[]{:S(2)}) collective-permute-start(f32[168,128]{1,0:T(8,128)S(1)} %get-tuple-element.31), channel_id=1, source_target_pairs={{0,1},{1,2},{2,3},{3,4},{4,5},{5,6},{6,7},{7,8},{8,9},{9,10},{10,1... | collective-permute-start | bytes 258056 | tf_op jit(solution)/shard_map/ppermute | solution.py:620
  4.2 8.1 %collective-permute-start.1 = (f32[168,128]{1,0:T(8,128)S(1)}, f32[168,128]{1,0:T(8,128)S(1)}, u32[]{:S(2)}, u32[]{:S(2)}) collective-permute-start(f32[168,128]{1,0:T(8,128)S(1)} %get-tuple-element.32), channel_id=1, source_target_pairs={{0,15},{1,0},{2,1},{3,2},{4,3},{5,4},{6,5},{7,6},{8,7},{9,8},{10,9... | collective-permute-start | bytes 258056 | tf_op jit(solution)/shard_map/ppermute | solution.py:620
  12.4 5.1 %collective-permute-start.2 = (f32[168,128]{1,0:T(8,128)S(1)}, f32[168,128]{1,0:T(8,128)S(1)}, u32[]{:S(2)}, u32[]{:S(2)}) collective-permute-start(f32[168,128]{1,0:T(8,128)S(1)} %get-tuple-element.41), channel_id=1, source_target_pairs={{0,112},{16,32},{32,16},{48,64},{64,48},{80,96},{96,80},{112,0},{1... | collective-permute-start | bytes 258056 | tf_op jit(solution)/shard_map/ppermute | solution.py:625
  14.5 3.0 %collective-permute-start.3 = (f32[168,128]{1,0:T(8,128)S(1)}, f32[168,128]{1,0:T(8,128)S(1)}, u32[]{:S(2)}, u32[]{:S(2)}) collective-permute-start(f32[168,128]{1,0:T(8,128)S(1)} %get-tuple-element.42), channel_id=1, source_target_pairs={{0,16},{16,0},{32,48},{48,32},{64,80},{80,64},{96,112},{112,96},{1... | collective-permute-start | bytes 258056 | tf_op jit(solution)/shard_map/ppermute | solution.py:625
  18.9 18.4 %all-to-all-start = ((f32[128,2,128]{2,1,0:T(2,128)}), f32[128,2,128]{2,1,0:T(2,128)S(1)}, u32[]{:S(2)}, u32[]{:S(2)}) async-start(f32[128,2,128]{2,1,0:T(2,128)} %bitcast.2), calls=%async_computation | async-start | bytes 262144 | tf_op jit(solution)/shard_map/all_to_all | solution.py:675
  26.7 8.6 %collective-permute-start.4 = (f32[80,128]{1,0:T(8,128)S(1)}, f32[80,128]{1,0:T(8,128)S(1)}, u32[]{:S(2)}, u32[]{:S(2)}) collective-permute-start(f32[80,128]{1,0:T(8,128)S(1)} %get-tuple-element.44), channel_id=1, source_target_pairs={{0,1},{1,2},{2,3},{3,4},{4,5},{5,6},{6,7},{7,8},{8,9},{9,10},{10,1... | collective-permute-start | bytes 122888 | tf_op jit(solution)/shard_map/ppermute | solution.py:620
  28.2 7.1 %collective-permute-start.5 = (f32[80,128]{1,0:T(8,128)S(1)}, f32[80,128]{1,0:T(8,128)S(1)}, u32[]{:S(2)}, u32[]{:S(2)}) collective-permute-start(f32[80,128]{1,0:T(8,128)S(1)} %get-tuple-element.45), channel_id=1, source_target_pairs={{0,15},{1,0},{2,1},{3,2},{4,3},{5,4},{6,5},{7,6},{8,7},{9,8},{10,9... | collective-permute-start | bytes 122888 | tf_op jit(solution)/shard_map/ppermute | solution.py:620
  32.4 4.8 %collective-permute-start.6 = (f32[80,128]{1,0:T(8,128)S(1)}, f32[80,128]{1,0:T(8,128)S(1)}, u32[]{:S(2)}, u32[]{:S(2)}) collective-permute-start(f32[80,128]{1,0:T(8,128)S(1)} %get-tuple-element.49), channel_id=1, source_target_pairs={{0,112},{16,32},{32,16},{48,64},{64,48},{80,96},{96,80},{112,0},{1... | collective-permute-start | bytes 122888 | tf_op jit(solution)/shard_map/ppermute | solution.py:625
  34.2 3.1 %collective-permute-start.7 = (f32[80,128]{1,0:T(8,128)S(1)}, f32[80,128]{1,0:T(8,128)S(1)}, u32[]{:S(2)}, u32[]{:S(2)}) collective-permute-start(f32[80,128]{1,0:T(8,128)S(1)} %get-tuple-element.50), channel_id=1, source_target_pairs={{0,16},{16,0},{32,48},{48,32},{64,80},{80,64},{96,112},{112,96},{1... | collective-permute-start | bytes 122888 | tf_op jit(solution)/shard_map/ppermute | solution.py:625

commit v5 on v4

--- a/solution.py
+++ b/solution.py
@@ -202,32 +202,37 @@
     store_wrapped(put, yt * TILE, cy, value)
 
 
-def by_parity(even, odd):
-    is_odd = jnp.full(even.shape, lax.axis_index("gx") & 1, jnp.int32) == 1
+def by_parity(axis, even, odd):
+    is_odd = jnp.full(even.shape, lax.axis_index(axis) & 1, jnp.int32) == 1
     return jnp.where(is_odd, odd, even)
 
 
-def x_faces(fields, direction, first, second):
-    for n, field in enumerate(fields):
-        pairs = zip(moving(0, 1, direction), moving(0, -1, direction))
-        for k, (i_up, i_down) in enumerate(pairs):
-            up, down = field[i_up, 0], field[i_down, CX - 1]
-            line = pl.ds(n * FACE + k * CY, CY)
-            first[line, :] = by_parity(down, up)
-            second[line, :] = by_parity(up, down)
+def pair_up(up, down, first, second):
+    first[...] = by_parity("gx", down[...], up[...])
+    second[...] = by_parity("gx", up[...], down[...])
 
 
 def x_arrived(sign, line, first, second):
     a, b = first[line, :], second[line, :]
-    return by_parity(a, b) if sign == 1 else by_parity(b, a)
-
-
-def y_faces(fields, direction, y_up, y_down):
+    return by_parity("gx", a, b) if sign == 1 else by_parity("gx", b, a)
+
+
+def y_arrived(sign, line, low, high):
+    return low[line, :] if sign == 1 else high[line, :]
+
+
+def x_faces(fields, direction, x_up, x_down):
     for n, field in enumerate(fields):
-        for sign, row, message in ((1, 0, y_up), (-1, CY - 1, y_down)):
-            for k, i in enumerate(moving(1, sign, direction)):
-                for x in range(CX):
-                    message[pl.ds(n * FACE + k * CX + x, 1), :] = field[i, x, pl.ds(row, 1), :]
+        for sign, x, message in ((1, 0, x_up), (-1, CX - 1, x_down)):
+            for k, i in enumerate(moving(0, sign, direction)):
+                message[pl.ds(n * FACE + k * CY, CY), :] = field[i, x]
+
+
+def y_faces(field, y_up, y_down):
+    for sign, row, message in ((1, 0, y_up), (-1, CY - 1, y_down)):
+        for k, i in enumerate(moving(1, sign, -1)):
+            for x in range(CX):
+                message[pl.ds(k * CX + x, 1), :] = field[i, x, pl.ds(row, 1), :]
 
 
 def fill_x(fields, direction, first, second):
@@ -238,12 +243,14 @@
                 field[i, x] = x_arrived(sign, line, first, second)
 
 
-def fill_y(fields, direction, y_low, y_high):
+def fill_y(fields, direction, first, second):
     for n, field in enumerate(fields):
-        for sign, row, message in ((1, 0, y_low), (-1, CY - 1, y_high)):
+        for sign, row in ((1, 0), (-1, CY - 1)):
             for k, i in enumerate(moving(1, sign, direction)):
+                line = pl.ds(n * FACE + k * CX, CX)
+                face = y_arrived(sign, line, first, second)
                 for x in range(CX):
-                    field[i, x, pl.ds(row, 1), :] = message[pl.ds(n * FACE + k * CX + x, 1), :]
+                    field[i, x, pl.ds(row, 1), :] = face[x : x + 1]
 
 
 def rows(yt):
@@ -296,31 +303,33 @@
 
 def edge_kernel(
     f_hbm, porosity_hbm, porous_hbm, walls_hbm, owners_hbm, slots_hbm,
-    table, yu, yd, f, porosity, porous, walls, owners, slots, sems,
+    table, y_up, y_down, f, porosity, porous, walls, owners, slots, sems,
 ):
     numbers = [
         pltpu.make_async_copy(owners_hbm, owners, sems.at[0]),
         pltpu.make_async_copy(slots_hbm, slots, sems.at[1]),
     ]
+    faces = [(1, CY - 1, y_up), (-1, 0, y_down)]
     lines = []
-    for n, y in enumerate((CY - 1, 0)):
-        lines += [
-            pltpu.make_async_copy(f_hbm.at[:, :, y, :], f.at[n], sems.at[4 * n + 2]),
-            pltpu.make_async_copy(porosity_hbm.at[:, y, :], porosity.at[n], sems.at[4 * n + 3]),
-            pltpu.make_async_copy(porous_hbm.at[:, y, :], porous.at[n], sems.at[4 * n + 4]),
-            pltpu.make_async_copy(walls_hbm.at[:, y, :], walls.at[n], sems.at[4 * n + 5]),
-        ]
-    for copy in numbers + lines:
+    for n, (_, y, _) in enumerate(faces):
+        copies = [pltpu.make_async_copy(f_hbm.at[:, :, y, :], f.at[n], sems.at[4 * n + 2])]
+        for k, (source, target) in enumerate(
+            ((porosity_hbm, porosity), (porous_hbm, porous), (walls_hbm, walls))
+        ):
+            node = source.at[:, y, :]
+            copies.append(pltpu.make_async_copy(node, target.at[n], sems.at[4 * n + 3 + k]))
+        lines.append(copies)
+    for copy in sum(lines, numbers):
         copy.start()
     for copy in numbers:
         copy.wait()
-    block_numbers(owners, slots, table, yu, yd)
-    for copy in lines:
-        copy.wait()
-    for n, (sign, message) in enumerate(((1, yu), (-1, yd))):
-        for xt in range(CX // TILE):
-            at = (n, rows(xt))
-            pops = [f[n, i, rows(xt), :] for i in range(Q)]
+    block_numbers(owners, slots, table, y_up, y_down)
+    for n, (sign, _, message) in enumerate(faces):
+        for copy in lines[n]:
+            copy.wait()
+        for tile in range(CX // TILE):
+            at = (n, rows(tile))
+            pops = [f[n, i, rows(tile), :] for i in range(Q)]
             fraction, open_panel = solidity(porosity[at], porous[at], walls[at])
             c = correction(off_equilibrium(pops)[1])
             for k, i in enumerate(moving(1, sign, 1)):
@@ -328,20 +337,40 @@
                 change = pops[opposite[i]] - relaxed
                 pair = (relaxed + fraction * change, open_panel * change)
                 for field, value in enumerate(pair):
-                    cx, _, cz = velocities[i]
-                    if cz:
-                        value = pltpu.roll(value, cz % NZ, axis=1)
+                    if velocities[i][2]:
+                        value = pltpu.roll(value, velocities[i][2] % NZ, axis=1)
 
                     def put(row, part, base=field * FACE + k * CX, message=message):
                         message[pl.ds(base + row, part.shape[0]), :] = part
 
-                    store_wrapped(put, xt * TILE, cx, value)
+                    store_wrapped(put, tile * TILE, velocities[i][0], value)
+
+
+def turn_kernel(y_first, y_second, frac, first, second, up, down):
+    del frac
+    for sx, message in ((1, up), (-1, down)):
+        for n, sy in enumerate((1, -1)):
+            k = moving(1, sy, 1).index(velocities.index((sx, sy, 0)))
+            row = k * CX + (0 if sx == 1 else CX - 1)
+            for field in range(2):
+                line = pl.ds(field * FACE + row, 1)
+                value = y_arrived(sy, line, y_first, y_second)
+                message[pl.ds(2 * n + field, 1), :] = value
+            numbers = y_arrived(sy, pl.ds(META, 1), y_first, y_second)
+            message[pl.ds(4 + n, 1), :] = numbers
+    pair_up(up, down, first, second)
+
+
+def corner_arrived(sx, sy, row, messages):
+    n = 0 if sy == 1 else 1
+    line = pl.ds(4 + n if row == 2 else 2 * n + row, 1)
+    return x_arrived(sx, line, *messages)
 
 
 def forward_kernel(
-    f_hbm, porosity_hbm, porous_hbm, walls_hbm, adjoint_hbm,
-    moved, gap, adjoint, frac, mask, vel,
-    f, porosity, porous, walls, f_sems, sems,
+    f_hbm, porosity_hbm, porous_hbm, walls_hbm, adjoint_hbm, table,
+    moved, gap, adjoint, frac, mask, vel, x_first, x_second,
+    f, porosity, porous, walls, x_up, x_down, f_sems, sems,
 ):
     def planes(n):
         part = pl.ds(n * PLANES, PLANES)
@@ -384,30 +413,20 @@
         for k in range(PLANES):
             plane(n * PLANES + k)
 
+    x_faces((moved, gap), 1, x_up, x_down)
+    x_up[pl.ds(META, 1), :] = table[pl.ds(8, 1), :]
+    x_down[pl.ds(META, 1), :] = table[pl.ds(1, 1), :]
+    pair_up(x_up, x_down, x_first, x_second)
     later.wait()
 
 
-def turn_kernel(moved_in, gap_in, table, y_low, y_high, moved, gap, ext, first, second):
-    del moved_in, gap_in
-    fill_y((moved, gap), 1, y_low, y_high)
-    x_faces((moved, gap), 1, first, second)
-    shape = (16, NZ)
-    row, lane = iota(shape, 0), iota(shape, 1)
-    low = column(y_low[pl.ds(META, 1), :], row == lane)
-    high = column(y_high[pl.ds(META, 1), :], row == lane)
-    held = jnp.where(lane == 0, low, jnp.where(lane == 9, high, table[...]))
-    ext[...] = held
-    first[pl.ds(META, 1), :] = by_parity(held[1:2], held[8:9])
-    second[pl.ds(META, 1), :] = by_parity(held[8:9], held[1:2])
-
-
-def late_blocks(xb, halves, take, adjoint, frac, mask, late, sums):
+def late_blocks(xb, halves, fields, adjoint, frac, mask, late, sums):
     for yt in range(CY // TILE):
         parts = {}
         for half in halves:
             x = xb * 2 + half
             at = (x, rows(yt))
-            read = [take(0, i, x, yt) for i in range(Q)]
+            read = [fields[0][i, x, rows(yt), :] for i in range(Q)]
             u, e, df = off_equilibrium(read)
             b = [adjoint[i, x, rows(yt), :] for i in range(Q)]
             t, db = covector(b)
@@ -419,7 +438,7 @@
             for i in range(Q):
                 cx, cy, _ = velocities[i]
                 key = ((half - cx) // 2, cy)
-                early = out[i] * take(1, i, x, yt)
+                early = out[i] * fields[1][i, x, rows(yt), :]
                 parts[key] = parts[key] + early if key in parts else early
                 put_moved(late, i, x, yt, out[i], -1)
         for (step, cy), part in parts.items():
@@ -427,15 +446,16 @@
             sums[at] = sums[at] + part
 
 
-def late_kernel(moved, gap, adjoint, frac, mask, late, sums):
+def late_kernel(
+    moved_in, gap_in, y_first, y_second, adjoint, frac, mask, moved, gap, late, sums
+):
+    del moved_in, gap_in
     fields = (moved, gap)
+    fill_y(fields, 1, y_first, y_second)
     sums[...] = jnp.zeros((EXT_XB, EXT_Y, NZ), jnp.float32)
 
-    def take(n, i, x, yt):
-        return fields[n][i, x, rows(yt), :]
-
     def step(xb, halves=(0, 1)):
-        late_blocks(xb, halves, take, adjoint, frac, mask, late, sums)
+        late_blocks(xb, halves, fields, adjoint, frac, mask, late, sums)
 
     step(0, (1,))
     step(CX // 2 - 1, (0,))
@@ -443,26 +463,38 @@
 
 
 def late_rest_kernel(
-    late_in, sums_in, moved, gap, ext_in, first, second, adjoint, frac, mask,
-    late, sums, xf, xs, yu, yd, send_hbm, ext, ring, owner_of, scaled, send, sem,
+    late_in, sums_in, moved_in, gap_in, table, xf_in, xs_in, yf_in, ys_in,
+    c_first, c_second, adjoint, frac, mask,
+    late, sums, moved, gap, xf, xs, yu, yd, send_hbm,
+    xu, xd, ext, ring, owner_of, scaled, send, sem,
 ):
-    del late_in, sums_in
+    del late_in, sums_in, moved_in, gap_in
     fields = (moved, gap)
-
-    def take(n, i, x, yt):
-        cx = velocities[i][0]
-        if (cx, x) in ((1, 0), (-1, CX - 1)):
-            start = n * FACE + moving(0, cx, 1).index(i) * CY + yt * TILE
-            return x_arrived(cx, pl.ds(start, TILE), first, second)
-        return fields[n][i, x, rows(yt), :]
-
+    messages = (c_first, c_second)
+    fill_x(fields, 1, xf_in, xs_in)
+    for sx, x in ((1, 0), (-1, CX - 1)):
+        for sy, y in ((1, 0), (-1, CY - 1)):
+            i = velocities.index((sx, sy, 0))
+            for n, field in enumerate(fields):
+                field[i, x, pl.ds(y, 1), :] = corner_arrived(sx, sy, n, messages)
     for xb, half in ((0, 0), (CX // 2 - 1, 1)):
-        late_blocks(xb, (half,), take, adjoint, frac, mask, late, sums)
-
-    row = iota((16, NZ), 0)
+        late_blocks(xb, (half,), fields, adjoint, frac, mask, late, sums)
+
+    row, lane = iota((16, NZ), 0), iota((16, NZ), 1)
     numbers = pl.ds(META, 1)
-    held = jnp.where(row == 0, x_arrived(1, numbers, first, second), ext_in[...])
-    ext[...] = jnp.where(row == 9, x_arrived(-1, numbers, first, second), held)
+    held = table[...]
+    for sign, place in ((1, 0), (-1, 9)):
+        here = x_arrived(sign, numbers, xf_in, xs_in)
+        held = jnp.where(row == place, here, held)
+    for sign, place in ((1, 0), (-1, 9)):
+        here = column(y_arrived(sign, numbers, yf_in, ys_in), row == lane)
+        held = jnp.where((lane == place) & (row > 0) & (row < 9), here, held)
+    for sx, x in ((1, 0), (-1, 9)):
+        for sy, y in ((1, 0), (-1, 9)):
+            there = iota((1, NZ), 1) == (8 if sx == 1 else 1)
+            here = column(corner_arrived(sx, sy, 2, messages), there)
+            held = jnp.where((row == x) & (lane == y), here, held)
+    ext[...] = held
 
     def put_lines(start, number, spot, total):
         number = number.astype(jnp.int32)
@@ -504,8 +536,9 @@
         send[pl.ds(2 * there + 1, 1), :] = late[i, x, pl.ds(y, 1), :]
     copy = pltpu.make_async_copy(send, send_hbm, sem)
     copy.start()
-    x_faces((late,), -1, xf, xs)
-    y_faces((late,), -1, yu, yd)
+    x_faces((late,), -1, xu, xd)
+    y_faces(late, yu, yd)
+    pair_up(xu, xd, xf, xs)
     copy.wait()
 
 
@@ -530,9 +563,9 @@
             put(i, yt, result[i])
 
 
-def early_kernel(late_in, yl, yh, frac, vel, late, out, hold, sems):
+def early_kernel(late_in, y_first, y_second, frac, vel, late, out, hold, sems):
     del late_in
-    fill_y((late,), -1, yl, yh)
+    fill_y((late,), -1, y_first, y_second)
 
     def planes(n):
         part = pl.ds(1 + n * 2, 2)
@@ -630,7 +663,7 @@
 def body(populations, porosity, adjoint_in, porous, walls, owners, slots):
     ints = pltpu.VMEM((CX, CY, NZ), jnp.int32)
     dma = pltpu.SemaphoreType.DMA
-    table, y_up, y_down = call(
+    table, yf, ys = call(
         edge_kernel,
         [populations, porosity, porous, walls, owners.reshape(1, 64), slots.reshape(1, 64)],
         [vmem(16, NZ), MESSAGE, MESSAGE],
@@ -640,47 +673,48 @@
         + [dma((10,))],
         hbm_ins=6,
     )
-    y_low = shift(y_up, "gy", 1)
-    y_high = shift(y_down, "gy", -1)
-    moved, gap, adjoint, frac, mask, vel = call(
+    yf = shift(yf, "gy", 1)
+    ys = shift(ys, "gy", -1)
+    moved, gap, adjoint, frac, mask, vel, xf, xs = call(
         forward_kernel,
-        [populations, porosity, porous, walls, adjoint_in],
-        [FIELD] * 3 + [NODE] * 2 + [vmem(3, CX, CY, NZ)],
-        scratch=[FIELD, NODE, ints, ints, dma((CX // PLANES,)), dma((4,))],
+        [populations, porosity, porous, walls, adjoint_in, table],
+        [FIELD] * 3 + [NODE] * 2 + [vmem(3, CX, CY, NZ), MESSAGE, MESSAGE],
+        scratch=[FIELD, NODE, ints, ints, MESSAGE, MESSAGE, dma((CX // PLANES,)), dma((4,))],
         hbm_ins=5,
         flops=20_000_000,
     )
-    moved, gap, ext, first, second = call(
-        turn_kernel,
-        [moved, gap, table, y_low, y_high],
-        [FIELD, FIELD, vmem(16, NZ), MESSAGE, MESSAGE],
+    xf = swap(xf, "gx", -1)
+    xs = swap(xs, "gx", 1)
+    corner = call(
+        turn_kernel, [yf, ys, frac], [vmem(TILE, NZ)] * 2, scratch=[vmem(TILE, NZ)] * 2
+    )
+    corner = [swap(corner[0], "gx", -1), swap(corner[1], "gx", 1)]
+    sums_shape = vmem(EXT_XB, EXT_Y, NZ)
+    moved, gap, late, sums = call(
+        late_kernel,
+        [moved, gap, yf, ys, adjoint, frac, mask],
+        [FIELD, FIELD, FIELD, sums_shape],
         aliases={0: 0, 1: 1},
-    )
-    first = swap(first, "gx", -1)
-    second = swap(second, "gx", 1)
-    late, sums = call(
-        late_kernel,
-        [moved, gap, adjoint, frac, mask],
-        [FIELD, vmem(EXT_XB, EXT_Y, NZ)],
         flops=20_000_000,
     )
-    late, _, first, second, y_up, y_down, send = call(
+    late, _, _, _, xf, xs, yf, ys, send = call(
         late_rest_kernel,
-        [late, sums, moved, gap, ext, first, second, adjoint, frac, mask],
-        [FIELD, vmem(EXT_XB, EXT_Y, NZ)] + [SHORT_MESSAGE] * 4,
+        [late, sums, moved, gap, table, xf, xs, yf, ys, *corner, adjoint, frac, mask],
+        [FIELD, sums_shape, FIELD, FIELD] + [SHORT_MESSAGE] * 4,
         hbm_outs=[jax.ShapeDtypeStruct((2 * DEVICES, NZ), jnp.float32)],
-        scratch=[vmem(16, NZ), vmem(32, NZ), LINES, LINES, vmem(2 * DEVICES, NZ), dma],
-        aliases={0: 0, 1: 1},
+        scratch=[SHORT_MESSAGE] * 2
+        + [vmem(16, NZ), vmem(32, NZ), LINES, LINES, vmem(2 * DEVICES, NZ), dma],
+        aliases={0: 0, 1: 1, 2: 2, 3: 3},
     )
     got = lax.all_to_all(send, ("gx", "gy"), split_axis=0, concat_axis=0, tiled=True)
-    y_low = shift(y_up, "gy", 1)
-    y_high = shift(y_down, "gy", -1)
-    first = swap(first, "gx", -1)
-    second = swap(second, "gx", 1)
+    yf = shift(yf, "gy", 1)
+    xf = swap(xf, "gx", -1)
+    xs = swap(xs, "gx", 1)
+    ys = shift(ys, "gy", -1)
     adjoint_shape = jax.ShapeDtypeStruct((Q, CX, CY, NZ), jnp.float32)
     late, adjoint_out = call(
         early_kernel,
-        [late, y_low, y_high, frac, vel],
+        [late, yf, ys, frac, vel],
         [FIELD],
         hbm_outs=[adjoint_shape],
         scratch=[FIELD, dma((CX // 2 - 1,))],
@@ -689,7 +723,7 @@
     )
     _, adjoint_out, patch = call(
         last_kernel,
-        [adjoint_out, late, first, second, got, frac, vel],
+        [adjoint_out, late, xf, xs, got, frac, vel],
         [FIELD],
         hbm_ins=1,
         hbm_outs=[adjoint_shape, jax.ShapeDtypeStruct((1, PATCH_DEV), jnp.float32)],

time: 38.5 us -> 38 us (0.987)
  starting transfers between devices: 26.5 us -> 26.1 us
    all_to_all x1, starting transfers between devices: 7.84 us -> 6.28 us  [body(): lax.all_to_all(send, ('gx', 'gy'), split_axis=0, concat_axis=0, tiled=True)]
    ppermute x4 -> x6, starting transfers between devices: 5.79 us -> 6.92 us  [swap(): lax.ppermute(block, axis, [(i, (i + (-step if i % 2 else step)) % count)...]
  transfers between devices with their start and end apart: 9 -> 11, of which waited for: 0 -> 0; matrix products, arithmetic and copies ran while one was open for 0% -> 0% of each run, Pallas kernels for 19% -> 19%
where the time goes in v5:
time: 38 us; the launch traced here: 37.9 us
  starting transfers between devices  26.1 us (69%)
  Pallas kernels  11 us (29%)
  between operations  0.72 us (2%)
    ppermute x4, starting transfers between devices, shift(): lax.ppermute(block, axis, [(i, (i + step) % count) for i in range(count)])  12.9 us
    pallas_call x7, Pallas kernels, call(): pl.pallas_call(kernel, out_shape=[*outs, *hbm_outs], in_specs=[ANY] * hbm...  11 us
    ppermute x6, starting transfers between devices, swap(): lax.ppermute(block, axis, [(i, (i + (-step if i % 2 else step)) % count)...  6.92 us
    all_to_all x1, starting transfers between devices, body(): lax.all_to_all(send, ('gx', 'gy'), split_axis=0, concat_axis=0, tiled=True)  6.28 us
  transfers between devices with their start and end apart: 11, of which 0 were waited for; matrix products, arithmetic and copies ran while one was open for 0% of the time, Pallas kernels for 19%

profile of v5, /device:TPU:1, one launch (start us, length us, event | category | flops | bytes accessed | tf_op | source)
XLA Modules:
  0.0 37.9 jit_solution(5102367631550369734)
XLA Ops:
  0.6 1.3 %shard_map.86 = (f32[16,128]{1,0:T(8,128)S(1)}, f32[168,128]{1,0:T(8,128)S(1)}, f32[168,128]{1,0:T(8,128)S(1)}) custom-call(f32[19,16,16,128]{3,2,1,0:T(8,128)} %f_hbm.3, f32[16,16,128]{2,1,0:T(8,128)} %porosity_hbm.3, s32[16,16,128]{2,1,0:T(8,128)} %porous_hbm.3, s32[16,16,128]{2,1,0:T(8,128)} %walls_hbm.3, s32[1,64]{1,0:T(1,128)} %bitcast.6, s32[1,64]{1,0:T(1,128)} %bitcast.7), custom_call_target="tpu_custom_call" | custom-call | tf_op jit(solution)/shard_map/pallas_call | solution.py:632
  1.9 2.2 %collective-permute-start = (f32[168,128]{1,0:T(8,128)S(1)}, f32[168,128]{1,0:T(8,128)S(1)}, u32[]{:S(2)}, u32[]{:S(2)}) collective-permute-start(f32[168,128]{1,0:T(8,128)S(1)} %get-tuple-element.32), channel_id=1, source_target_pairs={{0,1},{1,2},{2,3},{3,4},{4,5},{5,6},{6,7},{7,8},{8,9},{9,10},{10,1... | collective-permute-start | bytes 258056 | tf_op jit(solution)/shard_map/ppermute | solution.py:653
  4.1 5.0 %collective-permute-start.1 = (f32[168,128]{1,0:T(8,128)S(1)}, f32[168,128]{1,0:T(8,128)S(1)}, u32[]{:S(2)}, u32[]{:S(2)}) collective-permute-start(f32[168,128]{1,0:T(8,128)S(1)} %get-tuple-element.33), channel_id=1, source_target_pairs={{0,15},{1,0},{2,1},{3,2},{4,3},{5,4},{6,5},{7,6},{8,7},{9,8},{10,9... | collective-permute-start | bytes 258056 | tf_op jit(solution)/shard_map/ppermute | solution.py:653
  9.1 3.1 %shard_map.87 = (f32[19,16,16,128]{3,2,1,0:T(8,128)S(1)}, f32[19,16,16,128]{3,2,1,0:T(8,128)S(1)}, f32[19,16,16,128]{3,2,1,0:T(8,128)S(1)}, f32[16,16,128]{2,1,0...) custom-call(f32[19,16,16,128]{3,2,1,0:T(8,128)} %f_hbm.3, ...), custom_call_target="tpu_custom_call" | custom-call | flops 20000000 | tf_op jit(solution)/shard_map/pallas_call | solution.py:632
  12.2 2.1 %collective-permute-start.2 = (f32[168,128]{1,0:T(8,128)S(1)}, f32[168,128]{1,0:T(8,128)S(1)}, u32[]{:S(2)}, u32[]{:S(2)}) collective-permute-start(f32[168,128]{1,0:T(8,128)S(1)} %get-tuple-element.41), channel_id=1, source_target_pairs={{0,112},{16,32},{32,16},{48,64},{64,48},{80,96},{96,80},{112,0},{1... | collective-permute-start | bytes 258056 | tf_op jit(solution)/shard_map/ppermute | solution.py:658
  14.4 0.8 %collective-permute-start.3 = (f32[168,128]{1,0:T(8,128)S(1)}, f32[168,128]{1,0:T(8,128)S(1)}, u32[]{:S(2)}, u32[]{:S(2)}) collective-permute-start(f32[168,128]{1,0:T(8,128)S(1)} %get-tuple-element.42), channel_id=1, source_target_pairs={{0,16},{16,0},{32,48},{48,32},{64,80},{80,64},{96,112},{112,96},{1... | collective-permute-start | bytes 258056 | tf_op jit(solution)/shard_map/ppermute | solution.py:658
  15.2 0.0 collective-permute-done.y_first.yf_in
  15.2 0.0 collective-permute-done.1.y_second.ys_in
  15.2 0.9 %collective-permute-start.4 = (f32[8,128]{1,0:T(8,128)S(1)}, f32[8,128]{1,0:T(8,128)S(1)}, u32[]{:S(2)}, u32[]{:S(2)}) collective-permute-start(f32[8,128]{1,0:T(8,128)S(1)} %get-tuple-element.43), channel_id=1, source_target_pairs={{0,112},{16,32},{32,16},{48,64},{64,48},{80,96},{96,80},{112,0},{1... | collective-permute-start | bytes 12296 | tf_op jit(solution)/shard_map/ppermute | solution.py:658
  16.1 0.3 collective-permute-start.5
  16.3 2.2 %shard_map.88 = (f32[19,16,16,128]{3,2,1,0:T(8,128)S(1)}, f32[19,16,16,128]{3,2,1,0:T(8,128)S(1)}, f32[19,16,16,128]{3,2,1,0:T(8,128)S(1)}, f32[10,32,128]{2,1,0:T(8,128)S(1)}) custom-call(f32[19,16,16,128]{3,2,1,0:T(8,128)S(1)} %get-tuple-element.30.moved_in, ...), custom_call_target="tpu_custom_call", output_to_operand_aliasing={{0}: (0, {}), {1}: (1, {})} | custom-call | flops 20000000 | tf_op jit(solution)/shard_map/pallas_call | solution.py:632
  18.6 0.0 collective-permute-done.2.xf_in
  18.6 0.0 collective-permute-done.3.xs_in
  18.6 0.0 collective-permute-done.4.c_first
  18.6 0.0 collective-permute-done.5.c_second
  18.6 1.3 %shard_map.90 = (f32[19,16,16,128]{3,2,1,0:T(8,128)S(1)}, f32[10,32,128]{2,1,0:T(8,128)S(1)}, f32[19,16,16,128]{3,2,1,0:T(8,128)S(1)}, f32[19,16,16,128]{3,2,1,0...) custom-call(f32[19,16,16,128]{3,2,1,0:T(8,128)S(1)} %get-tuple-eleme, ...), custom_call_target="tpu_custom_call", output_to_operand_aliasing={{0}: (0, {}), {1}: (1, {}), {2}: (2, {}), {3}: (3, {})} | custom-call | tf_op jit(solution)/shard_map/pallas_call | solution.py:632
  20.0 6.3 %all-to-all-start = ((f32[128,2,128]{2,1,0:T(2,128)}), f32[128,2,128]{2,1,0:T(2,128)S(1)}, u32[]{:S(2)}, u32[]{:S(2)}) async-start(f32[128,2,128]{2,1,0:T(2,128)} %bitcast.2), calls=%async_computation | async-start | bytes 262144 | tf_op jit(solution)/shard_map/all_to_all | solution.py:709
  26.3 1.5 %collective-permute-start.6 = (f32[80,128]{1,0:T(8,128)S(1)}, f32[80,128]{1,0:T(8,128)S(1)}, u32[]{:S(2)}, u32[]{:S(2)}) collective-permute-start(f32[80,128]{1,0:T(8,128)S(1)} %get-tuple-element.46), channel_id=1, source_target_pairs={{0,1},{1,2},{2,3},{3,4},{4,5},{5,6},{6,7},{7,8},{8,9},{9,10},{10,1... | collective-permute-start | bytes 122888 | tf_op jit(solution)/shard_map/ppermute | solution.py:653
  27.7 4.3 %collective-permute-start.7 = (f32[80,128]{1,0:T(8,128)S(1)}, f32[80,128]{1,0:T(8,128)S(1)}, u32[]{:S(2)}, u32[]{:S(2)}) collective-permute-start(f32[80,128]{1,0:T(8,128)S(1)} %get-tuple-element.47), channel_id=1, source_target_pairs={{0,15},{1,0},{2,1},{3,2},{4,3},{5,4},{6,5},{7,6},{8,7},{9,8},{10,9... | collective-permute-start | bytes 122888 | tf_op jit(solution)/shard_map/ppermute | solution.py:653
  32.0 1.7 %collective-permute-start.8 = (f32[80,128]{1,0:T(8,128)S(1)}, f32[80,128]{1,0:T(8,128)S(1)}, u32[]{:S(2)}, u32[]{:S(2)}) collective-permute-start(f32[80,128]{1,0:T(8,128)S(1)} %get-tuple-element.51), channel_id=1, source_target_pairs={{0,112},{16,32},{32,16},{48,64},{64,48},{80,96},{96,80},{112,0},{1... | collective-permute-start | bytes 122888 | tf_op jit(solution)/shard_map/ppermute | solution.py:658
  33.7 1.1 %collective-permute-start.9 = (f32[80,128]{1,0:T(8,128)S(1)}, f32[80,128]{1,0:T(8,128)S(1)}, u32[]{:S(2)}, u32[]{:S(2)}) collective-permute-start(f32[80,128]{1,0:T(8,128)S(1)} %get-tuple-element.52), channel_id=1, source_target_pairs={{0,16},{16,0},{32,48},{48,32},{64,80},{80,64},{96,112},{112,96},{1... | collective-permute-start | bytes 122888 | tf_op jit(solution)/shard_map/ppermute | solution.py:658
  34.8 0.0 collective-permute-done.6.y_first
  34.8 0.0 collective-permute-done.7.y_second
  34.8 1.9 %shard_map.91 = (f32[19,16,16,128]{3,2,1,0:T(8,128)S(1)}, f32[19,16,16,128]{3,2,1,0:T(8,128)}) custom-call(f32[19,16,16,128]{3,2,1,0:T(8,128)S(1)} %get-tuple-element.45.late_in, f32[80,128]{1,0:T(8,128)S(1)} %collective-permute-done.6.y_first, f32[80,128]{1,0:T(8,128)S(1)} %collective-permute-done.7.y_second, ...), custom_call_target="tpu_custom_call", output_to_operand_aliasing={{0}: (0, {})} | custom-call | flops 20000000 | tf_op jit(solution)/shard_map/pallas_call | solution.py:632
  36.8 0.0 collective-permute-done.8.first
  36.8 0.0 collective-permute-done.9.second
  36.8 0.0 all-to-all-done
  36.8 1.1 %shard_map.92 = (f32[19,16,16,128]{3,2,1,0:T(8,128)S(1)}, f32[19,16,16,128]{3,2,1,0:T(8,128)}, f32[1,256]{1,0:T(1,128)}) custom-call(f32[19,16,16,128]{3,2,1,0:T(8,128)} %get-tuple-element.49.out_in, f32[19,16,16,128]{3,2,1,0:T(8,128)S(1)} %get-tuple-element.50.late_in, ...), custom_call_target="tpu_custom_call", output_to_operand_aliasing={{1}: (0, {}), {0}: (1, {})} | custom-call | tf_op jit(solution)/shard_map/pallas_call | solution.py:632
  (1 shorter events, 0.0 us)
Async XLA Ops:
  1.9 13.2 %collective-permute-start = (f32[168,128]{1,0:T(8,128)S(1)}, f32[168,128]{1,0:T(8,128)S(1)}, u32[]{:S(2)}, u32[]{:S(2)}) collective-permute-start(f32[168,128]{1,0:T(8,128)S(1)} %get-tuple-element.32), channel_id=1, source_target_pairs={{0,1},{1,2},{2,3},{3,4},{4,5},{5,6},{6,7},{7,8},{8,9},{9,10},{10,1... | collective-permute-start | bytes 258056 | tf_op jit(solution)/shard_map/ppermute | solution.py:653
  4.1 11.1 %collective-permute-start.1 = (f32[168,128]{1,0:T(8,128)S(1)}, f32[168,128]{1,0:T(8,128)S(1)}, u32[]{:S(2)}, u32[]{:S(2)}) collective-permute-start(f32[168,128]{1,0:T(8,128)S(1)} %get-tuple-element.33), channel_id=1, source_target_pairs={{0,15},{1,0},{2,1},{3,2},{4,3},{5,4},{6,5},{7,6},{8,7},{9,8},{10,9... | collective-permute-start | bytes 258056 | tf_op jit(solution)/shard_map/ppermute | solution.py:653
  12.2 6.3 %collective-permute-start.2 = (f32[168,128]{1,0:T(8,128)S(1)}, f32[168,128]{1,0:T(8,128)S(1)}, u32[]{:S(2)}, u32[]{:S(2)}) collective-permute-start(f32[168,128]{1,0:T(8,128)S(1)} %get-tuple-element.41), channel_id=1, source_target_pairs={{0,112},{16,32},{32,16},{48,64},{64,48},{80,96},{96,80},{112,0},{1... | collective-permute-start | bytes 258056 | tf_op jit(solution)/shard_map/ppermute | solution.py:658
  14.4 4.2 %collective-permute-start.3 = (f32[168,128]{1,0:T(8,128)S(1)}, f32[168,128]{1,0:T(8,128)S(1)}, u32[]{:S(2)}, u32[]{:S(2)}) collective-permute-start(f32[168,128]{1,0:T(8,128)S(1)} %get-tuple-element.42), channel_id=1, source_target_pairs={{0,16},{16,0},{32,48},{48,32},{64,80},{80,64},{96,112},{112,96},{1... | collective-permute-start | bytes 258056 | tf_op jit(solution)/shard_map/ppermute | solution.py:658
  15.2 3.4 %collective-permute-start.4 = (f32[8,128]{1,0:T(8,128)S(1)}, f32[8,128]{1,0:T(8,128)S(1)}, u32[]{:S(2)}, u32[]{:S(2)}) collective-permute-start(f32[8,128]{1,0:T(8,128)S(1)} %get-tuple-element.43), channel_id=1, source_target_pairs={{0,112},{16,32},{32,16},{48,64},{64,48},{80,96},{96,80},{112,0},{1... | collective-permute-start | bytes 12296 | tf_op jit(solution)/shard_map/ppermute | solution.py:658
  16.1 2.5 %collective-permute-start.5 = (f32[8,128]{1,0:T(8,128)S(1)}, f32[8,128]{1,0:T(8,128)S(1)}, u32[]{:S(2)}, u32[]{:S(2)}) collective-permute-start(f32[8,128]{1,0:T(8,128)S(1)} %get-tuple-element.44), channel_id=1, source_target_pairs={{0,16},{16,0},{32,48},{48,32},{64,80},{80,64},{96,112},{112,96},{1... | collective-permute-start | bytes 12296 | tf_op jit(solution)/shard_map/ppermute | solution.py:658
  20.0 16.8 %all-to-all-start = ((f32[128,2,128]{2,1,0:T(2,128)}), f32[128,2,128]{2,1,0:T(2,128)S(1)}, u32[]{:S(2)}, u32[]{:S(2)}) async-start(f32[128,2,128]{2,1,0:T(2,128)} %bitcast.2), calls=%async_computation | async-start | bytes 262144 | tf_op jit(solution)/shard_map/all_to_all | solution.py:709
  26.3 8.6 %collective-permute-start.6 = (f32[80,128]{1,0:T(8,128)S(1)}, f32[80,128]{1,0:T(8,128)S(1)}, u32[]{:S(2)}, u32[]{:S(2)}) collective-permute-start(f32[80,128]{1,0:T(8,128)S(1)} %get-tuple-element.46), channel_id=1, source_target_pairs={{0,1},{1,2},{2,3},{3,4},{4,5},{5,6},{6,7},{7,8},{8,9},{9,10},{10,1... | collective-permute-start | bytes 122888 | tf_op jit(solution)/shard_map/ppermute | solution.py:653
  27.7 7.1 %collective-permute-start.7 = (f32[80,128]{1,0:T(8,128)S(1)}, f32[80,128]{1,0:T(8,128)S(1)}, u32[]{:S(2)}, u32[]{:S(2)}) collective-permute-start(f32[80,128]{1,0:T(8,128)S(1)} %get-tuple-element.47), channel_id=1, source_target_pairs={{0,15},{1,0},{2,1},{3,2},{4,3},{5,4},{6,5},{7,6},{8,7},{9,8},{10,9... | collective-permute-start | bytes 122888 | tf_op jit(solution)/shard_map/ppermute | solution.py:653
  32.0 4.8 %collective-permute-start.8 = (f32[80,128]{1,0:T(8,128)S(1)}, f32[80,128]{1,0:T(8,128)S(1)}, u32[]{:S(2)}, u32[]{:S(2)}) collective-permute-start(f32[80,128]{1,0:T(8,128)S(1)} %get-tuple-element.51), channel_id=1, source_target_pairs={{0,112},{16,32},{32,16},{48,64},{64,48},{80,96},{96,80},{112,0},{1... | collective-permute-start | bytes 122888 | tf_op jit(solution)/shard_map/ppermute | solution.py:658
  33.7 3.1 %collective-permute-start.9 = (f32[80,128]{1,0:T(8,128)S(1)}, f32[80,128]{1,0:T(8,128)S(1)}, u32[]{:S(2)}, u32[]{:S(2)}) collective-permute-start(f32[80,128]{1,0:T(8,128)S(1)} %get-tuple-element.52), channel_id=1, source_target_pairs={{0,16},{16,0},{32,48},{48,32},{64,80},{80,64},{96,112},{112,96},{1... | collective-permute-start | bytes 122888 | tf_op jit(solution)/shard_map/ppermute | solution.py:658

commit v6 on v5

--- a/solution.py
+++ b/solution.py
@@ -587,7 +587,7 @@
 
 
 def last_kernel(
-    out_in, late_in, first, second, got, frac, vel, late, out, patch_out, hold, patch, sems
+    out_in, late_in, second, first, got, frac, vel, late, out, patch_out, hold, patch, sems
 ):
     del out_in, late_in
     fill_x((late,), -1, first, second)
@@ -708,9 +708,9 @@
     )
     got = lax.all_to_all(send, ("gx", "gy"), split_axis=0, concat_axis=0, tiled=True)
     yf = shift(yf, "gy", 1)
+    ys = shift(ys, "gy", -1)
+    xs = swap(xs, "gx", 1)
     xf = swap(xf, "gx", -1)
-    xs = swap(xs, "gx", 1)
-    ys = shift(ys, "gy", -1)
     adjoint_shape = jax.ShapeDtypeStruct((Q, CX, CY, NZ), jnp.float32)
     late, adjoint_out = call(
         early_kernel,
@@ -723,7 +723,7 @@
     )
     _, adjoint_out, patch = call(
         last_kernel,
-        [adjoint_out, late, xf, xs, got, frac, vel],
+        [adjoint_out, late, xs, xf, got, frac, vel],
         [FIELD],
         hbm_ins=1,
         hbm_outs=[adjoint_shape, jax.ShapeDtypeStruct((1, PATCH_DEV), jnp.float32)],

time: 38 us -> 37.7 us (level)
  starting transfers between devices: 26.1 us -> 25 us
  waiting for transfers between devices: 0.05 us -> 0.84 us
    ppermute x6, starting transfers between devices: 6.92 us -> 5.81 us  [swap(): lax.ppermute(block, axis, [(i, (i + (-step if i % 2 else step)) % count)...]
    ppermute x6, waiting for transfers between devices: 0.04 us -> 0.49 us  [swap(): lax.ppermute(block, axis, [(i, (i + (-step if i % 2 else step)) % count)...]
  transfers between devices with their start and end apart: 11 -> 11, of which waited for: 0 -> 2; matrix products, arithmetic and copies ran while one was open for 0% -> 0% of each run, Pallas kernels for 19% -> 19%
where the time goes in v6:
time: 37.7 us; the launch traced here: 37.5 us
  starting transfers between devices  25 us (66%)
  Pallas kernels  11 us (29%)
  waiting for transfers between devices  0.84 us (2%)
  between operations  0.71 us (2%)
    ppermute x4, starting transfers between devices, shift(): lax.ppermute(block, axis, [(i, (i + step) % count) for i in range(count)])  12.9 us
    pallas_call x7, Pallas kernels, call(): pl.pallas_call(kernel, out_shape=[*outs, *hbm_outs], in_specs=[ANY] * hbm...  11 us
    all_to_all x1, starting transfers between devices, body(): lax.all_to_all(send, ('gx', 'gy'), split_axis=0, concat_axis=0, tiled=True)  6.28 us
    ppermute x6, starting transfers between devices, swap(): lax.ppermute(block, axis, [(i, (i + (-step if i % 2 else step)) % count)...  5.81 us
  transfers between devices with their start and end apart: 11, of which 2 were waited for; matrix products, arithmetic and copies ran while one was open for 0% of the time, Pallas kernels for 19%

profile of v6, /device:TPU:1, one launch (start us, length us, event | category | flops | bytes accessed | tf_op | source)
XLA Modules:
  0.0 37.5 jit_solution(8014310217379843606)
XLA Ops:
  0.6 1.3 %shard_map.86 = (f32[16,128]{1,0:T(8,128)S(1)}, f32[168,128]{1,0:T(8,128)S(1)}, f32[168,128]{1,0:T(8,128)S(1)}) custom-call(f32[19,16,16,128]{3,2,1,0:T(8,128)} %f_hbm.3, f32[16,16,128]{2,1,0:T(8,128)} %porosity_hbm.3, s32[16,16,128]{2,1,0:T(8,128)} %porous_hbm.3, s32[16,16,128]{2,1,0:T(8,128)} %walls_hbm.3, s32[1,64]{1,0:T(1,128)} %bitcast.6, s32[1,64]{1,0:T(1,128)} %bitcast.7), custom_call_target="tpu_custom_call" | custom-call | tf_op jit(solution)/shard_map/pallas_call | solution.py:632
  1.9 2.2 %collective-permute-start = (f32[168,128]{1,0:T(8,128)S(1)}, f32[168,128]{1,0:T(8,128)S(1)}, u32[]{:S(2)}, u32[]{:S(2)}) collective-permute-start(f32[168,128]{1,0:T(8,128)S(1)} %get-tuple-element.32), channel_id=1, source_target_pairs={{0,1},{1,2},{2,3},{3,4},{4,5},{5,6},{6,7},{7,8},{8,9},{9,10},{10,1... | collective-permute-start | bytes 258056 | tf_op jit(solution)/shard_map/ppermute | solution.py:653
  4.1 5.0 %collective-permute-start.1 = (f32[168,128]{1,0:T(8,128)S(1)}, f32[168,128]{1,0:T(8,128)S(1)}, u32[]{:S(2)}, u32[]{:S(2)}) collective-permute-start(f32[168,128]{1,0:T(8,128)S(1)} %get-tuple-element.33), channel_id=1, source_target_pairs={{0,15},{1,0},{2,1},{3,2},{4,3},{5,4},{6,5},{7,6},{8,7},{9,8},{10,9... | collective-permute-start | bytes 258056 | tf_op jit(solution)/shard_map/ppermute | solution.py:653
  9.1 3.1 %shard_map.87 = (f32[19,16,16,128]{3,2,1,0:T(8,128)S(1)}, f32[19,16,16,128]{3,2,1,0:T(8,128)S(1)}, f32[19,16,16,128]{3,2,1,0:T(8,128)S(1)}, f32[16,16,128]{2,1,0...) custom-call(f32[19,16,16,128]{3,2,1,0:T(8,128)} %f_hbm.3, ...), custom_call_target="tpu_custom_call" | custom-call | flops 20000000 | tf_op jit(solution)/shard_map/pallas_call | solution.py:632
  12.2 2.1 %collective-permute-start.2 = (f32[168,128]{1,0:T(8,128)S(1)}, f32[168,128]{1,0:T(8,128)S(1)}, u32[]{:S(2)}, u32[]{:S(2)}) collective-permute-start(f32[168,128]{1,0:T(8,128)S(1)} %get-tuple-element.41), channel_id=1, source_target_pairs={{0,112},{16,32},{32,16},{48,64},{64,48},{80,96},{96,80},{112,0},{1... | collective-permute-start | bytes 258056 | tf_op jit(solution)/shard_map/ppermute | solution.py:658
  14.4 0.8 %collective-permute-start.3 = (f32[168,128]{1,0:T(8,128)S(1)}, f32[168,128]{1,0:T(8,128)S(1)}, u32[]{:S(2)}, u32[]{:S(2)}) collective-permute-start(f32[168,128]{1,0:T(8,128)S(1)} %get-tuple-element.42), channel_id=1, source_target_pairs={{0,16},{16,0},{32,48},{48,32},{64,80},{80,64},{96,112},{112,96},{1... | collective-permute-start | bytes 258056 | tf_op jit(solution)/shard_map/ppermute | solution.py:658
  15.2 0.0 collective-permute-done.y_first.yf_in
  15.2 0.0 collective-permute-done.1.y_second.ys_in
  15.2 0.9 %collective-permute-start.4 = (f32[8,128]{1,0:T(8,128)S(1)}, f32[8,128]{1,0:T(8,128)S(1)}, u32[]{:S(2)}, u32[]{:S(2)}) collective-permute-start(f32[8,128]{1,0:T(8,128)S(1)} %get-tuple-element.43), channel_id=1, source_target_pairs={{0,112},{16,32},{32,16},{48,64},{64,48},{80,96},{96,80},{112,0},{1... | collective-permute-start | bytes 12296 | tf_op jit(solution)/shard_map/ppermute | solution.py:658
  16.1 0.3 collective-permute-start.5
  16.3 2.2 %shard_map.88 = (f32[19,16,16,128]{3,2,1,0:T(8,128)S(1)}, f32[19,16,16,128]{3,2,1,0:T(8,128)S(1)}, f32[19,16,16,128]{3,2,1,0:T(8,128)S(1)}, f32[10,32,128]{2,1,0:T(8,128)S(1)}) custom-call(f32[19,16,16,128]{3,2,1,0:T(8,128)S(1)} %get-tuple-element.30.moved_in, ...), custom_call_target="tpu_custom_call", output_to_operand_aliasing={{0}: (0, {}), {1}: (1, {})} | custom-call | flops 20000000 | tf_op jit(solution)/shard_map/pallas_call | solution.py:632
  18.6 0.0 collective-permute-done.2.xf_in
  18.6 0.0 collective-permute-done.3.xs_in
  18.6 0.0 collective-permute-done.4.c_first
  18.6 0.0 collective-permute-done.5.c_second
  18.6 1.3 %shard_map.90 = (f32[19,16,16,128]{3,2,1,0:T(8,128)S(1)}, f32[10,32,128]{2,1,0:T(8,128)S(1)}, f32[19,16,16,128]{3,2,1,0:T(8,128)S(1)}, f32[19,16,16,128]{3,2,1,0...) custom-call(f32[19,16,16,128]{3,2,1,0:T(8,128)S(1)} %get-tuple-eleme, ...), custom_call_target="tpu_custom_call", output_to_operand_aliasing={{0}: (0, {}), {1}: (1, {}), {2}: (2, {}), {3}: (3, {})} | custom-call | tf_op jit(solution)/shard_map/pallas_call | solution.py:632
  20.0 6.3 %all-to-all-start = ((f32[128,2,128]{2,1,0:T(2,128)}), f32[128,2,128]{2,1,0:T(2,128)S(1)}, u32[]{:S(2)}, u32[]{:S(2)}) async-start(f32[128,2,128]{2,1,0:T(2,128)} %bitcast.2), calls=%async_computation | async-start | bytes 262144 | tf_op jit(solution)/shard_map/all_to_all | solution.py:709
  26.3 1.5 %collective-permute-start.6 = (f32[80,128]{1,0:T(8,128)S(1)}, f32[80,128]{1,0:T(8,128)S(1)}, u32[]{:S(2)}, u32[]{:S(2)}) collective-permute-start(f32[80,128]{1,0:T(8,128)S(1)} %get-tuple-element.46), channel_id=1, source_target_pairs={{0,1},{1,2},{2,3},{3,4},{4,5},{5,6},{6,7},{7,8},{8,9},{9,10},{10,1... | collective-permute-start | bytes 122888 | tf_op jit(solution)/shard_map/ppermute | solution.py:653
  27.7 4.3 %collective-permute-start.7 = (f32[80,128]{1,0:T(8,128)S(1)}, f32[80,128]{1,0:T(8,128)S(1)}, u32[]{:S(2)}, u32[]{:S(2)}) collective-permute-start(f32[80,128]{1,0:T(8,128)S(1)} %get-tuple-element.47), channel_id=1, source_target_pairs={{0,15},{1,0},{2,1},{3,2},{4,3},{5,4},{6,5},{7,6},{8,7},{9,8},{10,9... | collective-permute-start | bytes 122888 | tf_op jit(solution)/shard_map/ppermute | solution.py:653
  32.0 0.8 %collective-permute-start.8 = (f32[80,128]{1,0:T(8,128)S(1)}, f32[80,128]{1,0:T(8,128)S(1)}, u32[]{:S(2)}, u32[]{:S(2)}) collective-permute-start(f32[80,128]{1,0:T(8,128)S(1)} %get-tuple-element.51), channel_id=1, source_target_pairs={{0,16},{16,0},{32,48},{48,32},{64,80},{80,64},{96,112},{112,96},{1... | collective-permute-start | bytes 122888 | tf_op jit(solution)/shard_map/ppermute | solution.py:658
  32.7 1.0 %collective-permute-start.9 = (f32[80,128]{1,0:T(8,128)S(1)}, f32[80,128]{1,0:T(8,128)S(1)}, u32[]{:S(2)}, u32[]{:S(2)}) collective-permute-start(f32[80,128]{1,0:T(8,128)S(1)} %get-tuple-element.52), channel_id=1, source_target_pairs={{0,112},{16,32},{32,16},{48,64},{64,48},{80,96},{96,80},{112,0},{1... | collective-permute-start | bytes 122888 | tf_op jit(solution)/shard_map/ppermute | solution.py:658
  33.7 0.3 collective-permute-done.6.y_first
  34.0 0.0 collective-permute-done.7.y_second
  34.1 1.9 %shard_map.91 = (f32[19,16,16,128]{3,2,1,0:T(8,128)S(1)}, f32[19,16,16,128]{3,2,1,0:T(8,128)}) custom-call(f32[19,16,16,128]{3,2,1,0:T(8,128)S(1)} %get-tuple-element.45.late_in, f32[80,128]{1,0:T(8,128)S(1)} %collective-permute-done.6.y_first, f32[80,128]{1,0:T(8,128)S(1)} %collective-permute-done.7.y_second, ...), custom_call_target="tpu_custom_call", output_to_operand_aliasing={{0}: (0, {})} | custom-call | flops 20000000 | tf_op jit(solution)/shard_map/pallas_call | solution.py:632
  36.0 0.0 collective-permute-done.8.second
  36.0 0.5 %collective-permute-done.9.first = f32[80,128]{1,0:T(8,128)S(1)} collective-permute-done((f32[80,128]{1,0:T(8,128)S(1)}, f32[80,128]{1,0:T(8,128)S(1)}, u32[]{:S(2)}, u32[]{:S(2)}) %collective-permute-start.9) | collective-permute-done | bytes 40992 | tf_op jit(solution)/shard_map/ppermute | solution.py:658
  36.5 0.0 all-to-all-done
  36.5 1.1 %shard_map.92 = (f32[19,16,16,128]{3,2,1,0:T(8,128)S(1)}, f32[19,16,16,128]{3,2,1,0:T(8,128)}, f32[1,256]{1,0:T(1,128)}) custom-call(f32[19,16,16,128]{3,2,1,0:T(8,128)} %get-tuple-element.49.out_in, f32[19,16,16,128]{3,2,1,0:T(8,128)S(1)} %get-tuple-element.50.late_in, ...), custom_call_target="tpu_custom_call", output_to_operand_aliasing={{1}: (0, {}), {0}: (1, {})} | custom-call | tf_op jit(solution)/shard_map/pallas_call | solution.py:632
  (1 shorter events, 0.0 us)
Async XLA Ops:
  1.9 13.2 %collective-permute-start = (f32[168,128]{1,0:T(8,128)S(1)}, f32[168,128]{1,0:T(8,128)S(1)}, u32[]{:S(2)}, u32[]{:S(2)}) collective-permute-start(f32[168,128]{1,0:T(8,128)S(1)} %get-tuple-element.32), channel_id=1, source_target_pairs={{0,1},{1,2},{2,3},{3,4},{4,5},{5,6},{6,7},{7,8},{8,9},{9,10},{10,1... | collective-permute-start | bytes 258056 | tf_op jit(solution)/shard_map/ppermute | solution.py:653
  4.1 11.1 %collective-permute-start.1 = (f32[168,128]{1,0:T(8,128)S(1)}, f32[168,128]{1,0:T(8,128)S(1)}, u32[]{:S(2)}, u32[]{:S(2)}) collective-permute-start(f32[168,128]{1,0:T(8,128)S(1)} %get-tuple-element.33), channel_id=1, source_target_pairs={{0,15},{1,0},{2,1},{3,2},{4,3},{5,4},{6,5},{7,6},{8,7},{9,8},{10,9... | collective-permute-start | bytes 258056 | tf_op jit(solution)/shard_map/ppermute | solution.py:653
  12.2 6.3 %collective-permute-start.2 = (f32[168,128]{1,0:T(8,128)S(1)}, f32[168,128]{1,0:T(8,128)S(1)}, u32[]{:S(2)}, u32[]{:S(2)}) collective-permute-start(f32[168,128]{1,0:T(8,128)S(1)} %get-tuple-element.41), channel_id=1, source_target_pairs={{0,112},{16,32},{32,16},{48,64},{64,48},{80,96},{96,80},{112,0},{1... | collective-permute-start | bytes 258056 | tf_op jit(solution)/shard_map/ppermute | solution.py:658
  14.4 4.2 %collective-permute-start.3 = (f32[168,128]{1,0:T(8,128)S(1)}, f32[168,128]{1,0:T(8,128)S(1)}, u32[]{:S(2)}, u32[]{:S(2)}) collective-permute-start(f32[168,128]{1,0:T(8,128)S(1)} %get-tuple-element.42), channel_id=1, source_target_pairs={{0,16},{16,0},{32,48},{48,32},{64,80},{80,64},{96,112},{112,96},{1... | collective-permute-start | bytes 258056 | tf_op jit(solution)/shard_map/ppermute | solution.py:658
  15.2 3.4 %collective-permute-start.4 = (f32[8,128]{1,0:T(8,128)S(1)}, f32[8,128]{1,0:T(8,128)S(1)}, u32[]{:S(2)}, u32[]{:S(2)}) collective-permute-start(f32[8,128]{1,0:T(8,128)S(1)} %get-tuple-element.43), channel_id=1, source_target_pairs={{0,112},{16,32},{32,16},{48,64},{64,48},{80,96},{96,80},{112,0},{1... | collective-permute-start | bytes 12296 | tf_op jit(solution)/shard_map/ppermute | solution.py:658
  16.1 2.5 %collective-permute-start.5 = (f32[8,128]{1,0:T(8,128)S(1)}, f32[8,128]{1,0:T(8,128)S(1)}, u32[]{:S(2)}, u32[]{:S(2)}) collective-permute-start(f32[8,128]{1,0:T(8,128)S(1)} %get-tuple-element.44), channel_id=1, source_target_pairs={{0,16},{16,0},{32,48},{48,32},{64,80},{80,64},{96,112},{112,96},{1... | collective-permute-start | bytes 12296 | tf_op jit(solution)/shard_map/ppermute | solution.py:658
  20.0 16.5 %all-to-all-start = ((f32[128,2,128]{2,1,0:T(2,128)}), f32[128,2,128]{2,1,0:T(2,128)S(1)}, u32[]{:S(2)}, u32[]{:S(2)}) async-start(f32[128,2,128]{2,1,0:T(2,128)} %bitcast.2), calls=%async_computation | async-start | bytes 262144 | tf_op jit(solution)/shard_map/all_to_all | solution.py:709
  26.3 7.8 %collective-permute-start.6 = (f32[80,128]{1,0:T(8,128)S(1)}, f32[80,128]{1,0:T(8,128)S(1)}, u32[]{:S(2)}, u32[]{:S(2)}) collective-permute-start(f32[80,128]{1,0:T(8,128)S(1)} %get-tuple-element.46), channel_id=1, source_target_pairs={{0,1},{1,2},{2,3},{3,4},{4,5},{5,6},{6,7},{7,8},{8,9},{9,10},{10,1... | collective-permute-start | bytes 122888 | tf_op jit(solution)/shard_map/ppermute | solution.py:653
  27.7 6.3 %collective-permute-start.7 = (f32[80,128]{1,0:T(8,128)S(1)}, f32[80,128]{1,0:T(8,128)S(1)}, u32[]{:S(2)}, u32[]{:S(2)}) collective-permute-start(f32[80,128]{1,0:T(8,128)S(1)} %get-tuple-element.47), channel_id=1, source_target_pairs={{0,15},{1,0},{2,1},{3,2},{4,3},{5,4},{6,5},{7,6},{8,7},{9,8},{10,9... | collective-permute-start | bytes 122888 | tf_op jit(solution)/shard_map/ppermute | solution.py:653
  32.0 4.0 %collective-permute-start.8 = (f32[80,128]{1,0:T(8,128)S(1)}, f32[80,128]{1,0:T(8,128)S(1)}, u32[]{:S(2)}, u32[]{:S(2)}) collective-permute-start(f32[80,128]{1,0:T(8,128)S(1)} %get-tuple-element.51), channel_id=1, source_target_pairs={{0,16},{16,0},{32,48},{48,32},{64,80},{80,64},{96,112},{112,96},{1... | collective-permute-start | bytes 122888 | tf_op jit(solution)/shard_map/ppermute | solution.py:658
  32.7 3.7 %collective-permute-start.9 = (f32[80,128]{1,0:T(8,128)S(1)}, f32[80,128]{1,0:T(8,128)S(1)}, u32[]{:S(2)}, u32[]{:S(2)}) collective-permute-start(f32[80,128]{1,0:T(8,128)S(1)} %get-tuple-element.52), channel_id=1, source_target_pairs={{0,112},{16,32},{32,16},{48,64},{64,48},{80,96},{96,80},{112,0},{1... | collective-permute-start | bytes 122888 | tf_op jit(solution)/shard_map/ppermute | solution.py:658

commit v7 on v6

--- a/solution.py
+++ b/solution.py
@@ -463,7 +463,7 @@
 
 
 def late_rest_kernel(
-    late_in, sums_in, moved_in, gap_in, table, xf_in, xs_in, yf_in, ys_in,
+    late_in, sums_in, moved_in, gap_in, table, xs_in, xf_in, yf_in, ys_in,
     c_first, c_second, adjoint, frac, mask,
     late, sums, moved, gap, xf, xs, yu, yd, send_hbm,
     xu, xd, ext, ring, owner_of, scaled, send, sem,
@@ -683,8 +683,8 @@
         hbm_ins=5,
         flops=20_000_000,
     )
+    xs = swap(xs, "gx", 1)
     xf = swap(xf, "gx", -1)
-    xs = swap(xs, "gx", 1)
     corner = call(
         turn_kernel, [yf, ys, frac], [vmem(TILE, NZ)] * 2, scratch=[vmem(TILE, NZ)] * 2
     )
@@ -699,7 +699,7 @@
     )
     late, _, _, _, xf, xs, yf, ys, send = call(
         late_rest_kernel,
-        [late, sums, moved, gap, table, xf, xs, yf, ys, *corner, adjoint, frac, mask],
+        [late, sums, moved, gap, table, xs, xf, yf, ys, *corner, adjoint, frac, mask],
         [FIELD, sums_shape, FIELD, FIELD] + [SHORT_MESSAGE] * 4,
         hbm_outs=[jax.ShapeDtypeStruct((2 * DEVICES, NZ), jnp.float32)],
         scratch=[SHORT_MESSAGE] * 2

time: 37.7 us -> 37.7 us (level)
  no operation moved by 1% of the time
where the time goes in v7:
time: 37.7 us; the launch traced here: 37.5 us
  starting transfers between devices  25 us (66%)
  Pallas kernels  11 us (29%)
  waiting for transfers between devices  0.81 us (2%)
  between operations  0.72 us (2%)
    ppermute x4, starting transfers between devices, shift(): lax.ppermute(block, axis, [(i, (i + step) % count) for i in range(count)])  12.9 us
    pallas_call x7, Pallas kernels, call(): pl.pallas_call(kernel, out_shape=[*outs, *hbm_outs], in_specs=[ANY] * hbm...  11 us
    all_to_all x1, starting transfers between devices, body(): lax.all_to_all(send, ('gx', 'gy'), split_axis=0, concat_axis=0, tiled=True)  6.21 us
    ppermute x6, starting transfers between devices, swap(): lax.ppermute(block, axis, [(i, (i + (-step if i % 2 else step)) % count)...  5.89 us
  transfers between devices with their start and end apart: 11, of which 2 were waited for; matrix products, arithmetic and copies ran while one was open for 0% of the time, Pallas kernels for 19%

profile of v7, /device:TPU:1, one launch (start us, length us, event | category | flops | bytes accessed | tf_op | source)
XLA Modules:
  0.0 37.5 jit_solution(1655001507407152023)
XLA Ops:
  0.6 1.3 %shard_map.86 = (f32[16,128]{1,0:T(8,128)S(1)}, f32[168,128]{1,0:T(8,128)S(1)}, f32[168,128]{1,0:T(8,128)S(1)}) custom-call(f32[19,16,16,128]{3,2,1,0:T(8,128)} %f_hbm.3, f32[16,16,128]{2,1,0:T(8,128)} %porosity_hbm.3, s32[16,16,128]{2,1,0:T(8,128)} %porous_hbm.3, s32[16,16,128]{2,1,0:T(8,128)} %walls_hbm.3, s32[1,64]{1,0:T(1,128)} %bitcast.6, s32[1,64]{1,0:T(1,128)} %bitcast.7), custom_call_target="tpu_custom_call" | custom-call | tf_op jit(solution)/shard_map/pallas_call | solution.py:632
  1.9 2.2 %collective-permute-start = (f32[168,128]{1,0:T(8,128)S(1)}, f32[168,128]{1,0:T(8,128)S(1)}, u32[]{:S(2)}, u32[]{:S(2)}) collective-permute-start(f32[168,128]{1,0:T(8,128)S(1)} %get-tuple-element.32), channel_id=1, source_target_pairs={{0,1},{1,2},{2,3},{3,4},{4,5},{5,6},{6,7},{7,8},{8,9},{9,10},{10,1... | collective-permute-start | bytes 258056 | tf_op jit(solution)/shard_map/ppermute | solution.py:653
  4.1 5.0 %collective-permute-start.1 = (f32[168,128]{1,0:T(8,128)S(1)}, f32[168,128]{1,0:T(8,128)S(1)}, u32[]{:S(2)}, u32[]{:S(2)}) collective-permute-start(f32[168,128]{1,0:T(8,128)S(1)} %get-tuple-element.33), channel_id=1, source_target_pairs={{0,15},{1,0},{2,1},{3,2},{4,3},{5,4},{6,5},{7,6},{8,7},{9,8},{10,9... | collective-permute-start | bytes 258056 | tf_op jit(solution)/shard_map/ppermute | solution.py:653
  9.1 3.1 %shard_map.87 = (f32[19,16,16,128]{3,2,1,0:T(8,128)S(1)}, f32[19,16,16,128]{3,2,1,0:T(8,128)S(1)}, f32[19,16,16,128]{3,2,1,0:T(8,128)S(1)}, f32[16,16,128]{2,1,0...) custom-call(f32[19,16,16,128]{3,2,1,0:T(8,128)} %f_hbm.3, ...), custom_call_target="tpu_custom_call" | custom-call | flops 20000000 | tf_op jit(solution)/shard_map/pallas_call | solution.py:632
  12.2 1.0 %collective-permute-start.2 = (f32[168,128]{1,0:T(8,128)S(1)}, f32[168,128]{1,0:T(8,128)S(1)}, u32[]{:S(2)}, u32[]{:S(2)}) collective-permute-start(f32[168,128]{1,0:T(8,128)S(1)} %get-tuple-element.41), channel_id=1, source_target_pairs={{0,16},{16,0},{32,48},{48,32},{64,80},{80,64},{96,112},{112,96},{1... | collective-permute-start | bytes 258056 | tf_op jit(solution)/shard_map/ppermute | solution.py:658
  13.3 1.2 %collective-permute-start.3 = (f32[168,128]{1,0:T(8,128)S(1)}, f32[168,128]{1,0:T(8,128)S(1)}, u32[]{:S(2)}, u32[]{:S(2)}) collective-permute-start(f32[168,128]{1,0:T(8,128)S(1)} %get-tuple-element.42), channel_id=1, source_target_pairs={{0,112},{16,32},{32,16},{48,64},{64,48},{80,96},{96,80},{112,0},{1... | collective-permute-start | bytes 258056 | tf_op jit(solution)/shard_map/ppermute | solution.py:658
  14.5 0.0 collective-permute-done.y_first.yf_in
  14.5 0.0 collective-permute-done.1.y_second.ys_in
  14.5 0.6 %collective-permute-start.4 = (f32[8,128]{1,0:T(8,128)S(1)}, f32[8,128]{1,0:T(8,128)S(1)}, u32[]{:S(2)}, u32[]{:S(2)}) collective-permute-start(f32[8,128]{1,0:T(8,128)S(1)} %get-tuple-element.43), channel_id=1, source_target_pairs={{0,112},{16,32},{32,16},{48,64},{64,48},{80,96},{96,80},{112,0},{1... | collective-permute-start | bytes 12296 | tf_op jit(solution)/shard_map/ppermute | solution.py:658
  15.1 1.3 %collective-permute-start.5 = (f32[8,128]{1,0:T(8,128)S(1)}, f32[8,128]{1,0:T(8,128)S(1)}, u32[]{:S(2)}, u32[]{:S(2)}) collective-permute-start(f32[8,128]{1,0:T(8,128)S(1)} %get-tuple-element.44), channel_id=1, source_target_pairs={{0,16},{16,0},{32,48},{48,32},{64,80},{80,64},{96,112},{112,96},{1... | collective-permute-start | bytes 12296 | tf_op jit(solution)/shard_map/ppermute | solution.py:658
  16.4 2.2 %shard_map.88 = (f32[19,16,16,128]{3,2,1,0:T(8,128)S(1)}, f32[19,16,16,128]{3,2,1,0:T(8,128)S(1)}, f32[19,16,16,128]{3,2,1,0:T(8,128)S(1)}, f32[10,32,128]{2,1,0:T(8,128)S(1)}) custom-call(f32[19,16,16,128]{3,2,1,0:T(8,128)S(1)} %get-tuple-element.30.moved_in, ...), custom_call_target="tpu_custom_call", output_to_operand_aliasing={{0}: (0, {}), {1}: (1, {})} | custom-call | flops 20000000 | tf_op jit(solution)/shard_map/pallas_call | solution.py:632
  18.6 0.0 collective-permute-done.2.xs_in
  18.7 0.0 collective-permute-done.3.xf_in
  18.7 0.0 collective-permute-done.4.c_first
  18.7 0.0 collective-permute-done.5.c_second
  18.7 1.4 %shard_map.90 = (f32[19,16,16,128]{3,2,1,0:T(8,128)S(1)}, f32[10,32,128]{2,1,0:T(8,128)S(1)}, f32[19,16,16,128]{3,2,1,0:T(8,128)S(1)}, f32[19,16,16,128]{3,2,1,0...) custom-call(f32[19,16,16,128]{3,2,1,0:T(8,128)S(1)} %get-tuple-eleme, ...), custom_call_target="tpu_custom_call", output_to_operand_aliasing={{0}: (0, {}), {1}: (1, {}), {2}: (2, {}), {3}: (3, {})} | custom-call | tf_op jit(solution)/shard_map/pallas_call | solution.py:632
  20.0 6.2 %all-to-all-start = ((f32[128,2,128]{2,1,0:T(2,128)}), f32[128,2,128]{2,1,0:T(2,128)S(1)}, u32[]{:S(2)}, u32[]{:S(2)}) async-start(f32[128,2,128]{2,1,0:T(2,128)} %bitcast.2), calls=%async_computation | async-start | bytes 262144 | tf_op jit(solution)/shard_map/all_to_all | solution.py:709
  26.3 1.5 %collective-permute-start.6 = (f32[80,128]{1,0:T(8,128)S(1)}, f32[80,128]{1,0:T(8,128)S(1)}, u32[]{:S(2)}, u32[]{:S(2)}) collective-permute-start(f32[80,128]{1,0:T(8,128)S(1)} %get-tuple-element.46), channel_id=1, source_target_pairs={{0,1},{1,2},{2,3},{3,4},{4,5},{5,6},{6,7},{7,8},{8,9},{9,10},{10,1... | collective-permute-start | bytes 122888 | tf_op jit(solution)/shard_map/ppermute | solution.py:653
  27.7 4.3 %collective-permute-start.7 = (f32[80,128]{1,0:T(8,128)S(1)}, f32[80,128]{1,0:T(8,128)S(1)}, u32[]{:S(2)}, u32[]{:S(2)}) collective-permute-start(f32[80,128]{1,0:T(8,128)S(1)} %get-tuple-element.47), channel_id=1, source_target_pairs={{0,15},{1,0},{2,1},{3,2},{4,3},{5,4},{6,5},{7,6},{8,7},{9,8},{10,9... | collective-permute-start | bytes 122888 | tf_op jit(solution)/shard_map/ppermute | solution.py:653
  32.0 0.8 %collective-permute-start.8 = (f32[80,128]{1,0:T(8,128)S(1)}, f32[80,128]{1,0:T(8,128)S(1)}, u32[]{:S(2)}, u32[]{:S(2)}) collective-permute-start(f32[80,128]{1,0:T(8,128)S(1)} %get-tuple-element.51), channel_id=1, source_target_pairs={{0,16},{16,0},{32,48},{48,32},{64,80},{80,64},{96,112},{112,96},{1... | collective-permute-start | bytes 122888 | tf_op jit(solution)/shard_map/ppermute | solution.py:658
  32.7 1.0 %collective-permute-start.9 = (f32[80,128]{1,0:T(8,128)S(1)}, f32[80,128]{1,0:T(8,128)S(1)}, u32[]{:S(2)}, u32[]{:S(2)}) collective-permute-start(f32[80,128]{1,0:T(8,128)S(1)} %get-tuple-element.52), channel_id=1, source_target_pairs={{0,112},{16,32},{32,16},{48,64},{64,48},{80,96},{96,80},{112,0},{1... | collective-permute-start | bytes 122888 | tf_op jit(solution)/shard_map/ppermute | solution.py:658
  33.7 0.3 collective-permute-done.6.y_first
  34.0 0.0 collective-permute-done.7.y_second
  34.1 1.9 %shard_map.91 = (f32[19,16,16,128]{3,2,1,0:T(8,128)S(1)}, f32[19,16,16,128]{3,2,1,0:T(8,128)}) custom-call(f32[19,16,16,128]{3,2,1,0:T(8,128)S(1)} %get-tuple-element.45.late_in, f32[80,128]{1,0:T(8,128)S(1)} %collective-permute-done.6.y_first, f32[80,128]{1,0:T(8,128)S(1)} %collective-permute-done.7.y_second, ...), custom_call_target="tpu_custom_call", output_to_operand_aliasing={{0}: (0, {})} | custom-call | flops 20000000 | tf_op jit(solution)/shard_map/pallas_call | solution.py:632
  36.0 0.0 collective-permute-done.8.second
  36.0 0.5 %collective-permute-done.9.first = f32[80,128]{1,0:T(8,128)S(1)} collective-permute-done((f32[80,128]{1,0:T(8,128)S(1)}, f32[80,128]{1,0:T(8,128)S(1)}, u32[]{:S(2)}, u32[]{:S(2)}) %collective-permute-start.9) | collective-permute-done | bytes 40992 | tf_op jit(solution)/shard_map/ppermute | solution.py:658
  36.5 0.0 all-to-all-done
  36.5 1.1 %shard_map.92 = (f32[19,16,16,128]{3,2,1,0:T(8,128)S(1)}, f32[19,16,16,128]{3,2,1,0:T(8,128)}, f32[1,256]{1,0:T(1,128)}) custom-call(f32[19,16,16,128]{3,2,1,0:T(8,128)} %get-tuple-element.49.out_in, f32[19,16,16,128]{3,2,1,0:T(8,128)S(1)} %get-tuple-element.50.late_in, ...), custom_call_target="tpu_custom_call", output_to_operand_aliasing={{1}: (0, {}), {0}: (1, {})} | custom-call | tf_op jit(solution)/shard_map/pallas_call | solution.py:632
  (1 shorter events, 0.0 us)
Async XLA Ops:
  1.9 12.5 %collective-permute-start = (f32[168,128]{1,0:T(8,128)S(1)}, f32[168,128]{1,0:T(8,128)S(1)}, u32[]{:S(2)}, u32[]{:S(2)}) collective-permute-start(f32[168,128]{1,0:T(8,128)S(1)} %get-tuple-element.32), channel_id=1, source_target_pairs={{0,1},{1,2},{2,3},{3,4},{4,5},{5,6},{6,7},{7,8},{8,9},{9,10},{10,1... | collective-permute-start | bytes 258056 | tf_op jit(solution)/shard_map/ppermute | solution.py:653
  4.1 10.3 %collective-permute-start.1 = (f32[168,128]{1,0:T(8,128)S(1)}, f32[168,128]{1,0:T(8,128)S(1)}, u32[]{:S(2)}, u32[]{:S(2)}) collective-permute-start(f32[168,128]{1,0:T(8,128)S(1)} %get-tuple-element.33), channel_id=1, source_target_pairs={{0,15},{1,0},{2,1},{3,2},{4,3},{5,4},{6,5},{7,6},{8,7},{9,8},{10,9... | collective-permute-start | bytes 258056 | tf_op jit(solution)/shard_map/ppermute | solution.py:653
  12.2 6.4 %collective-permute-start.2 = (f32[168,128]{1,0:T(8,128)S(1)}, f32[168,128]{1,0:T(8,128)S(1)}, u32[]{:S(2)}, u32[]{:S(2)}) collective-permute-start(f32[168,128]{1,0:T(8,128)S(1)} %get-tuple-element.41), channel_id=1, source_target_pairs={{0,16},{16,0},{32,48},{48,32},{64,80},{80,64},{96,112},{112,96},{1... | collective-permute-start | bytes 258056 | tf_op jit(solution)/shard_map/ppermute | solution.py:658
  13.3 5.4 %collective-permute-start.3 = (f32[168,128]{1,0:T(8,128)S(1)}, f32[168,128]{1,0:T(8,128)S(1)}, u32[]{:S(2)}, u32[]{:S(2)}) collective-permute-start(f32[168,128]{1,0:T(8,128)S(1)} %get-tuple-element.42), channel_id=1, source_target_pairs={{0,112},{16,32},{32,16},{48,64},{64,48},{80,96},{96,80},{112,0},{1... | collective-permute-start | bytes 258056 | tf_op jit(solution)/shard_map/ppermute | solution.py:658
  14.5 4.2 %collective-permute-start.4 = (f32[8,128]{1,0:T(8,128)S(1)}, f32[8,128]{1,0:T(8,128)S(1)}, u32[]{:S(2)}, u32[]{:S(2)}) collective-permute-start(f32[8,128]{1,0:T(8,128)S(1)} %get-tuple-element.43), channel_id=1, source_target_pairs={{0,112},{16,32},{32,16},{48,64},{64,48},{80,96},{96,80},{112,0},{1... | collective-permute-start | bytes 12296 | tf_op jit(solution)/shard_map/ppermute | solution.py:658
  15.1 3.6 %collective-permute-start.5 = (f32[8,128]{1,0:T(8,128)S(1)}, f32[8,128]{1,0:T(8,128)S(1)}, u32[]{:S(2)}, u32[]{:S(2)}) collective-permute-start(f32[8,128]{1,0:T(8,128)S(1)} %get-tuple-element.44), channel_id=1, source_target_pairs={{0,16},{16,0},{32,48},{48,32},{64,80},{80,64},{96,112},{112,96},{1... | collective-permute-start | bytes 12296 | tf_op jit(solution)/shard_map/ppermute | solution.py:658
  20.0 16.4 %all-to-all-start = ((f32[128,2,128]{2,1,0:T(2,128)}), f32[128,2,128]{2,1,0:T(2,128)S(1)}, u32[]{:S(2)}, u32[]{:S(2)}) async-start(f32[128,2,128]{2,1,0:T(2,128)} %bitcast.2), calls=%async_computation | async-start | bytes 262144 | tf_op jit(solution)/shard_map/all_to_all | solution.py:709
  26.3 7.8 %collective-permute-start.6 = (f32[80,128]{1,0:T(8,128)S(1)}, f32[80,128]{1,0:T(8,128)S(1)}, u32[]{:S(2)}, u32[]{:S(2)}) collective-permute-start(f32[80,128]{1,0:T(8,128)S(1)} %get-tuple-element.46), channel_id=1, source_target_pairs={{0,1},{1,2},{2,3},{3,4},{4,5},{5,6},{6,7},{7,8},{8,9},{9,10},{10,1... | collective-permute-start | bytes 122888 | tf_op jit(solution)/shard_map/ppermute | solution.py:653
  27.7 6.3 %collective-permute-start.7 = (f32[80,128]{1,0:T(8,128)S(1)}, f32[80,128]{1,0:T(8,128)S(1)}, u32[]{:S(2)}, u32[]{:S(2)}) collective-permute-start(f32[80,128]{1,0:T(8,128)S(1)} %get-tuple-element.47), channel_id=1, source_target_pairs={{0,15},{1,0},{2,1},{3,2},{4,3},{5,4},{6,5},{7,6},{8,7},{9,8},{10,9... | collective-permute-start | bytes 122888 | tf_op jit(solution)/shard_map/ppermute | solution.py:653
  32.0 4.0 %collective-permute-start.8 = (f32[80,128]{1,0:T(8,128)S(1)}, f32[80,128]{1,0:T(8,128)S(1)}, u32[]{:S(2)}, u32[]{:S(2)}) collective-permute-start(f32[80,128]{1,0:T(8,128)S(1)} %get-tuple-element.51), channel_id=1, source_target_pairs={{0,16},{16,0},{32,48},{48,32},{64,80},{80,64},{96,112},{112,96},{1... | collective-permute-start | bytes 122888 | tf_op jit(solution)/shard_map/ppermute | solution.py:658
  32.7 3.7 %collective-permute-start.9 = (f32[80,128]{1,0:T(8,128)S(1)}, f32[80,128]{1,0:T(8,128)S(1)}, u32[]{:S(2)}, u32[]{:S(2)}) collective-permute-start(f32[80,128]{1,0:T(8,128)S(1)} %get-tuple-element.52), channel_id=1, source_target_pairs={{0,112},{16,32},{32,16},{48,64},{64,48},{80,96},{96,80},{112,0},{1... | collective-permute-start | bytes 122888 | tf_op jit(solution)/shard_map/ppermute | solution.py:658

commit v8 on v7

--- a/solution.py
+++ b/solution.py
@@ -567,23 +567,19 @@
     del late_in
     fill_y((late,), -1, y_first, y_second)
 
-    def planes(n):
-        part = pl.ds(1 + n * 2, 2)
-        return pltpu.make_async_copy(hold.at[:, part], out.at[:, part], sems.at[n])
-
-    @pl.loop(0, CX // 2 - 1)
-    def _(n):
-        for k in range(2):
-            x = 1 + n * 2 + k
-
-            def put(i, yt, value, x=x):
-                hold[i, x, rows(yt), :] = value
-
-            early_plane(x, late, frac, vel, put)
-        planes(n).start()
-
-    for n in range(CX // 2 - 1):
-        planes(n).wait()
+    def copy(x):
+        return pltpu.make_async_copy(hold.at[:, x], out.at[:, x], sems.at[x])
+
+    def step(x):
+        def put(i, yt, value):
+            hold[i, x, rows(yt), :] = value
+
+        early_plane(x, late, frac, vel, put)
+        copy(x).start()
+
+    unrolled(1, CX - 1, 7, step)
+    for x in range(1, CX - 1):
+        copy(x).wait()
 
 
 def last_kernel(
@@ -717,7 +713,7 @@
         [late, yf, ys, frac, vel],
         [FIELD],
         hbm_outs=[adjoint_shape],
-        scratch=[FIELD, dma((CX // 2 - 1,))],
+        scratch=[FIELD, dma((CX,))],
         aliases={0: 0},
         flops=20_000_000,
     )

time: 37.7 us -> 37.7 us (level)
  no operation moved by 1% of the time
where the time goes in v8:
time: 37.7 us; the launch traced here: 37.5 us
  starting transfers between devices  25 us (66%)
  Pallas kernels  11 us (29%)
  waiting for transfers between devices  0.84 us (2%)
  between operations  0.72 us (2%)
    ppermute x4, starting transfers between devices, shift(): lax.ppermute(block, axis, [(i, (i + step) % count) for i in range(count)])  12.9 us
    pallas_call x7, Pallas kernels, call(): pl.pallas_call(kernel, out_shape=[*outs, *hbm_outs], in_specs=[ANY] * hbm...  11 us
    all_to_all x1, starting transfers between devices, body(): lax.all_to_all(send, ('gx', 'gy'), split_axis=0, concat_axis=0, tiled=True)  6.21 us
    ppermute x6, starting transfers between devices, swap(): lax.ppermute(block, axis, [(i, (i + (-step if i % 2 else step)) % count)...  5.89 us
  transfers between devices with their start and end apart: 11, of which 2 were waited for; matrix products, arithmetic and copies ran while one was open for 0% of the time, Pallas kernels for 19%

profile of v8, /device:TPU:1, one launch (start us, length us, event | category | flops | bytes accessed | tf_op | source)
XLA Modules:
  0.0 37.5 jit_solution(7953228917455212161)
XLA Ops:
  0.6 1.3 %shard_map.86 = (f32[16,128]{1,0:T(8,128)S(1)}, f32[168,128]{1,0:T(8,128)S(1)}, f32[168,128]{1,0:T(8,128)S(1)}) custom-call(f32[19,16,16,128]{3,2,1,0:T(8,128)} %f_hbm.3, f32[16,16,128]{2,1,0:T(8,128)} %porosity_hbm.3, s32[16,16,128]{2,1,0:T(8,128)} %porous_hbm.3, s32[16,16,128]{2,1,0:T(8,128)} %walls_hbm.3, s32[1,64]{1,0:T(1,128)} %bitcast.6, s32[1,64]{1,0:T(1,128)} %bitcast.7), custom_call_target="tpu_custom_call" | custom-call | tf_op jit(solution)/shard_map/pallas_call | solution.py:628
  1.9 2.2 %collective-permute-start = (f32[168,128]{1,0:T(8,128)S(1)}, f32[168,128]{1,0:T(8,128)S(1)}, u32[]{:S(2)}, u32[]{:S(2)}) collective-permute-start(f32[168,128]{1,0:T(8,128)S(1)} %get-tuple-element.32), channel_id=1, source_target_pairs={{0,1},{1,2},{2,3},{3,4},{4,5},{5,6},{6,7},{7,8},{8,9},{9,10},{10,1... | collective-permute-start | bytes 258056 | tf_op jit(solution)/shard_map/ppermute | solution.py:649
  4.1 5.0 %collective-permute-start.1 = (f32[168,128]{1,0:T(8,128)S(1)}, f32[168,128]{1,0:T(8,128)S(1)}, u32[]{:S(2)}, u32[]{:S(2)}) collective-permute-start(f32[168,128]{1,0:T(8,128)S(1)} %get-tuple-element.33), channel_id=1, source_target_pairs={{0,15},{1,0},{2,1},{3,2},{4,3},{5,4},{6,5},{7,6},{8,7},{9,8},{10,9... | collective-permute-start | bytes 258056 | tf_op jit(solution)/shard_map/ppermute | solution.py:649
  9.1 3.1 %shard_map.87 = (f32[19,16,16,128]{3,2,1,0:T(8,128)S(1)}, f32[19,16,16,128]{3,2,1,0:T(8,128)S(1)}, f32[19,16,16,128]{3,2,1,0:T(8,128)S(1)}, f32[16,16,128]{2,1,0...) custom-call(f32[19,16,16,128]{3,2,1,0:T(8,128)} %f_hbm.3, ...), custom_call_target="tpu_custom_call" | custom-call | flops 20000000 | tf_op jit(solution)/shard_map/pallas_call | solution.py:628
  12.2 1.0 %collective-permute-start.2 = (f32[168,128]{1,0:T(8,128)S(1)}, f32[168,128]{1,0:T(8,128)S(1)}, u32[]{:S(2)}, u32[]{:S(2)}) collective-permute-start(f32[168,128]{1,0:T(8,128)S(1)} %get-tuple-element.41), channel_id=1, source_target_pairs={{0,16},{16,0},{32,48},{48,32},{64,80},{80,64},{96,112},{112,96},{1... | collective-permute-start | bytes 258056 | tf_op jit(solution)/shard_map/ppermute | solution.py:654
  13.3 1.2 %collective-permute-start.3 = (f32[168,128]{1,0:T(8,128)S(1)}, f32[168,128]{1,0:T(8,128)S(1)}, u32[]{:S(2)}, u32[]{:S(2)}) collective-permute-start(f32[168,128]{1,0:T(8,128)S(1)} %get-tuple-element.42), channel_id=1, source_target_pairs={{0,112},{16,32},{32,16},{48,64},{64,48},{80,96},{96,80},{112,0},{1... | collective-permute-start | bytes 258056 | tf_op jit(solution)/shard_map/ppermute | solution.py:654
  14.5 0.0 collective-permute-done.y_first.yf_in
  14.5 0.0 collective-permute-done.1.y_second.ys_in
  14.5 0.6 %collective-permute-start.4 = (f32[8,128]{1,0:T(8,128)S(1)}, f32[8,128]{1,0:T(8,128)S(1)}, u32[]{:S(2)}, u32[]{:S(2)}) collective-permute-start(f32[8,128]{1,0:T(8,128)S(1)} %get-tuple-element.43), channel_id=1, source_target_pairs={{0,112},{16,32},{32,16},{48,64},{64,48},{80,96},{96,80},{112,0},{1... | collective-permute-start | bytes 12296 | tf_op jit(solution)/shard_map/ppermute | solution.py:654
  15.1 1.3 %collective-permute-start.5 = (f32[8,128]{1,0:T(8,128)S(1)}, f32[8,128]{1,0:T(8,128)S(1)}, u32[]{:S(2)}, u32[]{:S(2)}) collective-permute-start(f32[8,128]{1,0:T(8,128)S(1)} %get-tuple-element.44), channel_id=1, source_target_pairs={{0,16},{16,0},{32,48},{48,32},{64,80},{80,64},{96,112},{112,96},{1... | collective-permute-start | bytes 12296 | tf_op jit(solution)/shard_map/ppermute | solution.py:654
  16.4 2.2 %shard_map.88 = (f32[19,16,16,128]{3,2,1,0:T(8,128)S(1)}, f32[19,16,16,128]{3,2,1,0:T(8,128)S(1)}, f32[19,16,16,128]{3,2,1,0:T(8,128)S(1)}, f32[10,32,128]{2,1,0:T(8,128)S(1)}) custom-call(f32[19,16,16,128]{3,2,1,0:T(8,128)S(1)} %get-tuple-element.30.moved_in, ...), custom_call_target="tpu_custom_call", output_to_operand_aliasing={{0}: (0, {}), {1}: (1, {})} | custom-call | flops 20000000 | tf_op jit(solution)/shard_map/pallas_call | solution.py:628
  18.6 0.0 collective-permute-done.2.xs_in
  18.7 0.0 collective-permute-done.3.xf_in
  18.7 0.0 collective-permute-done.4.c_first
  18.7 0.0 collective-permute-done.5.c_second
  18.7 1.4 %shard_map.90 = (f32[19,16,16,128]{3,2,1,0:T(8,128)S(1)}, f32[10,32,128]{2,1,0:T(8,128)S(1)}, f32[19,16,16,128]{3,2,1,0:T(8,128)S(1)}, f32[19,16,16,128]{3,2,1,0...) custom-call(f32[19,16,16,128]{3,2,1,0:T(8,128)S(1)} %get-tuple-eleme, ...), custom_call_target="tpu_custom_call", output_to_operand_aliasing={{0}: (0, {}), {1}: (1, {}), {2}: (2, {}), {3}: (3, {})} | custom-call | tf_op jit(solution)/shard_map/pallas_call | solution.py:628
  20.0 6.2 %all-to-all-start = ((f32[128,2,128]{2,1,0:T(2,128)}), f32[128,2,128]{2,1,0:T(2,128)S(1)}, u32[]{:S(2)}, u32[]{:S(2)}) async-start(f32[128,2,128]{2,1,0:T(2,128)} %bitcast.2), calls=%async_computation | async-start | bytes 262144 | tf_op jit(solution)/shard_map/all_to_all | solution.py:705
  26.3 1.5 %collective-permute-start.6 = (f32[80,128]{1,0:T(8,128)S(1)}, f32[80,128]{1,0:T(8,128)S(1)}, u32[]{:S(2)}, u32[]{:S(2)}) collective-permute-start(f32[80,128]{1,0:T(8,128)S(1)} %get-tuple-element.46), channel_id=1, source_target_pairs={{0,1},{1,2},{2,3},{3,4},{4,5},{5,6},{6,7},{7,8},{8,9},{9,10},{10,1... | collective-permute-start | bytes 122888 | tf_op jit(solution)/shard_map/ppermute | solution.py:649
  27.7 4.3 %collective-permute-start.7 = (f32[80,128]{1,0:T(8,128)S(1)}, f32[80,128]{1,0:T(8,128)S(1)}, u32[]{:S(2)}, u32[]{:S(2)}) collective-permute-start(f32[80,128]{1,0:T(8,128)S(1)} %get-tuple-element.47), channel_id=1, source_target_pairs={{0,15},{1,0},{2,1},{3,2},{4,3},{5,4},{6,5},{7,6},{8,7},{9,8},{10,9... | collective-permute-start | bytes 122888 | tf_op jit(solution)/shard_map/ppermute | solution.py:649
  32.0 0.8 %collective-permute-start.8 = (f32[80,128]{1,0:T(8,128)S(1)}, f32[80,128]{1,0:T(8,128)S(1)}, u32[]{:S(2)}, u32[]{:S(2)}) collective-permute-start(f32[80,128]{1,0:T(8,128)S(1)} %get-tuple-element.51), channel_id=1, source_target_pairs={{0,16},{16,0},{32,48},{48,32},{64,80},{80,64},{96,112},{112,96},{1... | collective-permute-start | bytes 122888 | tf_op jit(solution)/shard_map/ppermute | solution.py:654
  32.7 1.0 %collective-permute-start.9 = (f32[80,128]{1,0:T(8,128)S(1)}, f32[80,128]{1,0:T(8,128)S(1)}, u32[]{:S(2)}, u32[]{:S(2)}) collective-permute-start(f32[80,128]{1,0:T(8,128)S(1)} %get-tuple-element.52), channel_id=1, source_target_pairs={{0,112},{16,32},{32,16},{48,64},{64,48},{80,96},{96,80},{112,0},{1... | collective-permute-start | bytes 122888 | tf_op jit(solution)/shard_map/ppermute | solution.py:654
  33.7 0.3 collective-permute-done.6.y_first
  34.0 0.0 collective-permute-done.7.y_second
  34.1 1.9 %shard_map.91 = (f32[19,16,16,128]{3,2,1,0:T(8,128)S(1)}, f32[19,16,16,128]{3,2,1,0:T(8,128)}) custom-call(f32[19,16,16,128]{3,2,1,0:T(8,128)S(1)} %get-tuple-element.45.late_in, f32[80,128]{1,0:T(8,128)S(1)} %collective-permute-done.6.y_first, f32[80,128]{1,0:T(8,128)S(1)} %collective-permute-done.7.y_second, ...), custom_call_target="tpu_custom_call", output_to_operand_aliasing={{0}: (0, {})} | custom-call | flops 20000000 | tf_op jit(solution)/shard_map/pallas_call | solution.py:628
  36.0 0.0 collective-permute-done.8.second
  36.0 0.5 %collective-permute-done.9.first = f32[80,128]{1,0:T(8,128)S(1)} collective-permute-done((f32[80,128]{1,0:T(8,128)S(1)}, f32[80,128]{1,0:T(8,128)S(1)}, u32[]{:S(2)}, u32[]{:S(2)}) %collective-permute-start.9) | collective-permute-done | bytes 40992 | tf_op jit(solution)/shard_map/ppermute | solution.py:654
  36.5 0.0 all-to-all-done
  36.5 1.1 %shard_map.92 = (f32[19,16,16,128]{3,2,1,0:T(8,128)S(1)}, f32[19,16,16,128]{3,2,1,0:T(8,128)}, f32[1,256]{1,0:T(1,128)}) custom-call(f32[19,16,16,128]{3,2,1,0:T(8,128)} %get-tuple-element.49.out_in, f32[19,16,16,128]{3,2,1,0:T(8,128)S(1)} %get-tuple-element.50.late_in, ...), custom_call_target="tpu_custom_call", output_to_operand_aliasing={{1}: (0, {}), {0}: (1, {})} | custom-call | tf_op jit(solution)/shard_map/pallas_call | solution.py:628
  (1 shorter events, 0.0 us)
Async XLA Ops:
  1.9 12.5 %collective-permute-start = (f32[168,128]{1,0:T(8,128)S(1)}, f32[168,128]{1,0:T(8,128)S(1)}, u32[]{:S(2)}, u32[]{:S(2)}) collective-permute-start(f32[168,128]{1,0:T(8,128)S(1)} %get-tuple-element.32), channel_id=1, source_target_pairs={{0,1},{1,2},{2,3},{3,4},{4,5},{5,6},{6,7},{7,8},{8,9},{9,10},{10,1... | collective-permute-start | bytes 258056 | tf_op jit(solution)/shard_map/ppermute | solution.py:649
  4.1 10.3 %collective-permute-start.1 = (f32[168,128]{1,0:T(8,128)S(1)}, f32[168,128]{1,0:T(8,128)S(1)}, u32[]{:S(2)}, u32[]{:S(2)}) collective-permute-start(f32[168,128]{1,0:T(8,128)S(1)} %get-tuple-element.33), channel_id=1, source_target_pairs={{0,15},{1,0},{2,1},{3,2},{4,3},{5,4},{6,5},{7,6},{8,7},{9,8},{10,9... | collective-permute-start | bytes 258056 | tf_op jit(solution)/shard_map/ppermute | solution.py:649
  12.2 6.4 %collective-permute-start.2 = (f32[168,128]{1,0:T(8,128)S(1)}, f32[168,128]{1,0:T(8,128)S(1)}, u32[]{:S(2)}, u32[]{:S(2)}) collective-permute-start(f32[168,128]{1,0:T(8,128)S(1)} %get-tuple-element.41), channel_id=1, source_target_pairs={{0,16},{16,0},{32,48},{48,32},{64,80},{80,64},{96,112},{112,96},{1... | collective-permute-start | bytes 258056 | tf_op jit(solution)/shard_map/ppermute | solution.py:654
  13.3 5.4 %collective-permute-start.3 = (f32[168,128]{1,0:T(8,128)S(1)}, f32[168,128]{1,0:T(8,128)S(1)}, u32[]{:S(2)}, u32[]{:S(2)}) collective-permute-start(f32[168,128]{1,0:T(8,128)S(1)} %get-tuple-element.42), channel_id=1, source_target_pairs={{0,112},{16,32},{32,16},{48,64},{64,48},{80,96},{96,80},{112,0},{1... | collective-permute-start | bytes 258056 | tf_op jit(solution)/shard_map/ppermute | solution.py:654
  14.5 4.2 %collective-permute-start.4 = (f32[8,128]{1,0:T(8,128)S(1)}, f32[8,128]{1,0:T(8,128)S(1)}, u32[]{:S(2)}, u32[]{:S(2)}) collective-permute-start(f32[8,128]{1,0:T(8,128)S(1)} %get-tuple-element.43), channel_id=1, source_target_pairs={{0,112},{16,32},{32,16},{48,64},{64,48},{80,96},{96,80},{112,0},{1... | collective-permute-start | bytes 12296 | tf_op jit(solution)/shard_map/ppermute | solution.py:654
  15.1 3.6 %collective-permute-start.5 = (f32[8,128]{1,0:T(8,128)S(1)}, f32[8,128]{1,0:T(8,128)S(1)}, u32[]{:S(2)}, u32[]{:S(2)}) collective-permute-start(f32[8,128]{1,0:T(8,128)S(1)} %get-tuple-element.44), channel_id=1, source_target_pairs={{0,16},{16,0},{32,48},{48,32},{64,80},{80,64},{96,112},{112,96},{1... | collective-permute-start | bytes 12296 | tf_op jit(solution)/shard_map/ppermute | solution.py:654
  20.0 16.4 %all-to-all-start = ((f32[128,2,128]{2,1,0:T(2,128)}), f32[128,2,128]{2,1,0:T(2,128)S(1)}, u32[]{:S(2)}, u32[]{:S(2)}) async-start(f32[128,2,128]{2,1,0:T(2,128)} %bitcast.2), calls=%async_computation | async-start | bytes 262144 | tf_op jit(solution)/shard_map/all_to_all | solution.py:705
  26.3 7.8 %collective-permute-start.6 = (f32[80,128]{1,0:T(8,128)S(1)}, f32[80,128]{1,0:T(8,128)S(1)}, u32[]{:S(2)}, u32[]{:S(2)}) collective-permute-start(f32[80,128]{1,0:T(8,128)S(1)} %get-tuple-element.46), channel_id=1, source_target_pairs={{0,1},{1,2},{2,3},{3,4},{4,5},{5,6},{6,7},{7,8},{8,9},{9,10},{10,1... | collective-permute-start | bytes 122888 | tf_op jit(solution)/shard_map/ppermute | solution.py:649
  27.7 6.3 %collective-permute-start.7 = (f32[80,128]{1,0:T(8,128)S(1)}, f32[80,128]{1,0:T(8,128)S(1)}, u32[]{:S(2)}, u32[]{:S(2)}) collective-permute-start(f32[80,128]{1,0:T(8,128)S(1)} %get-tuple-element.47), channel_id=1, source_target_pairs={{0,15},{1,0},{2,1},{3,2},{4,3},{5,4},{6,5},{7,6},{8,7},{9,8},{10,9... | collective-permute-start | bytes 122888 | tf_op jit(solution)/shard_map/ppermute | solution.py:649
  32.0 4.0 %collective-permute-start.8 = (f32[80,128]{1,0:T(8,128)S(1)}, f32[80,128]{1,0:T(8,128)S(1)}, u32[]{:S(2)}, u32[]{:S(2)}) collective-permute-start(f32[80,128]{1,0:T(8,128)S(1)} %get-tuple-element.51), channel_id=1, source_target_pairs={{0,16},{16,0},{32,48},{48,32},{64,80},{80,64},{96,112},{112,96},{1... | collective-permute-start | bytes 122888 | tf_op jit(solution)/shard_map/ppermute | solution.py:654
  32.7 3.7 %collective-permute-start.9 = (f32[80,128]{1,0:T(8,128)S(1)}, f32[80,128]{1,0:T(8,128)S(1)}, u32[]{:S(2)}, u32[]{:S(2)}) collective-permute-start(f32[80,128]{1,0:T(8,128)S(1)} %get-tuple-element.52), channel_id=1, source_target_pairs={{0,112},{16,32},{32,16},{48,64},{64,48},{80,96},{96,80},{112,0},{1... | collective-permute-start | bytes 122888 | tf_op jit(solution)/shard_map/ppermute | solution.py:654
